TPU v7x, 32 devices: a whole 2x2x4 slice. The times are simulated.
32 devices in a mesh: gx: 4 (over x, core), gy: 8 (over z, y).
Axes of the slice: x: 2, y: 2, z: 4, core: 2. Of those that a mesh axis runs over, the one named last changes fastest.
Arguments:
- features: bfloat16 [8, 16, 16, 512, 128], P('gx', 'gy'), may hold values from -6 to 6
- owner: int32 [8, 16, 16], P('gx', 'gy'), may hold values from -1 to 127, as said below
- norm_gain: float32 [8, 128], replicated, may hold values from 0.1 to 1.9
- time_shift: float32 [8, 512], replicated, may hold values from -4 to 4
- w_in: bfloat16 [8, 128, 512], replicated, may hold values from -0.5 to 0.5
- w_out: bfloat16 [8, 512, 128], replicated, may hold values from -0.25 to 0.25
- w_down: bfloat16 [2, 2, 2, 128, 128], replicated, may hold values from -0.1875 to 0.1875
- w_conv: bfloat16 [3, 3, 3, 128, 128], replicated, may hold values from -0.109375 to 0.109375
- w_up: bfloat16 [2, 2, 2, 128, 128], replicated, may hold values from -0.5 to 0.5
Outputs:
- denoised: bfloat16 [8, 16, 16, 512, 128], P('gx', 'gy')
Inputs may be any that keep to these rules, and one draw needn't show every extreme that they name: Within each gx index and gy group, every owner along gy gets exactly 16 bricks, one in each compute slot; at most 4 bricks of one device go to one owner, and some device sends 4 to some owner; a device holds at most 32 occupied bricks, and some device holds exactly that many.
All inputs are finite; a program needn't handle non-finite values.
Results may differ from a plain program's by a relative error of at most 0.029.
Values may be sent and summed in bfloat16 or wider, within the bound.
No kernel may reach another device: no remote copies, remote signals or barrier semaphores. Data moves between devices by JAX's collectives and lax.ppermute only.
A program may use at most 192 MiB of HBM per device.

v0:
```python
import math

import jax
import jax.numpy as jnp
from jax import lax
from jax.sharding import PartitionSpec as P

LOAD = 16


def extended(cells, sides, width):
    for axis, dim in sides:
        count = lax.axis_size(axis)
        ends = count - 1
        head = lax.slice_in_dim(cells, 0, width, axis=dim)
        tail = lax.slice_in_dim(cells, cells.shape[dim] - width, cells.shape[dim], axis=dim)
        cells = jnp.concatenate(
            [
                lax.ppermute(tail, axis, [(i, (i + 1) % count) for i in range(ends)]),
                cells,
                lax.ppermute(head, axis, [((i + 1) % count, i) for i in range(ends)]),
            ],
            axis=dim,
        )
    return cells


def brick_down(bricks, live, norm_gain, time_shift, w_in, w_out, w_down):
    count, voxels, chan = bricks.shape
    stream = bricks.reshape(-1, chan)
    for layer in range(w_in.shape[0]):
        whole = stream.astype(jnp.float32)
        scale = lax.rsqrt(jnp.mean(whole * whole, axis=-1, keepdims=True) + 1e-06)
        normed = (whole * scale * norm_gain[layer]).astype(jnp.bfloat16)
        hidden = jax.nn.silu(
            jnp.dot(normed, w_in[layer], preferred_element_type=jnp.float32) + time_shift[layer]
        ).astype(jnp.bfloat16)
        stream = (whole + jnp.dot(hidden, w_out[layer], preferred_element_type=jnp.float32)).astype(
            jnp.bfloat16
        )
    cells = stream.reshape(count, 4, 2, 4, 2, 4, 2, chan)
    down = jnp.einsum("giajbkcd,abcde->gijke", cells, w_down, preferred_element_type=jnp.float32)
    return (jax.nn.silu(down).reshape(count, 64, chan) * live[:, None, None]).astype(jnp.bfloat16)


def brick_up(bricks, mixed, live, w_up):
    count, voxels, chan = bricks.shape
    coarse = mixed.reshape(count, 4, 4, 4, chan)
    upward = jnp.einsum(
        "gijkd,abcde->giajbkce", coarse, w_up, preferred_element_type=jnp.float32
    ).reshape(count, voxels, chan)
    return ((bricks.astype(jnp.float32) + upward) * live[:, None, None]).astype(jnp.bfloat16)


def blockwise(func, count, arrays):
    block = math.gcd(count, 8)
    shaped = tuple((a.reshape((count // block, block) + a.shape[1:]) for a in arrays))
    result = lax.map(lambda group: func(*group), shaped)
    return result.reshape((count,) + result.shape[2:])


def local(features, owner, norm_gain, time_shift, w_in, w_out, w_down, w_conv, w_up):
    cols_x, cols_y, zcap, voxels, chan = features.shape
    slots = cols_x * cols_y * zcap
    flat = features.reshape(slots, voxels, chan)
    code = owner.reshape(slots)
    alive = code >= 0
    live = alive.astype(jnp.float32)

    def reduce_bricks(bricks, marks):
        return brick_down(bricks, marks, norm_gain, time_shift, w_in, w_out, w_down)

    width = lax.axis_size("gy")
    cap = (2 * LOAD + width - 1) // width
    dest = jnp.where(alive, code // LOAD, -1)
    target = jnp.where(alive, code % LOAD, -1)
    order = jnp.arange(slots, dtype=jnp.int32)
    earlier = (dest[:, None] == dest[None, :]) & alive[None, :] & (order[None, :] < order[:, None])
    rank = jnp.sum(earlier.astype(jnp.int32), axis=1)
    position = jnp.where(alive, dest * cap + rank, -1)
    picker = position[None, :] == jnp.arange(width * cap, dtype=jnp.int32)[:, None]
    picker_bf = picker.astype(jnp.bfloat16)
    packed = jnp.dot(
        picker_bf, flat.reshape(slots, voxels * chan), preferred_element_type=jnp.float32
    ).astype(jnp.bfloat16)
    labels = jnp.max(jnp.where(picker, target[None, :], -1), axis=1).astype(jnp.bfloat16)
    arrived, arrived_labels = (
        lax.all_to_all(
            packed.reshape(width, cap, voxels * chan), "gy", split_axis=0, concat_axis=0, tiled=True
        ),
        lax.all_to_all(labels.reshape(width, cap), "gy", split_axis=0, concat_axis=0, tiled=True),
    )
    slot_of = arrived_labels.reshape(width * cap).astype(jnp.int32)
    placer = (slot_of[None, :] == jnp.arange(LOAD, dtype=jnp.int32)[:, None]).astype(jnp.bfloat16)
    compact = jnp.dot(
        placer, arrived.reshape(width * cap, voxels * chan), preferred_element_type=jnp.float32
    ).astype(jnp.bfloat16)
    made = blockwise(
        reduce_bricks, LOAD, (compact.reshape(LOAD, voxels, chan), jnp.ones((LOAD,), jnp.float32))
    )
    returned = jnp.dot(
        placer.T, made.reshape(LOAD, 64 * chan), preferred_element_type=jnp.float32
    ).astype(jnp.bfloat16)
    home = lax.all_to_all(
        returned.reshape(width, cap, 64 * chan), "gy", split_axis=0, concat_axis=0, tiled=True
    )
    coarse_slots = jnp.dot(
        picker_bf.T, home.reshape(width * cap, 64 * chan), preferred_element_type=jnp.float32
    ).astype(jnp.bfloat16)
    gsx, gsy, gsz = (cols_x * 4, cols_y * 4, zcap * 4)
    grid = (
        coarse_slots.reshape(cols_x, cols_y, zcap, 4, 4, 4, chan)
        .transpose(0, 3, 1, 4, 2, 5, 6)
        .reshape(gsx, gsy, gsz, chan)
    )
    rimmed = extended(grid, (("gx", 0), ("gy", 1)), 1)
    padded = jnp.pad(rimmed, ((0, 0), (0, 0), (1, 1), (0, 0)))
    total = grid.astype(jnp.float32)
    for d in range(3):
        for e in range(3):
            for f in range(3):
                moved = padded[d : d + gsx, e : e + gsy, f : f + gsz].reshape(-1, chan)
                total = total + jnp.dot(
                    moved, w_conv[d, e, f], preferred_element_type=jnp.float32
                ).reshape(total.shape)
    live_grid = jnp.broadcast_to(
        live.reshape(cols_x, 1, cols_y, 1, zcap, 1, 1), (cols_x, 4, cols_y, 4, zcap, 4, 1)
    ).reshape(gsx, gsy, gsz, 1)
    mixed = (total * live_grid).astype(jnp.bfloat16)
    mixed = (
        mixed.reshape(cols_x, 4, cols_y, 4, zcap, 4, chan)
        .transpose(0, 2, 4, 1, 3, 5, 6)
        .reshape(slots, 64, chan)
    )

    def lift_bricks(bricks, coarse, marks):
        return brick_up(bricks, coarse, marks, w_up)

    result = blockwise(lift_bricks, slots, (flat, mixed, live))
    return result.reshape(cols_x, cols_y, zcap, voxels, chan)


def solution(mesh):
    in_specs = (
        P("gx", "gy", None, None, None),
        P("gx", "gy", None),
        P(),
        P(),
        P(),
        P(),
        P(),
        P(),
        P(),
    )
    out_specs = P("gx", "gy", None, None, None)
    return jax.shard_map(local, mesh=mesh, in_specs=in_specs, out_specs=out_specs, check_vma=False)
```

profile of v0, /device:TPU:9, one launch (start us, length us, event | category | flops | bytes accessed | tf_op | source)
XLA Modules:
  0.0 389.4 jit_solution(1084702342306966003)
XLA Ops:
  1.8 5.7 %all-to-all-start = ((bf16[8,1,4]{2,1,0:T(2,128)(2,1)}), bf16[8,1,4]{2,1,0:T(2,128)(2,1)S(1)}, u32[]{:S(2)}, u32[]{:S(2)}) async-start(bf16[8,1,4]{2,1,0:T(2,128)(2,1)} %convert_element_type.204), calls=%async_computation | async-start | bytes 8192 | tf_op jit(solution)/shard_map/all_to_all | solution.py:91
  7.5 11.1 %convolution_convert_fusion = bf16[32,65536]{1,0:T(8,128)(2,1)} fusion(bf16[8,8,512,128]{3,2,1,0:T(8,128)(2,1)} %bitcast.448, s32[64]{0:T(128)S(1)} %get-tuple-element.208), kind=kOutput, calls=%fused_computation.132 | convolution fusion | flops 270534656 | bytes 12583168 | tf_op jit(solution)/shard_map/dot_general | solution.py:83
  18.6 5.3 %reshape.392 = bf16[8,4,65536]{2,1,0:T(4,128)(2,1)} reshape(bf16[32,65536]{1,0:T(8,128)(2,1)} %convolution_convert_fusion) | data formatting | bytes 8388608 | tf_op jit(solution)/shard_map/reshape | solution.py:89
  24.0 5.4 %all-to-all-start.1 = ((bf16[8,4,65536]{2,1,0:T(4,128)(2,1)}), bf16[8,4,65536]{2,1,0:T(4,128)(2,1)}, u32[]{:S(2)}, u32[]{:S(2)}) async-start(bf16[8,4,65536]{2,1,0:T(4,128)(2,1)} %reshape.392), calls=%async_computation.1 | async-start | bytes 8388608 | tf_op jit(solution)/shard_map/all_to_all | solution.py:88
  29.5 91.4 %all-to-all-done.1 = bf16[8,4,65536]{2,1,0:T(4,128)(2,1)} async-done(((bf16[8,4,65536]{2,1,0:T(4,128)(2,1)}), bf16[8,4,65536]{2,1,0:T(4,128)(2,1)}, u32[]{:S(2)}, u32[]{:S(2)}) %all-to-all-start.1) | async-done | bytes 4194336 | tf_op jit(solution)/shard_map/all_to_all | solution.py:88
  120.9 5.1 %reshape.393 = bf16[32,65536]{1,0:T(8,128)(2,1)} reshape(bf16[8,4,65536]{2,1,0:T(4,128)(2,1)} %all-to-all-done.1) | data formatting | bytes 8388608 | tf_op jit(solution)/shard_map/reshape | solution.py:96
  126.0 2.9 fusion.115
  128.9 122.1 %while.20 = (s32[]{:T(128)}, bf16[2,8,64,128]{3,1,2,0:T(8,128)(2,1)S(1)}, bf16[2,8,512,128]{3,1,2,0:T(8,128)(2,1)S(1)}, f32[8,128]{1,0:T(8,128)S(1)}, bf16[8,128...) while((s32[]{:T(128)}, ...), condition=%wide.region_11.12_spmd, body=%wide.region_2.11_spmd.sunk | while | flops 8859779072 | bytes 78835896 | solution.py:58
  149.6 5.7 %multiply_reduce_fusion.17 = (f32[4096]{0:T(1024)S(1)}, f32[4096,128]{1,0:T(8,128)}) fusion(f32[4096,128]{1,0:T(8,128)S(1)} %bitcast.446, bf16[8,512,128]{2,1,0:T(8,128)(2,1)} %get-tuple-element.379, bf16[4096,128]{1,0:T(8,128)(2,1)S(1)} %bitcast.447, f32[512]{0:T(512)S(1)} %bitcast.462, bf16[8,128,512]{2,1,0:T(8,128)(2,1)} %get-tuple-element.377), kind=kOutput, calls=%fused_computation.44.clone.1 | convolution fusion | flops 1088942080 | bytes 5523456 | tf_op jit(solution)/shard_map/while/body/eval_jaxpr/dot_general | solution.py:38
  155.3 5.9 %multiply_reduce_fusion.18 = (f32[4096]{0:T(1024)S(1)}, f32[4096,128]{1,0:T(8,128)S(1)}) fusion(f32[4096,128]{1,0:T(8,128)} %get-tuple-element.321, bf16[8,512,128]{2,1,0:T(8,128)(2,1)} %get-tuple-element.379, f32[512]{0:T(512)S(1)} %bitcast.461, f32[128]{0:T(128)S(1)} %get-tuple-element.323, f32[4096]{0:T(1024)S(1)} %add_rsqrt_fusion.17, ...), kind=kOutput, calls=%fused_computation.42.clone.1 | convolution fusion | flops 1090514944 | bytes 6588928 | tf_op jit(solution)/shard_map/while/body/eval_jaxpr/dot_general | solution.py:38
  161.3 5.8 %multiply_reduce_fusion.19 = (f32[4096]{0:T(1024)S(1)}, f32[4096,128]{1,0:T(8,128)}) fusion(f32[4096,128]{1,0:T(8,128)S(1)} %get-tuple-element.325, bf16[8,512,128]{2,1,0:T(8,128)(2,1)} %get-tuple-element.379, f32[512]{0:T(512)S(1)} %bitcast.460, f32[128]{0:T(128)S(1)} %get-tuple-element.327, f32[4096]{0:T(1024)S(1)} %add_rsqrt_fusion.18, ...), kind=kOutput, calls=%fused_computation.40.clone.1 | convolution fusion | flops 1090514944 | bytes 6588928 | tf_op jit(solution)/shard_map/while/body/eval_jaxpr/dot_general | solution.py:38
  167.1 5.9 %multiply_reduce_fusion.20 = (f32[4096]{0:T(1024)S(1)}, f32[4096,128]{1,0:T(8,128)S(1)}) fusion(f32[4096,128]{1,0:T(8,128)} %get-tuple-element.329, bf16[8,512,128]{2,1,0:T(8,128)(2,1)} %get-tuple-element.379, f32[512]{0:T(512)S(1)} %bitcast.459, f32[128]{0:T(128)S(1)} %get-tuple-element.331, f32[4096]{0:T(1024)S(1)} %add_rsqrt_fusion.19, ...), kind=kOutput, calls=%fused_computation.38.clone.1 | convolution fusion | flops 1090514944 | bytes 6588928 | tf_op jit(solution)/shard_map/while/body/eval_jaxpr/dot_general | solution.py:38
  173.1 5.8 %multiply_reduce_fusion.21 = (f32[4096]{0:T(1024)S(1)}, f32[4096,128]{1,0:T(8,128)}) fusion(f32[4096,128]{1,0:T(8,128)S(1)} %get-tuple-element.333, bf16[8,512,128]{2,1,0:T(8,128)(2,1)} %get-tuple-element.379, f32[512]{0:T(512)S(1)} %bitcast.458, f32[128]{0:T(128)S(1)} %get-tuple-element.335, f32[4096]{0:T(1024)S(1)} %add_rsqrt_fusion.20, ...), kind=kOutput, calls=%fused_computation.36.clone.1 | convolution fusion | flops 1090514944 | bytes 6588928 | tf_op jit(solution)/shard_map/while/body/eval_jaxpr/dot_general | solution.py:38
  178.9 5.9 %multiply_reduce_fusion.22 = (f32[4096]{0:T(1024)S(1)}, f32[4096,128]{1,0:T(8,128)S(1)}) fusion(f32[4096,128]{1,0:T(8,128)} %get-tuple-element.337, bf16[8,512,128]{2,1,0:T(8,128)(2,1)} %get-tuple-element.379, f32[512]{0:T(512)S(1)} %bitcast.457, f32[128]{0:T(128)S(1)} %get-tuple-element.339, f32[4096]{0:T(1024)S(1)} %add_rsqrt_fusion.21, ...), kind=kOutput, calls=%fused_computation.34.clone.1 | convolution fusion | flops 1090514944 | bytes 6588928 | tf_op jit(solution)/shard_map/while/body/eval_jaxpr/dot_general | solution.py:38
  184.8 5.8 %multiply_reduce_fusion.23 = (f32[4096]{0:T(1024)S(1)}, f32[4096,128]{1,0:T(8,128)}) fusion(f32[4096,128]{1,0:T(8,128)S(1)} %get-tuple-element.341, bf16[8,512,128]{2,1,0:T(8,128)(2,1)} %get-tuple-element.379, f32[512]{0:T(512)S(1)} %bitcast.456, f32[128]{0:T(128)S(1)} %get-tuple-element.343, f32[4096]{0:T(1024)S(1)} %add_rsqrt_fusion.22, ...), kind=kOutput, calls=%fused_computation.32.clone.1 | convolution fusion | flops 1090514944 | bytes 6588928 | tf_op jit(solution)/shard_map/while/body/eval_jaxpr/dot_general | solution.py:38
  190.6 6.6 %fusion.284 = bf16[4096,128]{1,0:T(8,128)(2,1)} fusion(f32[4096,128]{1,0:T(8,128)} %get-tuple-element.345, f32[512]{0:T(512)S(1)} %bitcast.455, f32[128]{0:T(128)S(1)} %get-tuple-element.347, f32[4096]{0:T(1024)S(1)} %add_rsqrt_fusion.23, bf16[8,512,128]{2,1,0:T(8,128)(2,1)} %get-tuple-element.379, bf16[8,128,512]{2,1,0:T(8,128)(2,1)} %get-tuple-element.377), kind=kOutput, calls=%fused_computation.30.clone.1 | convolution fusion | flops 1088946176 | bytes 5523968 | tf_op jit(solution)/shard_map/while/body/eval_jaxpr/dot_general | solution.py:38
  197.2 2.1 multiply_convert_fusion.63
  201.0 5.7 %multiply_reduce_fusion.17 = (f32[4096]{0:T(1024)S(1)}, f32[4096,128]{1,0:T(8,128)}) fusion(f32[4096,128]{1,0:T(8,128)S(1)} %bitcast.446, bf16[8,512,128]{2,1,0:T(8,128)(2,1)} %get-tuple-element.379, bf16[4096,128]{1,0:T(8,128)(2,1)S(1)} %bitcast.447, f32[512]{0:T(512)S(1)} %bitcast.462, bf16[8,128,512]{2,1,0:T(8,128)(2,1)} %get-tuple-element.377), kind=kOutput, calls=%fused_computation.44.clone.1 | convolution fusion | flops 1088942080 | bytes 5523456 | tf_op jit(solution)/shard_map/while/body/eval_jaxpr/dot_general | solution.py:38
  206.7 5.9 %multiply_reduce_fusion.18 = (f32[4096]{0:T(1024)S(1)}, f32[4096,128]{1,0:T(8,128)S(1)}) fusion(f32[4096,128]{1,0:T(8,128)} %get-tuple-element.321, bf16[8,512,128]{2,1,0:T(8,128)(2,1)} %get-tuple-element.379, f32[512]{0:T(512)S(1)} %bitcast.461, f32[128]{0:T(128)S(1)} %get-tuple-element.323, f32[4096]{0:T(1024)S(1)} %add_rsqrt_fusion.17, ...), kind=kOutput, calls=%fused_computation.42.clone.1 | convolution fusion | flops 1090514944 | bytes 6588928 | tf_op jit(solution)/shard_map/while/body/eval_jaxpr/dot_general | solution.py:38
  212.7 5.8 %multiply_reduce_fusion.19 = (f32[4096]{0:T(1024)S(1)}, f32[4096,128]{1,0:T(8,128)}) fusion(f32[4096,128]{1,0:T(8,128)S(1)} %get-tuple-element.325, bf16[8,512,128]{2,1,0:T(8,128)(2,1)} %get-tuple-element.379, f32[512]{0:T(512)S(1)} %bitcast.460, f32[128]{0:T(128)S(1)} %get-tuple-element.327, f32[4096]{0:T(1024)S(1)} %add_rsqrt_fusion.18, ...), kind=kOutput, calls=%fused_computation.40.clone.1 | convolution fusion | flops 1090514944 | bytes 6588928 | tf_op jit(solution)/shard_map/while/body/eval_jaxpr/dot_general | solution.py:38
  218.5 5.9 %multiply_reduce_fusion.20 = (f32[4096]{0:T(1024)S(1)}, f32[4096,128]{1,0:T(8,128)S(1)}) fusion(f32[4096,128]{1,0:T(8,128)} %get-tuple-element.329, bf16[8,512,128]{2,1,0:T(8,128)(2,1)} %get-tuple-element.379, f32[512]{0:T(512)S(1)} %bitcast.459, f32[128]{0:T(128)S(1)} %get-tuple-element.331, f32[4096]{0:T(1024)S(1)} %add_rsqrt_fusion.19, ...), kind=kOutput, calls=%fused_computation.38.clone.1 | convolution fusion | flops 1090514944 | bytes 6588928 | tf_op jit(solution)/shard_map/while/body/eval_jaxpr/dot_general | solution.py:38
  224.4 5.8 %multiply_reduce_fusion.21 = (f32[4096]{0:T(1024)S(1)}, f32[4096,128]{1,0:T(8,128)}) fusion(f32[4096,128]{1,0:T(8,128)S(1)} %get-tuple-element.333, bf16[8,512,128]{2,1,0:T(8,128)(2,1)} %get-tuple-element.379, f32[512]{0:T(512)S(1)} %bitcast.458, f32[128]{0:T(128)S(1)} %get-tuple-element.335, f32[4096]{0:T(1024)S(1)} %add_rsqrt_fusion.20, ...), kind=kOutput, calls=%fused_computation.36.clone.1 | convolution fusion | flops 1090514944 | bytes 6588928 | tf_op jit(solution)/shard_map/while/body/eval_jaxpr/dot_general | solution.py:38
  230.2 5.9 %multiply_reduce_fusion.22 = (f32[4096]{0:T(1024)S(1)}, f32[4096,128]{1,0:T(8,128)S(1)}) fusion(f32[4096,128]{1,0:T(8,128)} %get-tuple-element.337, bf16[8,512,128]{2,1,0:T(8,128)(2,1)} %get-tuple-element.379, f32[512]{0:T(512)S(1)} %bitcast.457, f32[128]{0:T(128)S(1)} %get-tuple-element.339, f32[4096]{0:T(1024)S(1)} %add_rsqrt_fusion.21, ...), kind=kOutput, calls=%fused_computation.34.clone.1 | convolution fusion | flops 1090514944 | bytes 6588928 | tf_op jit(solution)/shard_map/while/body/eval_jaxpr/dot_general | solution.py:38
  236.2 5.8 %multiply_reduce_fusion.23 = (f32[4096]{0:T(1024)S(1)}, f32[4096,128]{1,0:T(8,128)}) fusion(f32[4096,128]{1,0:T(8,128)S(1)} %get-tuple-element.341, bf16[8,512,128]{2,1,0:T(8,128)(2,1)} %get-tuple-element.379, f32[512]{0:T(512)S(1)} %bitcast.456, f32[128]{0:T(128)S(1)} %get-tuple-element.343, f32[4096]{0:T(1024)S(1)} %add_rsqrt_fusion.22, ...), kind=kOutput, calls=%fused_computation.32.clone.1 | convolution fusion | flops 1090514944 | bytes 6588928 | tf_op jit(solution)/shard_map/while/body/eval_jaxpr/dot_general | solution.py:38
  242.0 6.6 %fusion.284 = bf16[4096,128]{1,0:T(8,128)(2,1)} fusion(f32[4096,128]{1,0:T(8,128)} %get-tuple-element.345, f32[512]{0:T(512)S(1)} %bitcast.455, f32[128]{0:T(128)S(1)} %get-tuple-element.347, f32[4096]{0:T(1024)S(1)} %add_rsqrt_fusion.23, bf16[8,512,128]{2,1,0:T(8,128)(2,1)} %get-tuple-element.379, bf16[8,128,512]{2,1,0:T(8,128)(2,1)} %get-tuple-element.377), kind=kOutput, calls=%fused_computation.30.clone.1 | convolution fusion | flops 1088946176 | bytes 5523968 | tf_op jit(solution)/shard_map/while/body/eval_jaxpr/dot_general | solution.py:38
  248.6 2.1 multiply_convert_fusion.63
  252.4 5.6 %all-to-all-start.2 = ((bf16[8,4,8192]{2,1,0:T(4,128)(2,1)}), bf16[8,4,8192]{2,1,0:T(4,128)(2,1)S(1)}, u32[]{:S(2)}, u32[]{:S(2)}) async-start(bf16[8,4,8192]{2,1,0:T(4,128)(2,1)} %reshape.394), calls=%async_computation.2 | async-start | bytes 1048576 | tf_op jit(solution)/shard_map/all_to_all | solution.py:104
  258.5 10.8 %all-to-all-done.2 = bf16[8,4,8192]{2,1,0:T(4,128)(2,1)S(1)} async-done(((bf16[8,4,8192]{2,1,0:T(4,128)(2,1)}), bf16[8,4,8192]{2,1,0:T(4,128)(2,1)S(1)}, u32[]{:S(2)}, u32[]{:S(2)}) %all-to-all-start.2) | async-done | bytes 524320 | tf_op jit(solution)/shard_map/all_to_all | solution.py:104
  271.2 6.3 %collective-permute-start = (bf16[1,8,64,128]{3,2,1,0:T(8,128)(2,1)S(1)}, bf16[1,8,64,128]{3,2,1,0:T(8,128)(2,1)S(1)}, u32[]{:S(2)}, u32[]{:S(2)}) collective-permute-start(bf16[1,8,64,128]{3,2,1,0:T(8,128)(2,1)S(1)} %get-tuple-element.205), channel_id=1, source_target_pairs={{0,8},{8,16},{16,24},{1,9},{9,17},{17,25},{2,10},{10,18},{18,26},{... | collective-permute-start | bytes 393224 | tf_op jit(solution)/shard_map/ppermute | solution.py:19
  277.5 1.9 collective-permute-start.1
  279.4 2.5 fusion.179
  282.0 1.8 collective-permute-done.1
  283.8 1.9 collective-permute-start.2
  285.8 4.3 %collective-permute-start.3 = (bf16[10,1,64,128]{3,2,1,0:T(8,128)(2,1)S(1)}, bf16[10,1,64,128]{3,2,1,0:T(8,128)(2,1)S(1)}, u32[]{:S(2)}, u32[]{:S(2)}) collective-permute-start(bf16[10,1,64,128]{3,2,1,0:T(8,128)(2,1)S(1)} %get-tuple-element.204), channel_id=1, source_target_pairs={{1,0},{2,1},{3,2},{4,3},{5,4},{6,5},{7,6},{9,8},{10,9},{11,10},{12... | collective-permute-start | bytes 491528 | tf_op jit(solution)/shard_map/ppermute | solution.py:21
  290.0 2.5 fusion.116
  292.5 2.5 fusion.120
  295.0 1.8 select_maximum_fusion
  300.4 1.8 fusion.132
  305.6 1.8 fusion.138
  309.1 1.8 fusion.142
  312.6 1.8 fusion.146
  316.1 1.8 fusion.150
  319.7 1.8 fusion.154
  323.2 1.8 fusion.158
  324.9 1.8 fusion.160
  326.7 1.7 fusion.194
  337.2 19.0 %multiply_convert_fusion.32 = bf16[8,8,64,128]{3,2,1,0:T(8,128)(2,1)} fusion(f32[8,8,64,128]{3,2,1,0:T(8,128)} %fusion.164, f32[8,8,64,128]{3,2,1,0:T(8,128)} %fusion.128, f32[8,8,64,128]{3,2,1,0:T(8,128)} %fusion.130, f32[8,8,64,128]{3,2,1,0:T(8,128)} %fusion.120, f32[8,8,64,128]{3,2,1,0:T(8,128)} %fusion.132, f32[8,8,64,128]{3,2,1,0:T(8,128)} %fusion.134, ...), kind=kOutput, calls=%fused_computation.141 | convolution fusion | flops 149946368 | bytes 57737216 | tf_op jit(solution)/shard_map/dot_general | solution.py:123
  357.7 31.5 %while.21 = (s32[]{:T(128)}, bf16[8,8,512,128]{3,2,1,0:T(8,128)(2,1)}, bf16[8,8,512,128]{3,2,1,0:T(8,128)(2,1)}, bf16[8,8,64,128]{3,1,0,2:T(8,128)(2,1)S(1)}, bf...) while((s32[]{:T(128)}, bf16[8,8,512,128]{3,2,1,0:T(8,128)(2,1)}, ...), condition=%wide.region_13.14_spmd, body=%wide.region_12.13_spmd.sunk | while | flops 136314880 | bytes 15336121 | solution.py:58
  (159 shorter events, 66.0 us)
Async XLA Ops:
  1.0 17.6 %copy-start.7 = (s32[64]{0:T(128)}, s32[64]{0:T(128)S(1)}, u32[]{:S(2)}) copy-start(s32[64]{0:T(128)S(1)} %get-tuple-element.208) | copy-start | bytes 772
  1.8 22.2 %all-to-all-start = ((bf16[8,1,4]{2,1,0:T(2,128)(2,1)}), bf16[8,1,4]{2,1,0:T(2,128)(2,1)S(1)}, u32[]{:S(2)}, u32[]{:S(2)}) async-start(bf16[8,1,4]{2,1,0:T(2,128)(2,1)} %convert_element_type.204), calls=%async_computation | async-start | bytes 8192 | tf_op jit(solution)/shard_map/all_to_all | solution.py:91
  24.0 96.9 %all-to-all-start.1 = ((bf16[8,4,65536]{2,1,0:T(4,128)(2,1)}), bf16[8,4,65536]{2,1,0:T(4,128)(2,1)}, u32[]{:S(2)}, u32[]{:S(2)}) async-start(bf16[8,4,65536]{2,1,0:T(4,128)(2,1)} %reshape.392), calls=%async_computation.1 | async-start | bytes 8388608 | tf_op jit(solution)/shard_map/all_to_all | solution.py:88
  29.5 96.5 %copy-start.9 = (s32[32]{0:T(128)}, s32[32]{0:T(128)S(1)}, u32[]{:S(2)}) copy-start(s32[32]{0:T(128)S(1)} %reshape.400) | copy-start | bytes 388
  126.0 2.9 copy-start.4
  126.0 2.9 copy-start.5
  128.9 122.1 %copy-start.10 = (s32[32]{0:T(128)S(1)}, s32[32]{0:T(128)}, u32[]{:S(2)}) copy-start(s32[32]{0:T(128)} %copy-done.9) | copy-start | bytes 388
  148.0 1.5 copy-start
  190.6 6.6 %copy-start.11 = (bf16[2,2,2,128,128]{4,3,2,1,0:T(8,128)(2,1)S(1)}, bf16[2,2,2,128,128]{4,3,2,1,0:T(8,128)(2,1)}, u32[]{:S(2)}) copy-start(bf16[2,2,2,128,128]{4,3,2,1,0:T(8,128)(2,1)} %get-tuple-element.380) | copy-start | bytes 786436 | tf_op jit(solution)/shard_map/while
  197.2 2.1 copy-start.1
  199.4 1.5 copy-start
  242.0 6.6 %copy-start.11 = (bf16[2,2,2,128,128]{4,3,2,1,0:T(8,128)(2,1)S(1)}, bf16[2,2,2,128,128]{4,3,2,1,0:T(8,128)(2,1)}, u32[]{:S(2)}) copy-start(bf16[2,2,2,128,128]{4,3,2,1,0:T(8,128)(2,1)} %get-tuple-element.380) | copy-start | bytes 786436 | tf_op jit(solution)/shard_map/while
  248.6 2.1 copy-start.1
  251.0 7.0 %copy-start.6 = (s32[2,2,16]{2,1,0:T(2,128)S(1)}, s32[2,2,16]{2,1,0:T(2,128)}, u32[]{:S(2)}) copy-start(s32[2,2,16]{2,1,0:T(2,128)} %param.14) | copy-start | bytes 772
  251.4 18.0 %copy-start.8 = (s32[64]{0:T(128)S(1)}, s32[64]{0:T(128)}, u32[]{:S(2)}) copy-start(s32[64]{0:T(128)} %copy-done.7) | copy-start | bytes 772
  252.4 16.8 %all-to-all-start.2 = ((bf16[8,4,8192]{2,1,0:T(4,128)(2,1)}), bf16[8,4,8192]{2,1,0:T(4,128)(2,1)S(1)}, u32[]{:S(2)}, u32[]{:S(2)}) async-start(bf16[8,4,8192]{2,1,0:T(4,128)(2,1)} %reshape.394), calls=%async_computation.2 | async-start | bytes 1048576 | tf_op jit(solution)/shard_map/all_to_all | solution.py:104
  271.2 10.7 %collective-permute-start = (bf16[1,8,64,128]{3,2,1,0:T(8,128)(2,1)S(1)}, bf16[1,8,64,128]{3,2,1,0:T(8,128)(2,1)S(1)}, u32[]{:S(2)}, u32[]{:S(2)}) collective-permute-start(bf16[1,8,64,128]{3,2,1,0:T(8,128)(2,1)S(1)} %get-tuple-element.205), channel_id=1, source_target_pairs={{0,8},{8,16},{16,24},{1,9},{9,17},{17,25},{2,10},{10,18},{18,26},{... | collective-permute-start | bytes 393224 | tf_op jit(solution)/shard_map/ppermute | solution.py:19
  277.5 6.3 %collective-permute-start.1 = (bf16[1,8,64,128]{3,2,1,0:T(8,128)(2,1)S(1)}, bf16[1,8,64,128]{3,2,1,0:T(8,128)(2,1)S(1)}, u32[]{:S(2)}, u32[]{:S(2)}) collective-permute-start(bf16[1,8,64,128]{3,2,1,0:T(8,128)(2,1)S(1)} %get-tuple-element.206), channel_id=1, source_target_pairs={{8,0},{16,8},{24,16},{9,1},{17,9},{25,17},{10,2},{18,10},{26,18},{... | collective-permute-start | bytes 393224 | tf_op jit(solution)/shard_map/ppermute | solution.py:21
  283.8 11.2 %collective-permute-start.2 = (bf16[10,1,64,128]{3,2,1,0:T(8,128)(2,1)S(1)}, bf16[10,1,64,128]{3,2,1,0:T(8,128)(2,1)S(1)}, u32[]{:S(2)}, u32[]{:S(2)}) collective-permute-start(bf16[10,1,64,128]{3,2,1,0:T(8,128)(2,1)S(1)} %get-tuple-element.203), channel_id=1, source_target_pairs={{0,1},{1,2},{2,3},{3,4},{4,5},{5,6},{6,7},{8,9},{9,10},{10,11},{11... | collective-permute-start | bytes 491528 | tf_op jit(solution)/shard_map/ppermute | solution.py:19
  285.8 9.3 %collective-permute-start.3 = (bf16[10,1,64,128]{3,2,1,0:T(8,128)(2,1)S(1)}, bf16[10,1,64,128]{3,2,1,0:T(8,128)(2,1)S(1)}, u32[]{:S(2)}, u32[]{:S(2)}) collective-permute-start(bf16[10,1,64,128]{3,2,1,0:T(8,128)(2,1)S(1)} %get-tuple-element.204), channel_id=1, source_target_pairs={{1,0},{2,1},{3,2},{4,3},{5,4},{6,5},{7,6},{9,8},{10,9},{11,10},{12... | collective-permute-start | bytes 491528 | tf_op jit(solution)/shard_map/ppermute | solution.py:21
  295.0 1.8 copy-start.3
  356.1 1.5 copy-start.2
where the time goes:
time: 396 us; the launch traced here: 389 us
  matrix products  184 us (46%)
  waiting for transfers between devices  104 us (26%)
  local copies, waits for them, and re-layouts  38.8 us (10%)
  starting transfers between devices  31.2 us (8%)
  loops' own time  20 us (5%)
  other arithmetic  11 us (3%)
    dot_general x16, matrix products, brick_down(): jnp.dot(hidden, w_out[layer], preferred_element_type=jnp.float32)  95 us
    all_to_all x1, waiting for transfers between devices, local(): lax.all_to_all(packed.reshape(width, cap, voxels * chan), 'gy', split_axi...  91.4 us
    dot_general x27, matrix products, local(): jnp.dot(moved, w_conv[d, e, f], preferred_element_type=jnp.float32)  66.8 us
    another operation x2, loops' own time, blockwise(): result = lax.map(lambda group: func(*group), shaped)  20 us
    dot_general x1, matrix products, local(): jnp.dot(picker_bf, flat.reshape(slots, voxels * chan), preferred_element_...  11.1 us
    dynamic_slice x18, local copies, waits for them, and re-layouts, blockwise(): result = lax.map(lambda group: func(*group), shaped)  10.9 us
    all_to_all x1, waiting for transfers between devices, local(): lax.all_to_all(returned.reshape(width, cap, 64 * chan), 'gy', split_axis=...  10.8 us
    dynamic_update_slice x10, local copies, waits for them, and re-layouts, blockwise(): result = lax.map(lambda group: func(*group), shaped)  8.95 us
  transfers between devices with their start and end apart: 7, of which 3 were waited for; matrix products, arithmetic and copies ran while one was open for 6% of the time, Pallas kernels for 0%

commit v1 on v0

v1 whole, which is shorter than its diff:
```python
import functools

import jax
import jax.numpy as jnp
from jax import lax
from jax.experimental import pallas as pl
from jax.experimental.pallas import tpu as pltpu
from jax.sharding import PartitionSpec as P

GROUP = 2
CHUNK = 256
VMEM_LIMIT = 56 * 1024 * 1024


def silu(value):
    half = 0.5 * value
    return half + half * jnp.tanh(half)


def down_kernel(
    owner_ref, feat_ref, gain_ref, shift_ref, w_in_ref, w_out_ref, w_down_ref, out_ref,
    held, stream, w_scaled, volume, index, sem,
):
    slots, voxels, chan = feat_ref.shape
    layers = w_in_ref.shape[0]
    cols_y, zcap = volume.shape[1] // 4, volume.shape[2] // 4

    def scan(slot, count):
        @pl.when(owner_ref[slot] >= 0)
        def _():
            index[count] = slot

        return count + (owner_ref[slot] >= 0).astype(jnp.int32)

    count = lax.fori_loop(0, slots, scan, 0)
    groups = (count + GROUP - 1) // GROUP

    def copies(group):
        side = lax.rem(group, 2)
        return [
            pltpu.make_async_copy(
                feat_ref.at[index[jnp.minimum(group * GROUP + b, count - 1)]],
                held.at[side, b],
                sem.at[side, b],
            )
            for b in range(GROUP)
        ]

    @pl.when(groups > 0)
    def _():
        for copy in copies(0):
            copy.start()

    for layer in range(layers):
        scale = 0.5 * gain_ref[:, layer : layer + 1]
        w_scaled[layer] = (w_in_ref[layer].astype(jnp.float32) * scale).astype(jnp.bfloat16)
    volume[...] = jnp.zeros_like(volume)

    pieces = GROUP * voxels // CHUNK

    def work(group, carry):
        @pl.when(group + 1 < groups)
        def _():
            for copy in copies(group + 1):
                copy.start()

        for copy in copies(group):
            copy.wait()
        side = lax.rem(group, 2)
        stream[...] = held[side].reshape(GROUP * voxels, chan).astype(jnp.float32)

        def enter(layer, piece):
            x = stream[piece * CHUNK : (piece + 1) * CHUNK]
            mean = jnp.mean(x * x, axis=-1, keepdims=True)
            normed = (x * lax.rsqrt(mean + 1e-6)).astype(jnp.bfloat16)
            return jnp.dot(normed, w_scaled[layer], preferred_element_type=jnp.float32)

        def leave(layer, piece, raw):
            half = (raw + 0.5 * shift_ref[pl.ds(layer, 1)]).astype(jnp.bfloat16)
            hidden = half + half * jnp.tanh(half)
            rows = slice(piece * CHUNK, (piece + 1) * CHUNK)
            stream[rows] = stream[rows] + jnp.dot(
                hidden, w_out_ref[layer], preferred_element_type=jnp.float32
            )

        def one_layer(layer, carry):
            raw = enter(layer, 0)
            for piece in range(pieces):
                later = enter(layer, piece + 1) if piece + 1 < pieces else None
                leave(layer, piece, raw)
                raw = later
            return carry

        lax.fori_loop(0, layers, one_layer, 0)

        weights = jnp.concatenate(
            [
                jnp.concatenate([w_down_ref[4 * a + c], w_down_ref[4 * a + 2 + c]], axis=1)
                for a in range(2)
                for c in range(2)
            ],
            axis=0,
        )
        for b in range(GROUP):
            slot = index[jnp.minimum(group * GROUP + b, count - 1)]
            taps = []
            for c in range(2):
                rows = stream[pl.ds(b * voxels + c, voxels // 2, stride=2)]
                taps.append(rows.astype(jnp.bfloat16).reshape(4, 2, 32, chan))
            cells = jnp.concatenate(
                [taps[c][:, a].reshape(128, chan) for a in range(2) for c in range(2)], axis=1
            )
            both = jnp.dot(cells, weights, preferred_element_type=jnp.float32)
            both = both.reshape(16, 8, 2 * chan)
            row = lax.broadcasted_iota(jnp.int32, (16, 8, chan), 1)
            part = jnp.where(row < 4, both[:, :, :chan], both[:, :, chan:])
            made = silu(part + pltpu.roll(part, 4, axis=1)).reshape(4, 4, 8, chan)
            z = lax.rem(slot, zcap)
            y = lax.rem(slot // zcap, cols_y)
            x = slot // (zcap * cols_y)
            where = (
                pl.ds(4 * x, 4),
                pl.ds(4 * y, 4),
                pl.ds(pl.multiple_of(8 * (z // 2), 8), 8),
            )
            row = lax.broadcasted_iota(jnp.int32, made.shape, 2)
            mine = (row // 4) == lax.rem(z, 2)
            volume[where] = jnp.where(mine, made, volume[where])
        return carry

    lax.fori_loop(0, groups, work, 0)
    out_ref[...] = volume[...].astype(jnp.bfloat16)


def up_kernel(cells_ref, feat_ref, live_ref, w_conv_ref, w_up_ref, out_ref, twice):
    chan = cells_ref.shape[-1]
    gsy, gsz = cells_ref.shape[1] - 2, cells_ref.shape[2]
    rows = gsy * gsz
    zcap = gsz // 4
    x = pl.program_id(0) * 4 + pl.program_id(1)
    planes = [cells_ref[x + d] for d in range(3)]
    near = jnp.concatenate(
        [planes[d][e : e + gsy].reshape(rows, chan) for d in range(3) for e in range(3)], axis=1
    )
    taps = jnp.concatenate(
        [
            jnp.concatenate([w_conv_ref[9 * d + 3 * e + f] for f in range(3)], axis=1)
            for d in range(3)
            for e in range(3)
        ],
        axis=0,
    )
    sums = jnp.dot(near, taps, preferred_element_type=jnp.float32).reshape(gsy, gsz, 3 * chan)
    z = lax.broadcasted_iota(jnp.int32, (gsy, gsz, chan), 1)
    below = jnp.where(z == 0, 0.0, pltpu.roll(sums[:, :, :chan], 1, axis=1))
    above = jnp.where(z == gsz - 1, 0.0, pltpu.roll(sums[:, :, 2 * chan :], gsz - 1, axis=1))
    total = planes[1][1 : 1 + gsy].astype(jnp.float32) + sums[:, :, chan : 2 * chan]
    total = (total + below + above).reshape(rows, chan)
    twice[pl.ds(0, rows, stride=2)] = total
    twice[pl.ds(1, rows, stride=2)] = total
    doubled = twice[...]
    odd = lax.rem(lax.broadcasted_iota(jnp.int32, doubled.shape, 0), 2) == 1
    split = jnp.concatenate(
        [jnp.where(odd, 0.0, doubled), jnp.where(odd, doubled, 0.0)], axis=1
    ).astype(jnp.bfloat16)
    weights = jnp.concatenate(
        [
            jnp.concatenate([w_up_ref[4 * a + 2 * b + c] for a in range(2) for b in range(2)], axis=1)
            for c in range(2)
        ],
        axis=0,
    )
    lifted = jnp.dot(split, weights, preferred_element_type=jnp.float32)
    line = 2 * gsz
    for q in range(gsy // 4):
        live = live_ref[0, q]
        live = jnp.concatenate([live, live], axis=1)
        for j in range(4):
            for a in range(2):
                top = lifted[(4 * q + j) * line : (4 * q + j + 1) * line]
                pair = [
                    top[:, (2 * a + b) * chan : (2 * a + b + 1) * chan].reshape(zcap, 8, chan)
                    for b in range(2)
                ]
                span = slice(64 * a + 16 * j, 64 * a + 16 * j + 16)
                whole = feat_ref[0, q, :, span].astype(jnp.float32) + jnp.concatenate(pair, axis=1)
                out_ref[0, q, :, span] = (whole * live).astype(jnp.bfloat16)


def extended(cells, sides, width):
    for axis, dim in sides:
        count = lax.axis_size(axis)
        ends = count - 1
        head = lax.slice_in_dim(cells, 0, width, axis=dim)
        tail = lax.slice_in_dim(cells, cells.shape[dim] - width, cells.shape[dim], axis=dim)
        cells = jnp.concatenate(
            [
                lax.ppermute(tail, axis, [(i, (i + 1) % count) for i in range(ends)]),
                cells,
                lax.ppermute(head, axis, [((i + 1) % count, i) for i in range(ends)]),
            ],
            axis=dim,
        )
    return cells


def local(features, owner, norm_gain, time_shift, w_in, w_out, w_down, w_conv, w_up):
    cols_x, cols_y, zcap, voxels, chan = features.shape
    slots = cols_x * cols_y * zcap
    gsx, gsy, gsz = cols_x * 4, cols_y * 4, zcap * 4
    layers, _, hid = w_in.shape
    vmem = pl.BlockSpec(memory_space=pltpu.VMEM)
    grid = pl.pallas_call(
        down_kernel,
        out_shape=jax.ShapeDtypeStruct((gsx, gsy, gsz, chan), jnp.bfloat16),
        in_specs=[
            pl.BlockSpec(memory_space=pltpu.SMEM),
            pl.BlockSpec(memory_space=pl.ANY),
            vmem, vmem, vmem, vmem, vmem,
        ],
        out_specs=vmem,
        scratch_shapes=[
            pltpu.VMEM((2, GROUP, voxels, chan), jnp.bfloat16),
            pltpu.VMEM((GROUP * voxels, chan), jnp.float32),
            pltpu.VMEM((layers, chan, hid), jnp.bfloat16),
            pltpu.VMEM((gsx, gsy, gsz, chan), jnp.float32),
            pltpu.SMEM((slots,), jnp.int32),
            pltpu.SemaphoreType.DMA((2, GROUP)),
        ],
        compiler_params=pltpu.CompilerParams(vmem_limit_bytes=VMEM_LIMIT),
        name="voxel_ff_down",
    )(
        owner.reshape(slots),
        features.reshape(slots, voxels, chan),
        norm_gain.T,
        time_shift,
        w_in,
        w_out,
        w_down.reshape(8, chan, chan),
    )
    rimmed = extended(grid, (("gx", 0), ("gy", 1)), 1)
    live = jnp.broadcast_to(
        (owner >= 0).astype(jnp.float32)[..., None, None], (cols_x, cols_y, zcap, 8, chan)
    )
    block = (1, cols_y, zcap, 2 * 64, chan)
    return pl.pallas_call(
        up_kernel,
        out_shape=jax.ShapeDtypeStruct(features.shape, jnp.bfloat16),
        grid=(cols_x, 4),
        in_specs=[
            vmem,
            pl.BlockSpec(block, lambda p, i: (p, 0, 0, i, 0)),
            pl.BlockSpec((1, cols_y, zcap, 8, chan), lambda p, i: (p, 0, 0, 0, 0)),
            vmem,
            vmem,
        ],
        out_specs=pl.BlockSpec(block, lambda p, i: (p, 0, 0, i, 0)),
        scratch_shapes=[pltpu.VMEM((2 * gsy * gsz, chan), jnp.float32)],
        compiler_params=pltpu.CompilerParams(vmem_limit_bytes=VMEM_LIMIT),
        name="conv_up",
    )(rimmed, features, live, w_conv.reshape(27, chan, chan), w_up.reshape(8, chan, chan))


def solution(mesh):
    in_specs = (
        P("gx", "gy", None, None, None),
        P("gx", "gy", None),
        P(),
        P(),
        P(),
        P(),
        P(),
        P(),
        P(),
    )
    out_specs = P("gx", "gy", None, None, None)
    return jax.shard_map(local, mesh=mesh, in_specs=in_specs, out_specs=out_specs, check_vma=False)
```

time: 396 us -> 193 us (0.49)
  the two profiles are of different devices: /device:TPU:9 before, /device:TPU:10 now
where the time goes in v1:
time: 193 us; the launch traced here: 190 us
  starting transfers between devices  130 us (67%)
  Pallas kernels  45.9 us (24%)
  waiting for transfers between devices  6.97 us (4%)
  local copies, waits for them, and re-layouts  4.66 us (2%)
  other arithmetic  2.48 us (1%)
    ppermute x2, starting transfers between devices, extended(): lax.ppermute(tail, axis, [(i, (i + 1) % count) for i in range(ends)])  77.1 us
    ppermute x2, starting transfers between devices, extended(): lax.ppermute(head, axis, [((i + 1) % count, i) for i in range(ends)])  53 us
    pallas_call x1, Pallas kernels, local(): pl.pallas_call(down_kernel, out_shape=jax.ShapeDtypeStruct((gsx, gsy, gsz...  31.9 us
    pallas_call x1, Pallas kernels, local(): pl.pallas_call(up_kernel, out_shape=jax.ShapeDtypeStruct(features.shape,...  14 us
    ppermute x2, waiting for transfers between devices, extended(): lax.ppermute(head, axis, [((i + 1) % count, i) for i in range(ends)])  5.53 us
  transfers between devices with their start and end apart: 4, of which 3 were waited for; matrix products, arithmetic and copies ran while one was open for 0% of the time, Pallas kernels for 0%

profile of v1, /device:TPU:10, one launch (start us, length us, event | category | flops | bytes accessed | tf_op | source)
XLA Modules:
  0.0 190.2 jit_solution(6409245069083303608)
XLA Ops:
  0.0 1.3 reshape.16.owner_ref
  1.3 1.4 copy.10
  2.7 31.9 %voxel_ff_down.1 = bf16[8,8,64,128]{3,2,1,0:T(8,128)(2,1)} custom-call(s32[64]{0:T(128)} %reshape.16.owner_ref, bf16[64,512,128]{2,1,0:T(8,128)(2,1)} %bitcast.5, f32[128,8]{1,0:T(8,128)} %bitcast.8, f32[8,512]{1,0:T(8,128)} %shift_ref.1, bf16[8,128,512]{2,1,0:T(8,128)(2,1)} %w_in_ref.1, bf16[8,512,128]{2,1,0:T(8,128)(2,1)} %w_out_ref.1, ...), custom_call_target="tpu_custom_call" | custom-call | tf_op jit(solution)/shard_map/voxel_ff_down/pallas_call | solution.py:213
  34.6 0.0 copy-start.1
  34.6 0.0 copy-start
  34.6 1.1 fusion
  35.7 75.1 %collective-permute-start = (bf16[1,8,64,128]{3,2,1,0:T(8,128)(2,1)S(1)}, bf16[1,8,64,128]{3,2,1,0:T(8,128)(2,1)S(1)}, u32[]{:S(2)}, u32[]{:S(2)}) collective-permute-start(bf16[1,8,64,128]{3,2,1,0:T(8,128)(2,1)S(1)} %get-tuple-element.7), channel_id=1, source_target_pairs={{0,8},{8,16},{16,24},{1,9},{9,17},{17,25},{2,10},{10,18},{18,26},{... | collective-permute-start | bytes 393224 | tf_op jit(solution)/shard_map/ppermute | solution.py:198
  110.9 1.9 %collective-permute-start.1 = (bf16[1,8,64,128]{3,2,1,0:T(8,128)(2,1)S(1)}, bf16[1,8,64,128]{3,2,1,0:T(8,128)(2,1)S(1)}, u32[]{:S(2)}, u32[]{:S(2)}) collective-permute-start(bf16[1,8,64,128]{3,2,1,0:T(8,128)(2,1)S(1)} %get-tuple-element.8), channel_id=1, source_target_pairs={{8,0},{16,8},{24,16},{9,1},{17,9},{25,17},{10,2},{18,10},{26,18},{... | collective-permute-start | bytes 393224 | tf_op jit(solution)/shard_map/ppermute | solution.py:200
  112.8 0.0 collective-permute-done
  112.8 2.5 %collective-permute-done.1 = bf16[1,8,64,128]{3,2,1,0:T(8,128)(2,1)S(1)} collective-permute-done((bf16[1,8,64,128]{3,2,1,0:T(8,128)(2,1)S(1)}, bf16[1,8,64,128]{3,2,1,0:T(8,128)(2,1)S(1)}, u32[]{:S(2)}, u32[]{:S(2)}) %collective-permute-start.1) | collective-permute-done | bytes 131104 | tf_op jit(solution)/shard_map/ppermute | solution.py:200
  115.3 1.0 pad_maximum_fusion.3
  116.3 1.9 %collective-permute-start.2 = (bf16[10,1,64,128]{3,2,1,0:T(8,128)(2,1)S(1)}, bf16[10,1,64,128]{3,2,1,0:T(8,128)(2,1)S(1)}, u32[]{:S(2)}, u32[]{:S(2)}) collective-permute-start(bf16[10,1,64,128]{3,2,1,0:T(8,128)(2,1)S(1)} %get-tuple-element.5), channel_id=1, source_target_pairs={{0,1},{1,2},{2,3},{3,4},{4,5},{5,6},{6,7},{8,9},{9,10},{10,11},{11... | collective-permute-start | bytes 491528 | tf_op jit(solution)/shard_map/ppermute | solution.py:198
  118.2 51.1 %collective-permute-start.3 = (bf16[10,1,64,128]{3,2,1,0:T(8,128)(2,1)S(1)}, bf16[10,1,64,128]{3,2,1,0:T(8,128)(2,1)S(1)}, u32[]{:S(2)}, u32[]{:S(2)}) collective-permute-start(bf16[10,1,64,128]{3,2,1,0:T(8,128)(2,1)S(1)} %get-tuple-element.6), channel_id=1, source_target_pairs={{1,0},{2,1},{3,2},{4,3},{5,4},{6,5},{7,6},{9,8},{10,9},{11,10},{12... | collective-permute-start | bytes 491528 | tf_op jit(solution)/shard_map/ppermute | solution.py:200
  169.3 0.0 copy-done.1
  169.4 1.4 collective-permute-done.2
  170.8 3.0 %collective-permute-done.3 = bf16[10,1,64,128]{3,2,1,0:T(8,128)(2,1)S(1)} collective-permute-done((bf16[10,1,64,128]{3,2,1,0:T(8,128)(2,1)S(1)}, bf16[10,1,64,128]{3,2,1,0:T(8,128)(2,1)S(1)}, u32[]{:S(2)}, u32[]{:S(2)}) %collective-permute-start.3) | collective-permute-done | bytes 163872 | tf_op jit(solution)/shard_map/ppermute | solution.py:200
  173.8 0.0 copy-done
  173.8 1.5 pad_maximum_fusion.cells_ref
  175.3 0.8 broadcast_in_dim.2.live_ref
  176.1 14.0 %conv_up.1 = bf16[2,2,16,512,128]{4,3,2,1,0:T(8,128)(2,1)} custom-call(bf16[10,10,64,128]{3,2,1,0:T(8,128)(2,1)} %pad_maximum_fusion.cells_ref, bf16[2,2,16,512,128]{4,3,2,1,0:T(8,128)(2,1)} %feat_ref.1, f32[2,2,16,8,128]{4,3,2,1,0:T(8,128)} %broadcast_in_dim.2.live_ref, bf16[27,128,128]{2,1,0:T(8,128)(2,1)} %bitcast.6, bf16[8,128,128]{2,1,0:T(8,128)(2,1)} %bitcast.7), custom_call_target="tpu_custom_call" | custom-call | tf_op jit(solution)/shard_map/conv_up/pallas_call | solution.py:246
  (1 shorter events, 0.0 us)
Async XLA Ops:
  34.6 134.7 %copy-start.1 = (s32[2,2,16]{2,1,0:T(2,128)S(1)}, s32[2,2,16]{2,1,0:T(2,128)}, u32[]{:S(2)}) copy-start(s32[2,2,16]{2,1,0:T(2,128)} %param.10) | copy-start | bytes 772
  34.6 139.2 %copy-start = (bf16[8,8,64,128]{3,2,1,0:T(8,128)(2,1)S(1)}, bf16[8,8,64,128]{3,2,1,0:T(8,128)(2,1)}, u32[]{:S(2)}) copy-start(bf16[8,8,64,128]{3,2,1,0:T(8,128)(2,1)} %voxel_ff_down.1) | copy-start | bytes 3145732
  35.7 77.1 %collective-permute-start = (bf16[1,8,64,128]{3,2,1,0:T(8,128)(2,1)S(1)}, bf16[1,8,64,128]{3,2,1,0:T(8,128)(2,1)S(1)}, u32[]{:S(2)}, u32[]{:S(2)}) collective-permute-start(bf16[1,8,64,128]{3,2,1,0:T(8,128)(2,1)S(1)} %get-tuple-element.7), channel_id=1, source_target_pairs={{0,8},{8,16},{16,24},{1,9},{9,17},{17,25},{2,10},{10,18},{18,26},{... | collective-permute-start | bytes 393224 | tf_op jit(solution)/shard_map/ppermute | solution.py:198
  110.9 4.4 %collective-permute-start.1 = (bf16[1,8,64,128]{3,2,1,0:T(8,128)(2,1)S(1)}, bf16[1,8,64,128]{3,2,1,0:T(8,128)(2,1)S(1)}, u32[]{:S(2)}, u32[]{:S(2)}) collective-permute-start(bf16[1,8,64,128]{3,2,1,0:T(8,128)(2,1)S(1)} %get-tuple-element.8), channel_id=1, source_target_pairs={{8,0},{16,8},{24,16},{9,1},{17,9},{25,17},{10,2},{18,10},{26,18},{... | collective-permute-start | bytes 393224 | tf_op jit(solution)/shard_map/ppermute | solution.py:200
  116.3 54.5 %collective-permute-start.2 = (bf16[10,1,64,128]{3,2,1,0:T(8,128)(2,1)S(1)}, bf16[10,1,64,128]{3,2,1,0:T(8,128)(2,1)S(1)}, u32[]{:S(2)}, u32[]{:S(2)}) collective-permute-start(bf16[10,1,64,128]{3,2,1,0:T(8,128)(2,1)S(1)} %get-tuple-element.5), channel_id=1, source_target_pairs={{0,1},{1,2},{2,3},{3,4},{4,5},{5,6},{6,7},{8,9},{9,10},{10,11},{11... | collective-permute-start | bytes 491528 | tf_op jit(solution)/shard_map/ppermute | solution.py:198
  118.2 55.6 %collective-permute-start.3 = (bf16[10,1,64,128]{3,2,1,0:T(8,128)(2,1)S(1)}, bf16[10,1,64,128]{3,2,1,0:T(8,128)(2,1)S(1)}, u32[]{:S(2)}, u32[]{:S(2)}) collective-permute-start(bf16[10,1,64,128]{3,2,1,0:T(8,128)(2,1)S(1)} %get-tuple-element.6), channel_id=1, source_target_pairs={{1,0},{2,1},{3,2},{4,3},{5,4},{6,5},{7,6},{9,8},{10,9},{11,10},{12... | collective-permute-start | bytes 491528 | tf_op jit(solution)/shard_map/ppermute | solution.py:200

commit v2 on v1

v2 whole, which is shorter than its diff:
```python
import functools

import jax
import jax.numpy as jnp
from jax import lax
from jax.experimental import pallas as pl
from jax.experimental.pallas import tpu as pltpu
from jax.sharding import PartitionSpec as P

GROUP = 4
CHUNK = 256
UNROLL = 2
VMEM_LIMIT = 56 * 1024 * 1024


def silu(value):
    half = 0.5 * value
    return half + half * jnp.tanh(half)


def down_kernel(
    owner_ref, feat_ref, gain_ref, shift_ref, w_in_ref, w_out_ref, w_down_ref, out_ref,
    held, stream, ahead, w_scaled, volume, index, sem,
):
    cols_x, cols_y, zcap, voxels, chan = feat_ref.shape
    slots = cols_x * cols_y * zcap
    layers = w_in_ref.shape[0]

    def place(slot):
        return slot // (zcap * cols_y), lax.rem(slot // zcap, cols_y), lax.rem(slot, zcap)

    def scan(slot, count):
        alive = owner_ref[place(slot)] >= 0

        @pl.when(alive)
        def _():
            index[count] = slot

        return count + alive.astype(jnp.int32)

    count = lax.fori_loop(0, slots, scan, 0)
    groups = (count + GROUP - 1) // GROUP

    def copies(group):
        side = lax.rem(group, 2)
        return [
            pltpu.make_async_copy(
                feat_ref.at[place(index[jnp.minimum(group * GROUP + b, count - 1)])],
                held.at[side, b],
                sem.at[side, b],
            )
            for b in range(GROUP)
        ]

    @pl.when(groups > 0)
    def _():
        for copy in copies(0):
            copy.start()

    across = lax.broadcasted_iota(jnp.int32, (chan, chan), 1)
    down = lax.broadcasted_iota(jnp.int32, (chan, chan), 0)
    for layer in range(layers):
        gain = jnp.where(across == down, 0.5 * gain_ref[layer : layer + 1], 0.0)
        gain = jnp.sum(gain, axis=1, keepdims=True)
        w_scaled[layer] = (w_in_ref[layer].astype(jnp.float32) * gain).astype(jnp.bfloat16)
    volume[...] = jnp.zeros_like(volume)

    pieces = GROUP * voxels // CHUNK

    def work(group, carry):
        @pl.when(group + 1 < groups)
        def _():
            for copy in copies(group + 1):
                copy.start()

        for copy in copies(group):
            copy.wait()
        side = lax.rem(group, 2)
        stream[...] = held[side].reshape(GROUP * voxels, chan).astype(jnp.float32)

        def enter(layer, piece):
            x = stream[piece * CHUNK : (piece + 1) * CHUNK]
            mean = jnp.mean(x * x, axis=-1, keepdims=True)
            normed = (x * lax.rsqrt(mean + 1e-6)).astype(jnp.bfloat16)
            raw = jnp.dot(normed, w_scaled[layer], preferred_element_type=jnp.float32)
            shift = (0.5 * shift_ref[pl.ds(layer, 1)]).astype(jnp.bfloat16)
            return raw.astype(jnp.bfloat16) + shift

        def leave(layer, piece, half):
            hidden = half + half * jnp.tanh(half)
            rows = slice(piece * CHUNK, (piece + 1) * CHUNK)
            stream[rows] = stream[rows] + jnp.dot(
                hidden, w_out_ref[layer], preferred_element_type=jnp.float32
            )

        def some_layers(step, carry):
            half = ahead[...]
            for more in range(UNROLL):
                layer = step * UNROLL + more
                for piece in range(pieces):
                    if piece + 1 < pieces:
                        later = enter(layer, piece + 1)
                    else:
                        later = enter(jnp.minimum(layer + 1, layers - 1), 0)
                    leave(layer, piece, half)
                    half = later
            ahead[...] = half
            return carry

        ahead[...] = enter(0, 0)
        lax.fori_loop(0, layers // UNROLL, some_layers, 0)

        weights = jnp.concatenate(
            [
                jnp.concatenate([w_down_ref[4 * a + c], w_down_ref[4 * a + 2 + c]], axis=1)
                for a in range(2)
                for c in range(2)
            ],
            axis=0,
        )
        for b in range(GROUP):
            slot = index[jnp.minimum(group * GROUP + b, count - 1)]
            taps = []
            for c in range(2):
                rows = stream[pl.ds(b * voxels + c, voxels // 2, stride=2)]
                taps.append(rows.astype(jnp.bfloat16).reshape(4, 2, 32, chan))
            cells = jnp.concatenate(
                [taps[c][:, a].reshape(128, chan) for a in range(2) for c in range(2)], axis=1
            )
            both = jnp.dot(cells, weights, preferred_element_type=jnp.float32)
            both = both.reshape(16, 8, 2 * chan)
            row = lax.broadcasted_iota(jnp.int32, (16, 8, chan), 1)
            part = jnp.where(row < 4, both[:, :, :chan], both[:, :, chan:])
            made = silu(part + pltpu.roll(part, 4, axis=1)).reshape(4, 4, 8, chan)
            x, y, z = place(slot)
            where = (
                pl.ds(4 * x, 4),
                pl.ds(4 * y, 4),
                pl.ds(pl.multiple_of(8 * (z // 2), 8), 8),
            )
            row = lax.broadcasted_iota(jnp.int32, made.shape, 2)
            mine = (row // 4) == lax.rem(z, 2)
            volume[where] = jnp.where(mine, made, volume[where])
        return carry

    lax.fori_loop(0, groups, work, 0)
    out_ref[...] = volume[...].astype(jnp.bfloat16)


def up_kernel(owner_ref, cells_ref, feat_ref, w_conv_ref, w_up_ref, out_ref, twice, live):
    chan = cells_ref.shape[-1]
    gsx, gsy, gsz = cells_ref.shape[0] - 2, cells_ref.shape[1] - 2, cells_ref.shape[2]
    rows = gsy * gsz
    zcap = gsz // 4
    step = pl.program_id(0)
    column = jnp.maximum(step - 1, 0) // 4
    side = lax.rem(step, 2)

    for q in range(gsy // 4):
        for r in range(zcap):
            alive = (owner_ref[column, q, r] >= 0).astype(jnp.float32)
            live[q, r] = jnp.full((16, chan), alive, jnp.float32)

    doubled = twice[1 - side]
    odd = lax.rem(lax.broadcasted_iota(jnp.int32, doubled.shape, 0), 2) == 1
    split = jnp.concatenate(
        [jnp.where(odd, 0.0, doubled), jnp.where(odd, doubled, 0.0)], axis=1
    ).astype(jnp.bfloat16)
    weights = jnp.concatenate(
        [
            jnp.concatenate([w_up_ref[4 * a + 2 * b + c] for a in range(2) for b in range(2)], axis=1)
            for c in range(2)
        ],
        axis=0,
    )
    line = 2 * gsz
    for q in range(gsy // 4):
        for j in range(4):
            span = slice((4 * q + j) * line, (4 * q + j + 1) * line)
            top = jnp.dot(split[span], weights, preferred_element_type=jnp.float32)
            for a in range(2):
                pair = [
                    top[:, (2 * a + b) * chan : (2 * a + b + 1) * chan].reshape(zcap, 8, chan)
                    for b in range(2)
                ]
                span = slice(64 * a + 16 * j, 64 * a + 16 * j + 16)
                whole = feat_ref[0, q, :, span].astype(jnp.float32) + jnp.concatenate(pair, axis=1)
                out_ref[0, q, :, span] = (whole * live[q]).astype(jnp.bfloat16)

    x = jnp.minimum(step, gsx - 1)
    planes = [cells_ref[x + d] for d in range(3)]
    near = jnp.concatenate(
        [planes[d][e : e + gsy].reshape(rows, chan) for d in range(3) for e in range(3)], axis=1
    )
    taps = jnp.concatenate(
        [
            jnp.concatenate([w_conv_ref[9 * d + 3 * e + f] for f in range(3)], axis=1)
            for d in range(3)
            for e in range(3)
        ],
        axis=0,
    )
    sums = jnp.dot(near, taps, preferred_element_type=jnp.float32).reshape(gsy, gsz, 3 * chan)
    z = lax.broadcasted_iota(jnp.int32, (gsy, gsz, chan), 1)
    below = jnp.where(z == 0, 0.0, pltpu.roll(sums[:, :, :chan], 1, axis=1))
    above = jnp.where(z == gsz - 1, 0.0, pltpu.roll(sums[:, :, 2 * chan :], gsz - 1, axis=1))
    total = planes[1][1 : 1 + gsy].astype(jnp.float32) + sums[:, :, chan : 2 * chan]
    total = (total + below + above).reshape(rows, chan)
    twice[side, pl.ds(0, rows, stride=2)] = total
    twice[side, pl.ds(1, rows, stride=2)] = total


def extended(cells, sides, width):
    for axis, dim in sides:
        count = lax.axis_size(axis)
        ends = count - 1
        head = lax.slice_in_dim(cells, 0, width, axis=dim)
        tail = lax.slice_in_dim(cells, cells.shape[dim] - width, cells.shape[dim], axis=dim)
        cells = jnp.concatenate(
            [
                lax.ppermute(tail, axis, [(i, (i + 1) % count) for i in range(ends)]),
                cells,
                lax.ppermute(head, axis, [((i + 1) % count, i) for i in range(ends)]),
            ],
            axis=dim,
        )
    return cells


def local(features, owner, norm_gain, time_shift, w_in, w_out, w_down, w_conv, w_up):
    cols_x, cols_y, zcap, voxels, chan = features.shape
    slots = cols_x * cols_y * zcap
    gsx, gsy, gsz = cols_x * 4, cols_y * 4, zcap * 4
    layers, _, hid = w_in.shape
    vmem = pl.BlockSpec(memory_space=pltpu.VMEM)
    grid = pl.pallas_call(
        down_kernel,
        out_shape=jax.ShapeDtypeStruct((gsx, gsy, gsz, chan), jnp.bfloat16),
        in_specs=[
            pl.BlockSpec(memory_space=pltpu.SMEM),
            pl.BlockSpec(memory_space=pl.ANY),
            vmem, vmem, vmem, vmem, vmem,
        ],
        out_specs=vmem,
        scratch_shapes=[
            pltpu.VMEM((2, GROUP, voxels, chan), jnp.bfloat16),
            pltpu.VMEM((GROUP * voxels, chan), jnp.float32),
            pltpu.VMEM((CHUNK, hid), jnp.bfloat16),
            pltpu.VMEM((layers, chan, hid), jnp.bfloat16),
            pltpu.VMEM((gsx, gsy, gsz, chan), jnp.float32),
            pltpu.SMEM((slots,), jnp.int32),
            pltpu.SemaphoreType.DMA((2, GROUP)),
        ],
        compiler_params=pltpu.CompilerParams(vmem_limit_bytes=VMEM_LIMIT),
        name="voxel_ff_down",
    )(
        owner,
        features,
        norm_gain,
        time_shift,
        w_in,
        w_out,
        w_down.reshape(8, chan, chan),
    )
    rimmed = extended(grid, (("gx", 0), ("gy", 1)), 1)
    block = (1, cols_y, zcap, 2 * 64, chan)

    def spot(step):
        plane = jnp.maximum(step - 1, 0)
        return plane // 4, 0, 0, lax.rem(plane, 4), 0

    return pl.pallas_call(
        up_kernel,
        out_shape=jax.ShapeDtypeStruct(features.shape, jnp.bfloat16),
        grid=(gsx + 1,),
        in_specs=[
            pl.BlockSpec(memory_space=pltpu.SMEM),
            vmem,
            pl.BlockSpec(block, spot),
            vmem,
            vmem,
        ],
        out_specs=pl.BlockSpec(block, spot),
        scratch_shapes=[
            pltpu.VMEM((2, 2 * gsy * gsz, chan), jnp.float32),
            pltpu.VMEM((cols_y, zcap, 16, chan), jnp.float32),
        ],
        compiler_params=pltpu.CompilerParams(vmem_limit_bytes=VMEM_LIMIT),
        name="conv_up",
    )(owner, rimmed, features, w_conv.reshape(27, chan, chan), w_up.reshape(8, chan, chan))


def solution(mesh):
    in_specs = (
        P("gx", "gy", None, None, None),
        P("gx", "gy", None),
        P(),
        P(),
        P(),
        P(),
        P(),
        P(),
        P(),
    )
    out_specs = P("gx", "gy", None, None, None)
    return jax.shard_map(local, mesh=mesh, in_specs=in_specs, out_specs=out_specs, check_vma=False)
```

time: 193 us -> 130 us (0.67)
  the two profiles are of different devices: /device:TPU:10 before, /device:TPU:17 now
where the time goes in v2:
time: 130 us; the launch traced here: 128 us
  Pallas kernels  62.9 us (48%)
  starting transfers between devices  33 us (25%)
  waiting for transfers between devices  28.4 us (22%)
  other arithmetic  2.48 us (2%)
    pallas_call x1, Pallas kernels, local(): pl.pallas_call(down_kernel, out_shape=jax.ShapeDtypeStruct((gsx, gsy, gsz...  47.7 us
    ppermute x2, waiting for transfers between devices, extended(): lax.ppermute(head, axis, [((i + 1) % count, i) for i in range(ends)])  27.6 us
    ppermute x2, starting transfers between devices, extended(): lax.ppermute(tail, axis, [(i, (i + 1) % count) for i in range(ends)])  26.9 us
    pallas_call x1, Pallas kernels, local(): pl.pallas_call(up_kernel, out_shape=jax.ShapeDtypeStruct(features.shape,...  15.2 us
    ppermute x2, starting transfers between devices, extended(): lax.ppermute(head, axis, [((i + 1) % count, i) for i in range(ends)])  6.18 us
  transfers between devices with their start and end apart: 4, of which 3 were waited for; matrix products, arithmetic and copies ran while one was open for 0% of the time, Pallas kernels for 0%

profile of v2, /device:TPU:17, one launch (start us, length us, event | category | flops | bytes accessed | tf_op | source)
XLA Modules:
  0.0 128.0 jit_solution(5335540747602648270)
XLA Ops:
  0.0 47.7 %voxel_ff_down.1 = bf16[8,8,64,128]{3,2,1,0:T(8,128)(2,1)} custom-call(s32[2,2,16]{2,1,0:T(2,128)} %owner_ref.3, bf16[2,2,16,512,128]{4,3,2,1,0:T(8,128)(2,1)} %feat_ref.3, f32[8,128]{1,0:T(8,128)} %gain_ref.1, f32[8,512]{1,0:T(8,128)} %shift_ref.1, bf16[8,128,512]{2,1,0:T(8,128)(2,1)} %w_in_ref.1, bf16[8,512,128]{2,1,0:T(8,128)(2,1)} %w_out_ref.1, ...), custom_call_target="tpu_custom_call" | custom-call | tf_op jit(solution)/shard_map/voxel_ff_down/pallas_call | solution.py:236
  47.7 0.0 copy-start
  47.7 1.1 fusion
  48.8 24.9 %collective-permute-start = (bf16[1,8,64,128]{3,2,1,0:T(8,128)(2,1)S(1)}, bf16[1,8,64,128]{3,2,1,0:T(8,128)(2,1)S(1)}, u32[]{:S(2)}, u32[]{:S(2)}) collective-permute-start(bf16[1,8,64,128]{3,2,1,0:T(8,128)(2,1)S(1)} %get-tuple-element.7), channel_id=1, source_target_pairs={{0,8},{8,16},{16,24},{1,9},{9,17},{17,25},{2,10},{10,18},{18,26},{... | collective-permute-start | bytes 393224 | tf_op jit(solution)/shard_map/ppermute | solution.py:221
  73.8 1.9 %collective-permute-start.1 = (bf16[1,8,64,128]{3,2,1,0:T(8,128)(2,1)S(1)}, bf16[1,8,64,128]{3,2,1,0:T(8,128)(2,1)S(1)}, u32[]{:S(2)}, u32[]{:S(2)}) collective-permute-start(bf16[1,8,64,128]{3,2,1,0:T(8,128)(2,1)S(1)} %get-tuple-element.8), channel_id=1, source_target_pairs={{8,0},{16,8},{24,16},{9,1},{17,9},{25,17},{10,2},{18,10},{26,18},{... | collective-permute-start | bytes 393224 | tf_op jit(solution)/shard_map/ppermute | solution.py:223
  75.7 0.0 collective-permute-done
  75.7 4.3 %collective-permute-done.1 = bf16[1,8,64,128]{3,2,1,0:T(8,128)(2,1)S(1)} collective-permute-done((bf16[1,8,64,128]{3,2,1,0:T(8,128)(2,1)S(1)}, bf16[1,8,64,128]{3,2,1,0:T(8,128)(2,1)S(1)}, u32[]{:S(2)}, u32[]{:S(2)}) %collective-permute-start.1) | collective-permute-done | bytes 131104 | tf_op jit(solution)/shard_map/ppermute | solution.py:223
  80.1 1.0 pad_maximum_fusion.3
  81.1 1.9 %collective-permute-start.2 = (bf16[10,1,64,128]{3,2,1,0:T(8,128)(2,1)S(1)}, bf16[10,1,64,128]{3,2,1,0:T(8,128)(2,1)S(1)}, u32[]{:S(2)}, u32[]{:S(2)}) collective-permute-start(bf16[10,1,64,128]{3,2,1,0:T(8,128)(2,1)S(1)} %get-tuple-element.5), channel_id=1, source_target_pairs={{0,1},{1,2},{2,3},{3,4},{4,5},{5,6},{6,7},{8,9},{9,10},{10,11},{11... | collective-permute-start | bytes 491528 | tf_op jit(solution)/shard_map/ppermute | solution.py:221
  83.0 4.3 %collective-permute-start.3 = (bf16[10,1,64,128]{3,2,1,0:T(8,128)(2,1)S(1)}, bf16[10,1,64,128]{3,2,1,0:T(8,128)(2,1)S(1)}, u32[]{:S(2)}, u32[]{:S(2)}) collective-permute-start(bf16[10,1,64,128]{3,2,1,0:T(8,128)(2,1)S(1)} %get-tuple-element.6), channel_id=1, source_target_pairs={{1,0},{2,1},{3,2},{4,3},{5,4},{6,5},{7,6},{9,8},{10,9},{11,10},{12... | collective-permute-start | bytes 491528 | tf_op jit(solution)/shard_map/ppermute | solution.py:223
  87.3 0.8 collective-permute-done.2
  88.0 23.3 %collective-permute-done.3 = bf16[10,1,64,128]{3,2,1,0:T(8,128)(2,1)S(1)} collective-permute-done((bf16[10,1,64,128]{3,2,1,0:T(8,128)(2,1)S(1)}, bf16[10,1,64,128]{3,2,1,0:T(8,128)(2,1)S(1)}, u32[]{:S(2)}, u32[]{:S(2)}) %collective-permute-start.3) | collective-permute-done | bytes 163872 | tf_op jit(solution)/shard_map/ppermute | solution.py:223
  111.3 0.0 copy-done
  111.3 1.5 %pad_maximum_fusion.cells_ref = bf16[10,10,64,128]{3,2,1,0:T(8,128)(2,1)} fusion(bf16[10,1,64,128]{3,2,1,0:T(8,128)(2,1)S(1)} %collective-permute-done.3, bf16[1,8,64,128]{3,2,1,0:T(8,128)(2,1)S(1)} %collective-permute-done.1, bf16[8,8,64,128]{3,2,1,0:T(8,128)(2,1)S(1)} %copy-done, bf16[1,8,64,128]{3,2,1,0:T(8,128)(2,1)S(1)} %collective-permute-done, ...), kind=kLoop, calls=%fused_computation | loop fusion | flops 3276800 | bytes 3276800 | tf_op jit(solution)/shard_map/concatenate | solution.py:219
  112.8 15.2 %conv_up.1 = bf16[2,2,16,512,128]{4,3,2,1,0:T(8,128)(2,1)} custom-call(s32[2,2,16]{2,1,0:T(2,128)} %owner_ref.3, bf16[10,10,64,128]{3,2,1,0:T(8,128)(2,1)} %pad_maximum_fusion.cells_ref, bf16[2,2,16,512,128]{4,3,2,1,0:T(8,128)(2,1)} %feat_ref.3, bf16[27,128,128]{2,1,0:T(8,128)(2,1)} %bitcast.3, bf16[8,128,128]{2,1,0:T(8,128)(2,1)} %bitcast.4), custom_call_target="tpu_custom_call" | custom-call | tf_op jit(solution)/shard_map/conv_up/pallas_call | solution.py:272
Async XLA Ops:
  47.7 63.6 %copy-start = (bf16[8,8,64,128]{3,2,1,0:T(8,128)(2,1)S(1)}, bf16[8,8,64,128]{3,2,1,0:T(8,128)(2,1)}, u32[]{:S(2)}) copy-start(bf16[8,8,64,128]{3,2,1,0:T(8,128)(2,1)} %voxel_ff_down.1) | copy-start | bytes 3145732
  48.8 26.9 %collective-permute-start = (bf16[1,8,64,128]{3,2,1,0:T(8,128)(2,1)S(1)}, bf16[1,8,64,128]{3,2,1,0:T(8,128)(2,1)S(1)}, u32[]{:S(2)}, u32[]{:S(2)}) collective-permute-start(bf16[1,8,64,128]{3,2,1,0:T(8,128)(2,1)S(1)} %get-tuple-element.7), channel_id=1, source_target_pairs={{0,8},{8,16},{16,24},{1,9},{9,17},{17,25},{2,10},{10,18},{18,26},{... | collective-permute-start | bytes 393224 | tf_op jit(solution)/shard_map/ppermute | solution.py:221
  73.8 6.3 %collective-permute-start.1 = (bf16[1,8,64,128]{3,2,1,0:T(8,128)(2,1)S(1)}, bf16[1,8,64,128]{3,2,1,0:T(8,128)(2,1)S(1)}, u32[]{:S(2)}, u32[]{:S(2)}) collective-permute-start(bf16[1,8,64,128]{3,2,1,0:T(8,128)(2,1)S(1)} %get-tuple-element.8), channel_id=1, source_target_pairs={{8,0},{16,8},{24,16},{9,1},{17,9},{25,17},{10,2},{18,10},{26,18},{... | collective-permute-start | bytes 393224 | tf_op jit(solution)/shard_map/ppermute | solution.py:223
  81.1 7.0 %collective-permute-start.2 = (bf16[10,1,64,128]{3,2,1,0:T(8,128)(2,1)S(1)}, bf16[10,1,64,128]{3,2,1,0:T(8,128)(2,1)S(1)}, u32[]{:S(2)}, u32[]{:S(2)}) collective-permute-start(bf16[10,1,64,128]{3,2,1,0:T(8,128)(2,1)S(1)} %get-tuple-element.5), channel_id=1, source_target_pairs={{0,1},{1,2},{2,3},{3,4},{4,5},{5,6},{6,7},{8,9},{9,10},{10,11},{11... | collective-permute-start | bytes 491528 | tf_op jit(solution)/shard_map/ppermute | solution.py:221
  83.0 28.3 %collective-permute-start.3 = (bf16[10,1,64,128]{3,2,1,0:T(8,128)(2,1)S(1)}, bf16[10,1,64,128]{3,2,1,0:T(8,128)(2,1)S(1)}, u32[]{:S(2)}, u32[]{:S(2)}) collective-permute-start(bf16[10,1,64,128]{3,2,1,0:T(8,128)(2,1)S(1)} %get-tuple-element.6), channel_id=1, source_target_pairs={{1,0},{2,1},{3,2},{4,3},{5,4},{6,5},{7,6},{9,8},{10,9},{11,10},{12... | collective-permute-start | bytes 491528 | tf_op jit(solution)/shard_map/ppermute | solution.py:223

commit v3 on v2

--- a/solution.py
+++ b/solution.py
@@ -8,7 +8,7 @@
 from jax.sharding import PartitionSpec as P
 
 GROUP = 4
-CHUNK = 256
+CHUNK = 512
 UNROLL = 2
 VMEM_LIMIT = 56 * 1024 * 1024
 
@@ -19,7 +19,8 @@
 
 
 def down_kernel(
-    owner_ref, feat_ref, gain_ref, shift_ref, w_in_ref, w_out_ref, w_down_ref, out_ref,
+    owner_ref, feat_ref, gain_ref, shift_ref, w_in_ref, w_out_ref, w_down_ref,
+    out_ref, x_low_ref, x_high_ref, y_low_ref, y_high_ref,
     held, stream, ahead, w_scaled, volume, index, sem,
 ):
     cols_x, cols_y, zcap, voxels, chan = feat_ref.shape
@@ -145,23 +146,90 @@
 
     lax.fori_loop(0, groups, work, 0)
     out_ref[...] = volume[...].astype(jnp.bfloat16)
-
-
-def up_kernel(owner_ref, cells_ref, feat_ref, w_conv_ref, w_up_ref, out_ref, twice, live):
-    chan = cells_ref.shape[-1]
-    gsx, gsy, gsz = cells_ref.shape[0] - 2, cells_ref.shape[1] - 2, cells_ref.shape[2]
+    x_low_ref[...] = out_ref[0]
+    x_high_ref[...] = out_ref[out_ref.shape[0] - 1]
+    y_low_ref[...] = out_ref[:, 0]
+    y_high_ref[...] = out_ref[:, out_ref.shape[1] - 1]
+
+
+def shifted(sums, chan):
+    z = lax.broadcasted_iota(jnp.int32, sums.shape[:2] + (chan,), 1)
+    length = sums.shape[1]
+    below = jnp.where(z == 0, 0.0, pltpu.roll(sums[:, :, :chan], 1, axis=1))
+    above = jnp.where(z == length - 1, 0.0, pltpu.roll(sums[:, :, 2 * chan :], length - 1, axis=1))
+    return sums[:, :, chan : 2 * chan] + below + above
+
+
+def conv_lines(pieces, w_conv_ref):
+    lines, gsz, chan = pieces[0][2].shape
+    near = jnp.concatenate([piece.reshape(lines * gsz, chan) for _, _, piece in pieces], axis=1)
+    taps = jnp.concatenate(
+        [
+            jnp.concatenate([w_conv_ref[9 * d + 3 * e + f] for f in range(3)], axis=1)
+            for d, e, _ in pieces
+        ],
+        axis=0,
+    )
+    sums = jnp.dot(near, taps, preferred_element_type=jnp.float32)
+    return shifted(sums.reshape(lines, gsz, 3 * chan), chan)
+
+
+def moved_lines(lines, e):
+    blank = jnp.zeros((1,) + lines.shape[1:], lines.dtype)
+    if e == 0:
+        return jnp.concatenate([blank, lines[:-1]], axis=0)
+    if e == 2:
+        return jnp.concatenate([lines[1:], blank], axis=0)
+    return lines
+
+
+def own_kernel(first, cells_ref, w_conv_ref, out_ref):
+    gsx = cells_ref.shape[0]
+    for plane in range(out_ref.shape[0]):
+        x = first + plane
+        pieces = [
+            (d, e, moved_lines(cells_ref[x + d - 1], e))
+            for d in range(3)
+            if 0 <= x + d - 1 < gsx
+            for e in range(3)
+        ]
+        total = cells_ref[x].astype(jnp.float32) + conv_lines(pieces, w_conv_ref)
+        out_ref[plane] = total.astype(jnp.bfloat16)
+
+
+def up_kernel(
+    owner_ref, near_ref, far_ref, x_low_ref, x_high_ref, y_low_ref, y_high_ref, feat_ref, w_conv_ref,
+    w_up_ref, out_ref, total, twice, live,
+):
+    gsx, gsy, gsz, chan = total.shape
     rows = gsy * gsz
     zcap = gsz // 4
     step = pl.program_id(0)
-    column = jnp.maximum(step - 1, 0) // 4
-    side = lax.rem(step, 2)
-
-    for q in range(gsy // 4):
-        for r in range(zcap):
-            alive = (owner_ref[column, q, r] >= 0).astype(jnp.float32)
-            live[q, r] = jnp.full((16, chan), alive, jnp.float32)
-
-    doubled = twice[1 - side]
+    column = step // 4
+
+    @pl.when(step == 0)
+    def _():
+        half = gsx // 2
+        total[:half] = near_ref[...].astype(jnp.float32)
+        total[half:] = far_ref[...].astype(jnp.float32)
+        for line, ref, e in ((0, y_low_ref, 0), (gsy - 1, y_high_ref, 2)):
+            pieces = [(d, e, ref[d : d + gsx]) for d in range(3)]
+            total[:, line] = total[:, line] + conv_lines(pieces, w_conv_ref)
+        for plane, ref, d in ((0, x_low_ref, 0), (gsx - 1, x_high_ref, 2)):
+            pieces = [(d, e, moved_lines(ref[...], e)) for e in range(3)]
+            total[plane] = total[plane] + conv_lines(pieces, w_conv_ref)
+
+    @pl.when(lax.rem(step, 4) == 0)
+    def _():
+        for q in range(gsy // 4):
+            for r in range(zcap):
+                alive = (owner_ref[column, q, r] >= 0).astype(jnp.float32)
+                live[q, r] = jnp.full((16, chan), alive, jnp.float32)
+
+    mixed = total[step].reshape(rows, chan)
+    twice[pl.ds(0, rows, stride=2)] = mixed
+    twice[pl.ds(1, rows, stride=2)] = mixed
+    doubled = twice[...]
     odd = lax.rem(lax.broadcasted_iota(jnp.int32, doubled.shape, 0), 2) == 1
     split = jnp.concatenate(
         [jnp.where(odd, 0.0, doubled), jnp.where(odd, doubled, 0.0)], axis=1
@@ -187,44 +255,11 @@
                 whole = feat_ref[0, q, :, span].astype(jnp.float32) + jnp.concatenate(pair, axis=1)
                 out_ref[0, q, :, span] = (whole * live[q]).astype(jnp.bfloat16)
 
-    x = jnp.minimum(step, gsx - 1)
-    planes = [cells_ref[x + d] for d in range(3)]
-    near = jnp.concatenate(
-        [planes[d][e : e + gsy].reshape(rows, chan) for d in range(3) for e in range(3)], axis=1
-    )
-    taps = jnp.concatenate(
-        [
-            jnp.concatenate([w_conv_ref[9 * d + 3 * e + f] for f in range(3)], axis=1)
-            for d in range(3)
-            for e in range(3)
-        ],
-        axis=0,
-    )
-    sums = jnp.dot(near, taps, preferred_element_type=jnp.float32).reshape(gsy, gsz, 3 * chan)
-    z = lax.broadcasted_iota(jnp.int32, (gsy, gsz, chan), 1)
-    below = jnp.where(z == 0, 0.0, pltpu.roll(sums[:, :, :chan], 1, axis=1))
-    above = jnp.where(z == gsz - 1, 0.0, pltpu.roll(sums[:, :, 2 * chan :], gsz - 1, axis=1))
-    total = planes[1][1 : 1 + gsy].astype(jnp.float32) + sums[:, :, chan : 2 * chan]
-    total = (total + below + above).reshape(rows, chan)
-    twice[side, pl.ds(0, rows, stride=2)] = total
-    twice[side, pl.ds(1, rows, stride=2)] = total
-
-
-def extended(cells, sides, width):
-    for axis, dim in sides:
-        count = lax.axis_size(axis)
-        ends = count - 1
-        head = lax.slice_in_dim(cells, 0, width, axis=dim)
-        tail = lax.slice_in_dim(cells, cells.shape[dim] - width, cells.shape[dim], axis=dim)
-        cells = jnp.concatenate(
-            [
-                lax.ppermute(tail, axis, [(i, (i + 1) % count) for i in range(ends)]),
-                cells,
-                lax.ppermute(head, axis, [((i + 1) % count, i) for i in range(ends)]),
-            ],
-            axis=dim,
-        )
-    return cells
+
+def exchange(low, high, axis):
+    count = lax.axis_size(axis)
+    up = [(i, i + 1) for i in range(count - 1)]
+    return lax.ppermute(high, axis, up), lax.ppermute(low, axis, [(j, i) for i, j in up])
 
 
 def local(features, owner, norm_gain, time_shift, w_in, w_out, w_down, w_conv, w_up):
@@ -233,15 +268,17 @@
     gsx, gsy, gsz = cols_x * 4, cols_y * 4, zcap * 4
     layers, _, hid = w_in.shape
     vmem = pl.BlockSpec(memory_space=pltpu.VMEM)
-    grid = pl.pallas_call(
+    smem = pl.BlockSpec(memory_space=pltpu.SMEM)
+    params = pltpu.CompilerParams(vmem_limit_bytes=VMEM_LIMIT)
+
+    def cells(*shape):
+        return jax.ShapeDtypeStruct(shape + (gsz, chan), jnp.bfloat16)
+
+    grid, x_low, x_high, y_low, y_high = pl.pallas_call(
         down_kernel,
-        out_shape=jax.ShapeDtypeStruct((gsx, gsy, gsz, chan), jnp.bfloat16),
-        in_specs=[
-            pl.BlockSpec(memory_space=pltpu.SMEM),
-            pl.BlockSpec(memory_space=pl.ANY),
-            vmem, vmem, vmem, vmem, vmem,
-        ],
-        out_specs=vmem,
+        out_shape=[cells(gsx, gsy), cells(gsy), cells(gsy), cells(gsx), cells(gsx)],
+        in_specs=[smem, pl.BlockSpec(memory_space=pl.ANY), vmem, vmem, vmem, vmem, vmem],
+        out_specs=[vmem] * 5,
         scratch_shapes=[
             pltpu.VMEM((2, GROUP, voxels, chan), jnp.bfloat16),
             pltpu.VMEM((GROUP * voxels, chan), jnp.float32),
@@ -251,43 +288,53 @@
             pltpu.SMEM((slots,), jnp.int32),
             pltpu.SemaphoreType.DMA((2, GROUP)),
         ],
-        compiler_params=pltpu.CompilerParams(vmem_limit_bytes=VMEM_LIMIT),
+        compiler_params=params,
         name="voxel_ff_down",
-    )(
-        owner,
-        features,
-        norm_gain,
-        time_shift,
-        w_in,
-        w_out,
-        w_down.reshape(8, chan, chan),
-    )
-    rimmed = extended(grid, (("gx", 0), ("gy", 1)), 1)
+    )(owner, features, norm_gain, time_shift, w_in, w_out, w_down.reshape(8, chan, chan))
+
+    taps = w_conv.reshape(27, chan, chan)
+    half = gsx // 2
+    flops = 2 * 27 * half * gsy * gsz * chan * chan
+    own = [
+        pl.pallas_call(
+            functools.partial(own_kernel, first),
+            out_shape=cells(half, gsy),
+            in_specs=[vmem, vmem],
+            out_specs=vmem,
+            compiler_params=params,
+            cost_estimate=pl.CostEstimate(
+                flops=4 * flops, bytes_accessed=4 * 1024 * 1024, transcendentals=0
+            ),
+            name="conv_own",
+        )(grid, taps)
+        for first in (0, half)
+    ]
+    x_low, x_high = exchange(x_low, x_high, "gx")
+    y_low = jnp.concatenate([x_low[:1], y_low, x_high[:1]], axis=0)
+    y_high = jnp.concatenate([x_low[-1:], y_high, x_high[-1:]], axis=0)
+    y_low, y_high = exchange(y_low, y_high, "gy")
+
     block = (1, cols_y, zcap, 2 * 64, chan)
 
-    def spot(step):
-        plane = jnp.maximum(step - 1, 0)
+    def spot(plane):
         return plane // 4, 0, 0, lax.rem(plane, 4), 0
 
     return pl.pallas_call(
         up_kernel,
         out_shape=jax.ShapeDtypeStruct(features.shape, jnp.bfloat16),
-        grid=(gsx + 1,),
-        in_specs=[
-            pl.BlockSpec(memory_space=pltpu.SMEM),
-            vmem,
-            pl.BlockSpec(block, spot),
-            vmem,
-            vmem,
-        ],
+        grid=(gsx,),
+        in_specs=[smem] + [vmem] * 6 + [pl.BlockSpec(block, spot), vmem, vmem],
         out_specs=pl.BlockSpec(block, spot),
         scratch_shapes=[
-            pltpu.VMEM((2, 2 * gsy * gsz, chan), jnp.float32),
+            pltpu.VMEM((gsx, gsy, gsz, chan), jnp.float32),
+            pltpu.VMEM((2 * gsy * gsz, chan), jnp.float32),
             pltpu.VMEM((cols_y, zcap, 16, chan), jnp.float32),
         ],
-        compiler_params=pltpu.CompilerParams(vmem_limit_bytes=VMEM_LIMIT),
-        name="conv_up",
-    )(owner, rimmed, features, w_conv.reshape(27, chan, chan), w_up.reshape(8, chan, chan))
+        compiler_params=params,
+        name="rim_up",
+    )(
+        owner, *own, x_low, x_high, y_low, y_high, features, taps, w_up.reshape(8, chan, chan)
+    )
 
 
 def solution(mesh):

time: 130 us -> 126 us (0.969)
  the two profiles are of different devices: /device:TPU:17 before, /device:TPU:10 now
where the time goes in v3:
time: 126 us
  Pallas kernels  70.3 us (56%)
  starting transfers between devices  53.1 us (42%)
  waiting for transfers between devices  1.29 us (1%)
    pallas_call x1, Pallas kernels, local(): pl.pallas_call(down_kernel, out_shape=[cells(gsx, gsy), cells(gsy), cells...  47.9 us
    ppermute x2, starting transfers between devices, exchange(): lax.ppermute(high, axis, up)  46.3 us
    pallas_call x1, Pallas kernels, local(): pl.pallas_call(up_kernel, out_shape=jax.ShapeDtypeStruct(features.shape,...  12.7 us
    pallas_call x2, Pallas kernels, local(): pl.pallas_call(functools.partial(own_kernel, first), out_shape=cells(half...  9.63 us
    ppermute x2, starting transfers between devices, exchange(): lax.ppermute(low, axis, [(j, i) for i, j in up])  6.74 us
  transfers between devices with their start and end apart: 4, of which 1 were waited for; matrix products, arithmetic and copies ran while one was open for 0% of the time, Pallas kernels for 8%

profile of v3, /device:TPU:10, one launch (start us, length us, event | category | flops | bytes accessed | tf_op | source)
XLA Modules:
  0.0 125.5 jit_solution(3737704629616702587)
XLA Ops:
  0.0 47.9 %voxel_ff_down.1 = (bf16[8,8,64,128]{3,2,1,0:T(8,128)(2,1)}, bf16[8,64,128]{2,1,0:T(8,128)(2,1)}, bf16[8,64,128]{2,1,0:T(8,128)(2,1)}, bf16[8,64,128]{2,1,0:T(8,128)(2,1)}, bf16[8,64,128]{2,1,0:T(8,128)(2,1)}) custom-call(s32[2,2,16]{2,1,0:T(2,128)} %owner_ref.3, bf16[2,2,16,512,128]{4,3,2,1,0:T(8,128)(2,1)} %feat_ref.3, f32[8,128]{1,0:T(8,128)} %gain_ref.1, ...), custom_call_target="tpu_custom_call" | custom-call | tf_op jit(solution)/shard_map/voxel_ff_down/pallas_call | solution.py:277
  47.9 44.4 %collective-permute-start = (bf16[8,64,128]{2,1,0:T(8,128)(2,1)}, bf16[8,64,128]{2,1,0:T(8,128)(2,1)S(1)}, u32[]{:S(2)}, u32[]{:S(2)}) collective-permute-start(bf16[8,64,128]{2,1,0:T(8,128)(2,1)} %get-tuple-element.11), channel_id=1, source_target_pairs={{0,8},{8,16},{16,24},{1,9},{9,17},{17,25},{2,10},{10,18},{18,26},{... | collective-permute-start | bytes 393224 | tf_op jit(solution)/shard_map/ppermute | solution.py:262
  92.3 1.9 %collective-permute-start.1 = (bf16[8,64,128]{2,1,0:T(8,128)(2,1)}, bf16[8,64,128]{2,1,0:T(8,128)(2,1)S(1)}, u32[]{:S(2)}, u32[]{:S(2)}) collective-permute-start(bf16[8,64,128]{2,1,0:T(8,128)(2,1)} %get-tuple-element.12), channel_id=1, source_target_pairs={{8,0},{16,8},{24,16},{9,1},{17,9},{25,17},{10,2},{18,10},{26,18},{... | collective-permute-start | bytes 393224 | tf_op jit(solution)/shard_map/ppermute | solution.py:262
  94.3 0.0 copy-start.5
  94.3 0.0 copy-start.4
  94.3 4.8 %conv_own.3.far_ref = bf16[4,8,64,128]{3,2,1,0:T(8,128)(2,1)} custom-call(bf16[8,8,64,128]{3,2,1,0:T(8,128)(2,1)} %get-tuple-element.10.cells_ref, bf16[27,128,128]{2,1,0:T(8,128)(2,1)} %bitcast.3), custom_call_target="tpu_custom_call" | custom-call | flops 7247757312 | bytes 4194304 | tf_op jit(solution)/shard_map/conv_own/pallas_call | solution.py:299
  99.1 0.0 collective-permute-done.x_low_ref
  99.1 0.0 copy-start
  99.1 0.0 collective-permute-done.1.x_high_ref
  99.2 0.0 copy-start.1
  99.2 0.0 copy-done.5
  99.2 1.9 %collective-permute-start.2 = (bf16[10,64,128]{2,1,0:T(8,128)(2,1)S(1)}, bf16[10,64,128]{2,1,0:T(8,128)(2,1)S(1)}, u32[]{:S(2)}, u32[]{:S(2)}) collective-permute-start(bf16[10,64,128]{2,1,0:T(8,128)(2,1)S(1)} %pad_maximum_fusion), channel_id=1, source_target_pairs={{0,1},{1,2},{2,3},{3,4},{4,5},{5,6},{6,7},{8,9},{9,10},{10,11},{11... | collective-permute-start | bytes 491528 | tf_op jit(solution)/shard_map/ppermute | solution.py:262
  101.1 0.0 copy-done.4
  101.2 4.8 %collective-permute-start.3 = (bf16[10,64,128]{2,1,0:T(8,128)(2,1)S(1)}, bf16[10,64,128]{2,1,0:T(8,128)(2,1)S(1)}, u32[]{:S(2)}, u32[]{:S(2)}) collective-permute-start(bf16[10,64,128]{2,1,0:T(8,128)(2,1)S(1)} %pad_maximum_fusion.1), channel_id=1, source_target_pairs={{1,0},{2,1},{3,2},{4,3},{5,4},{6,5},{7,6},{9,8},{10,9},{11,10},{12... | collective-permute-start | bytes 491528 | tf_op jit(solution)/shard_map/ppermute | solution.py:262
  106.0 4.8 %conv_own.2.near_ref = bf16[4,8,64,128]{3,2,1,0:T(8,128)(2,1)} custom-call(bf16[8,8,64,128]{3,2,1,0:T(8,128)(2,1)} %get-tuple-element.10.cells_ref, bf16[27,128,128]{2,1,0:T(8,128)(2,1)} %bitcast.4), custom_call_target="tpu_custom_call" | custom-call | flops 7247757312 | bytes 4194304 | tf_op jit(solution)/shard_map/conv_own/pallas_call | solution.py:299
  110.8 0.0 copy-done
  110.8 0.0 copy-done.1
  110.8 0.0 collective-permute-done.2.y_low_ref
  110.8 0.0 copy-start.2
  110.8 1.3 %collective-permute-done.3.y_high_ref = bf16[10,64,128]{2,1,0:T(8,128)(2,1)S(1)} collective-permute-done((bf16[10,64,128]{2,1,0:T(8,128)(2,1)S(1)}, bf16[10,64,128]{2,1,0:T(8,128)(2,1)S(1)}, u32[]{:S(2)}, u32[]{:S(2)}) %collective-permute-start.3) | collective-permute-done | bytes 163872 | tf_op jit(solution)/shard_map/ppermute | solution.py:262
  112.1 0.0 copy-start.3
  112.1 0.0 copy-done.2
  112.1 0.7 copy-done.3
  112.8 12.7 %rim_up.1 = bf16[2,2,16,512,128]{4,3,2,1,0:T(8,128)(2,1)} custom-call(s32[2,2,16]{2,1,0:T(2,128)} %owner_ref.3, bf16[4,8,64,128]{3,2,1,0:T(8,128)(2,1)} %conv_own.2.near_ref, bf16[4,8,64,128]{3,2,1,0:T(8,128)(2,1)} %conv_own.3.far_ref, bf16[8,64,128]{2,1,0:T(8,128)(2,1)} %copy-done, bf16[8,64,128]{2,1,0:T(8,128)(2,1)} %copy-done.1, ...), custom_call_target="tpu_custom_call" | custom-call | tf_op jit(solution)/shard_map/rim_up/pallas_call | solution.py:322
  (4 shorter events, 0.1 us)
Async XLA Ops:
  47.9 51.2 %collective-permute-start = (bf16[8,64,128]{2,1,0:T(8,128)(2,1)}, bf16[8,64,128]{2,1,0:T(8,128)(2,1)S(1)}, u32[]{:S(2)}, u32[]{:S(2)}) collective-permute-start(bf16[8,64,128]{2,1,0:T(8,128)(2,1)} %get-tuple-element.11), channel_id=1, source_target_pairs={{0,8},{8,16},{16,24},{1,9},{9,17},{17,25},{2,10},{10,18},{18,26},{... | collective-permute-start | bytes 393224 | tf_op jit(solution)/shard_map/ppermute | solution.py:262
  92.3 6.8 %collective-permute-start.1 = (bf16[8,64,128]{2,1,0:T(8,128)(2,1)}, bf16[8,64,128]{2,1,0:T(8,128)(2,1)S(1)}, u32[]{:S(2)}, u32[]{:S(2)}) collective-permute-start(bf16[8,64,128]{2,1,0:T(8,128)(2,1)} %get-tuple-element.12), channel_id=1, source_target_pairs={{8,0},{16,8},{24,16},{9,1},{17,9},{25,17},{10,2},{18,10},{26,18},{... | collective-permute-start | bytes 393224 | tf_op jit(solution)/shard_map/ppermute | solution.py:262
  94.3 4.9 %copy-start.5 = (bf16[8,64,128]{2,1,0:T(8,128)(2,1)S(1)}, bf16[8,64,128]{2,1,0:T(8,128)(2,1)}, u32[]{:S(2)}) copy-start(bf16[8,64,128]{2,1,0:T(8,128)(2,1)} %get-tuple-element.13) | copy-start | bytes 393220
  94.3 6.9 %copy-start.4 = (bf16[8,64,128]{2,1,0:T(8,128)(2,1)S(1)}, bf16[8,64,128]{2,1,0:T(8,128)(2,1)}, u32[]{:S(2)}) copy-start(bf16[8,64,128]{2,1,0:T(8,128)(2,1)} %get-tuple-element.14) | copy-start | bytes 393220
  99.1 11.7 %copy-start = (bf16[8,64,128]{2,1,0:T(8,128)(2,1)}, bf16[8,64,128]{2,1,0:T(8,128)(2,1)S(1)}, u32[]{:S(2)}) copy-start(bf16[8,64,128]{2,1,0:T(8,128)(2,1)S(1)} %collective-permute-done.x_low_ref) | copy-start | bytes 393220
  99.2 11.7 %copy-start.1 = (bf16[8,64,128]{2,1,0:T(8,128)(2,1)}, bf16[8,64,128]{2,1,0:T(8,128)(2,1)S(1)}, u32[]{:S(2)}) copy-start(bf16[8,64,128]{2,1,0:T(8,128)(2,1)S(1)} %collective-permute-done.1.x_high_ref) | copy-start | bytes 393220
  99.2 11.6 %collective-permute-start.2 = (bf16[10,64,128]{2,1,0:T(8,128)(2,1)S(1)}, bf16[10,64,128]{2,1,0:T(8,128)(2,1)S(1)}, u32[]{:S(2)}, u32[]{:S(2)}) collective-permute-start(bf16[10,64,128]{2,1,0:T(8,128)(2,1)S(1)} %pad_maximum_fusion), channel_id=1, source_target_pairs={{0,1},{1,2},{2,3},{3,4},{4,5},{5,6},{6,7},{8,9},{9,10},{10,11},{11... | collective-permute-start | bytes 491528 | tf_op jit(solution)/shard_map/ppermute | solution.py:262
  101.2 10.9 %collective-permute-start.3 = (bf16[10,64,128]{2,1,0:T(8,128)(2,1)S(1)}, bf16[10,64,128]{2,1,0:T(8,128)(2,1)S(1)}, u32[]{:S(2)}, u32[]{:S(2)}) collective-permute-start(bf16[10,64,128]{2,1,0:T(8,128)(2,1)S(1)} %pad_maximum_fusion.1), channel_id=1, source_target_pairs={{1,0},{2,1},{3,2},{4,3},{5,4},{6,5},{7,6},{9,8},{10,9},{11,10},{12... | collective-permute-start | bytes 491528 | tf_op jit(solution)/shard_map/ppermute | solution.py:262
  110.8 1.3 %copy-start.2 = (bf16[10,64,128]{2,1,0:T(8,128)(2,1)}, bf16[10,64,128]{2,1,0:T(8,128)(2,1)S(1)}, u32[]{:S(2)}) copy-start(bf16[10,64,128]{2,1,0:T(8,128)(2,1)S(1)} %collective-permute-done.2.y_low_ref) | copy-start | bytes 491524
  112.1 0.7 copy-start.3

commit v4 on v3

v4 whole, which is shorter than its diff:
```python
import functools

import jax
import jax.numpy as jnp
from jax import lax
from jax.experimental import pallas as pl
from jax.experimental.pallas import tpu as pltpu
from jax.sharding import PartitionSpec as P

GROUP = 4
MOST = 32
VMEM_LIMIT = 56 * 1024 * 1024


def silu(value):
    half = 0.5 * value
    return half + half * jnp.tanh(half)


def place(slot, cols_y, zcap):
    return slot // (zcap * cols_y), lax.rem(slot // zcap, cols_y), lax.rem(slot, zcap)


def down_kernel(
    owner_ref, feat_ref, gain_ref, shift_ref, w_in_ref, w_out_ref, w_down_ref,
    out_ref, x_low_ref, x_high_ref, y_low_ref, y_high_ref, blank_ref,
    held, stream, made, w_in, w_out, volume, zeros, index, sem, w_sem, zero_sem,
):
    cols_x, cols_y, zcap, voxels, chan = feat_ref.shape
    slots = cols_x * cols_y * zcap
    layers = w_in.shape[0]
    loads = [
        pltpu.make_async_copy(w_in_ref, w_in, w_sem.at[0]),
        pltpu.make_async_copy(w_out_ref, w_out, w_sem.at[1]),
    ]
    for load in loads:
        load.start()
    zeros[...] = jnp.zeros_like(zeros)

    def at(slot):
        return place(slot, cols_y, zcap)

    def blank(slot):
        return pltpu.make_async_copy(zeros, blank_ref.at[at(slot)], zero_sem.at[slot])

    def scan(slot, count):
        alive = owner_ref[at(slot)] >= 0

        @pl.when(alive)
        def _():
            index[count] = slot

        return count + alive.astype(jnp.int32)

    count = lax.fori_loop(0, slots, scan, 0)
    groups = (count + GROUP - 1) // GROUP

    def slot_of(group, b):
        return index[jnp.minimum(group * GROUP + b, count - 1)]

    def copies(group):
        side = lax.rem(group, 2)
        return [
            pltpu.make_async_copy(
                feat_ref.at[at(slot_of(group, b))], held.at[side, b], sem.at[side, b]
            )
            for b in range(GROUP)
        ]

    @pl.when(groups > 0)
    def _():
        for copy in copies(0):
            copy.start()

    @pl.loop(0, slots)
    def _(slot):
        @pl.when(owner_ref[at(slot)] < 0)
        def _():
            blank(slot).start()

    volume[...] = jnp.zeros_like(volume)
    across = lax.broadcasted_iota(jnp.int32, (chan, chan), 1)
    below = lax.broadcasted_iota(jnp.int32, (chan, chan), 0)
    loads[0].wait()
    for layer in range(layers):
        gain = jnp.where(across == below, gain_ref[layer : layer + 1], 0.0)
        gain = jnp.sum(gain, axis=1, keepdims=True) * (0.5 * chan**0.5)
        w_in[layer] = (w_in[layer].astype(jnp.float32) * gain).astype(jnp.bfloat16)
    loads[1].wait()

    def down(group, b):
        slot = slot_of(group, b)
        weights = jnp.concatenate(
            [
                jnp.concatenate([w_down_ref[4 * a + c], w_down_ref[4 * a + 2 + c]], axis=1)
                for a in range(2)
                for c in range(2)
            ],
            axis=0,
        )
        taps = []
        for c in range(2):
            rows = made[b, pl.ds(c, voxels // 2, stride=2)]
            taps.append(rows.astype(jnp.bfloat16).reshape(4, 2, 32, chan))
        cells = jnp.concatenate(
            [taps[c][:, a].reshape(128, chan) for a in range(2) for c in range(2)], axis=1
        )
        both = jnp.dot(cells, weights, preferred_element_type=jnp.float32)
        both = both.reshape(16, 8, 2 * chan)
        row = lax.broadcasted_iota(jnp.int32, (16, 8, chan), 1)
        part = jnp.where(row < 4, both[:, :, :chan], both[:, :, chan:])
        coarse = silu(part + pltpu.roll(part, 4, axis=1)).reshape(4, 4, 8, chan)
        x, y, z = at(slot)
        where = (
            pl.ds(4 * x, 4),
            pl.ds(4 * y, 4),
            pl.ds(pl.multiple_of(8 * (z // 2), 8), 8),
        )
        row = lax.broadcasted_iota(jnp.int32, coarse.shape, 2)
        mine = (row // 4) == lax.rem(z, 2)
        volume[where] = jnp.where(mine, coarse, volume[where])

    def work(group, carry):
        @pl.when(group + 1 < groups)
        def _():
            for copy in copies(group + 1):
                copy.start()

        for copy in copies(group):
            copy.wait()
        side = lax.rem(group, 2)

        def value(layer, b):
            return held[side, b].astype(jnp.float32) if layer == 0 else stream[b]

        def enter(layer, b):
            x = value(layer, b)
            power = jnp.sum(x * x, axis=-1, keepdims=True)
            normed = (x * lax.rsqrt(power + chan * 1e-6)).astype(jnp.bfloat16)
            raw = jnp.dot(normed, w_in[layer], preferred_element_type=jnp.float32)
            shift = (0.5 * shift_ref[layer : layer + 1]).astype(jnp.bfloat16)
            return raw.astype(jnp.bfloat16) + shift

        def leave(layer, b, half):
            hidden = half + half * jnp.tanh(half)
            result = value(layer, b) + jnp.dot(
                hidden, w_out[layer], preferred_element_type=jnp.float32
            )
            if layer + 1 < layers:
                stream[b] = result
            else:
                made[b] = result

        order = [(layer, b) for layer in range(layers) for b in range(GROUP)]
        half = enter(*order[0])
        for spot, here in enumerate(order):
            later = enter(*order[spot + 1]) if spot + 1 < len(order) else None
            leave(*here, half)
            if here[0] == 1:
                down(jnp.maximum(group - 1, 0), here[1])
            half = later
        return carry

    lax.fori_loop(0, groups, work, 0)

    @pl.when(groups > 0)
    def _():
        for b in range(GROUP):
            down(groups - 1, b)

    out_ref[...] = volume[...].astype(jnp.bfloat16)
    x_low_ref[...] = out_ref[0]
    x_high_ref[...] = out_ref[out_ref.shape[0] - 1]
    y_low_ref[...] = out_ref[:, 0]
    y_high_ref[...] = out_ref[:, out_ref.shape[1] - 1]

    @pl.loop(0, slots)
    def _(slot):
        @pl.when(owner_ref[at(slot)] < 0)
        def _():
            blank(slot).wait()


def shifted(sums, chan):
    z = lax.broadcasted_iota(jnp.int32, sums.shape[:2] + (chan,), 1)
    length = sums.shape[1]
    below = jnp.where(z == 0, 0.0, pltpu.roll(sums[:, :, :chan], 1, axis=1))
    above = jnp.where(z == length - 1, 0.0, pltpu.roll(sums[:, :, 2 * chan :], length - 1, axis=1))
    return sums[:, :, chan : 2 * chan] + below + above


def conv_lines(pieces, w_conv_ref):
    lines, gsz, chan = pieces[0][2].shape
    near = jnp.concatenate([piece.reshape(lines * gsz, chan) for _, _, piece in pieces], axis=1)
    taps = jnp.concatenate(
        [
            jnp.concatenate([w_conv_ref[9 * d + 3 * e + f] for f in range(3)], axis=1)
            for d, e, _ in pieces
        ],
        axis=0,
    )
    sums = jnp.dot(near, taps, preferred_element_type=jnp.float32)
    return shifted(sums.reshape(lines, gsz, 3 * chan), chan)


def moved_lines(lines, e):
    blank = jnp.zeros((1,) + lines.shape[1:], lines.dtype)
    if e == 0:
        return jnp.concatenate([blank, lines[:-1]], axis=0)
    if e == 2:
        return jnp.concatenate([lines[1:], blank], axis=0)
    return lines


def own_kernel(first, cells_ref, w_conv_ref, out_ref):
    gsx = cells_ref.shape[0]
    for plane in range(out_ref.shape[0]):
        x = first + plane
        pieces = [
            (d, e, moved_lines(cells_ref[x + d - 1], e))
            for d in range(3)
            if 0 <= x + d - 1 < gsx
            for e in range(3)
        ]
        total = cells_ref[x].astype(jnp.float32) + conv_lines(pieces, w_conv_ref)
        out_ref[plane] = total.astype(jnp.bfloat16)


def up_kernel(
    owner_ref, near_ref, far_ref, x_low_ref, x_high_ref, y_low_ref, y_high_ref, w_conv_ref, w_up_ref,
    feat_ref, blank_ref, out_ref, held, total, twice, index, in_sem, out_sem,
):
    gsx, gsy, gsz, chan = total.shape
    cols_x, cols_y, zcap = feat_ref.shape[:3]
    slots = cols_x * cols_y * zcap

    def at(slot):
        return place(slot, cols_y, zcap)

    def load(spot):
        return pltpu.make_async_copy(feat_ref.at[at(index[spot])], held.at[spot], in_sem.at[spot])

    def store(spot):
        return pltpu.make_async_copy(held.at[spot], out_ref.at[at(index[spot])], out_sem.at[spot])

    def scan(slot, count):
        alive = owner_ref[at(slot)] >= 0

        @pl.when(alive)
        def _():
            index[count] = slot
            load(count).start()

        return count + alive.astype(jnp.int32)

    count = lax.fori_loop(0, slots, scan, 0)
    groups = (count + GROUP - 1) // GROUP

    half = gsx // 2
    total[:half] = near_ref[...].astype(jnp.float32)
    total[half:] = far_ref[...].astype(jnp.float32)
    for line, ref, e in ((0, y_low_ref, 0), (gsy - 1, y_high_ref, 2)):
        pieces = [(d, e, ref[d : d + gsx]) for d in range(3)]
        total[:, line] = total[:, line] + conv_lines(pieces, w_conv_ref)
    for plane, ref, d in ((0, x_low_ref, 0), (gsx - 1, x_high_ref, 2)):
        pieces = [(d, e, moved_lines(ref[...], e)) for e in range(3)]
        total[plane] = total[plane] + conv_lines(pieces, w_conv_ref)
    for x in range(gsx):
        for c in range(2):
            twice[x, :, pl.ds(c, gsz, stride=2)] = total[x]

    @pl.loop(0, groups)
    def _(group):
        for b in range(GROUP):
            @pl.when(group * GROUP + b < count)
            def _():
                load(group * GROUP + b).wait()

        cells = []
        for b in range(GROUP):
            x, y, z = at(index[jnp.minimum(group * GROUP + b, count - 1)])
            where = (pl.ds(4 * x, 4), pl.ds(4 * y, 4), pl.ds(pl.multiple_of(8 * z, 8), 8))
            cells.append(twice[where].reshape(128, chan))
        cells = jnp.concatenate(cells, axis=0)
        odd = lax.rem(lax.broadcasted_iota(jnp.int32, cells.shape, 0), 2) == 1
        split = jnp.concatenate(
            [jnp.where(odd, 0.0, cells), jnp.where(odd, cells, 0.0)], axis=1
        ).astype(jnp.bfloat16)
        weights = jnp.concatenate(
            [
                jnp.concatenate(
                    [w_up_ref[4 * a + 2 * b + c] for a in range(2) for b in range(2)], axis=1
                )
                for c in range(2)
            ],
            axis=0,
        )
        lifted = jnp.dot(split, weights, preferred_element_type=jnp.float32)
        for b in range(GROUP):
            top = lifted[128 * b : 128 * b + 128].reshape(16, 8, 4 * chan)
            spot = group * GROUP + b
            for a in range(2):
                pair = [top[:, :, (2 * a + e) * chan : (2 * a + e + 1) * chan] for e in range(2)]
                pair = jnp.concatenate(pair, axis=1).reshape(4, 64, chan)
                held[spot, :, a] = (held[spot, :, a].astype(jnp.float32) + pair).astype(jnp.bfloat16)
        for b in range(GROUP):
            @pl.when(group * GROUP + b < count)
            def _():
                store(group * GROUP + b).start()

    @pl.loop(0, count)
    def _(spot):
        store(spot).wait()


def exchange(low, high, axis):
    count = lax.axis_size(axis)
    up = [(i, i + 1) for i in range(count - 1)]
    return lax.ppermute(high, axis, up), lax.ppermute(low, axis, [(j, i) for i, j in up])


def local(features, owner, norm_gain, time_shift, w_in, w_out, w_down, w_conv, w_up):
    cols_x, cols_y, zcap, voxels, chan = features.shape
    slots = cols_x * cols_y * zcap
    gsx, gsy, gsz = cols_x * 4, cols_y * 4, zcap * 4
    layers, _, hid = w_in.shape
    vmem = pl.BlockSpec(memory_space=pltpu.VMEM)
    smem = pl.BlockSpec(memory_space=pltpu.SMEM)
    params = pltpu.CompilerParams(vmem_limit_bytes=VMEM_LIMIT)

    def cells(*shape):
        return jax.ShapeDtypeStruct(shape + (gsz, chan), jnp.bfloat16)

    brick = (4, 2, voxels // 8, chan)
    hbm = pl.BlockSpec(memory_space=pl.ANY)
    blank = jax.ShapeDtypeStruct((cols_x, cols_y, zcap) + brick, jnp.bfloat16)
    grid, x_low, x_high, y_low, y_high, blank = pl.pallas_call(
        down_kernel,
        out_shape=[cells(gsx, gsy), cells(gsy), cells(gsy), cells(gsx), cells(gsx), blank],
        in_specs=[smem, hbm, vmem, vmem, hbm, hbm, vmem],
        out_specs=[vmem] * 5 + [hbm],
        scratch_shapes=[
            pltpu.VMEM((2, GROUP, voxels, chan), jnp.bfloat16),
            pltpu.VMEM((GROUP, voxels, chan), jnp.float32),
            pltpu.VMEM((GROUP, voxels, chan), jnp.float32),
            pltpu.VMEM((layers, chan, hid), jnp.bfloat16),
            pltpu.VMEM((layers, hid, chan), jnp.bfloat16),
            pltpu.VMEM((gsx, gsy, gsz, chan), jnp.float32),
            pltpu.VMEM(brick, jnp.bfloat16),
            pltpu.SMEM((slots,), jnp.int32),
            pltpu.SemaphoreType.DMA((2, GROUP)),
            pltpu.SemaphoreType.DMA((2,)),
            pltpu.SemaphoreType.DMA((slots,)),
        ],
        compiler_params=params,
        name="voxel_ff_down",
    )(owner, features, norm_gain, time_shift, w_in, w_out, w_down.reshape(8, chan, chan))

    taps = w_conv.reshape(27, chan, chan)
    half = gsx // 2
    flops = 2 * 27 * half * gsy * gsz * chan * chan
    own = [
        pl.pallas_call(
            functools.partial(own_kernel, first),
            out_shape=cells(half, gsy),
            in_specs=[vmem, vmem],
            out_specs=vmem,
            compiler_params=params,
            cost_estimate=pl.CostEstimate(
                flops=4 * flops, bytes_accessed=4 * 1024 * 1024, transcendentals=0
            ),
            name="conv_own",
        )(grid, taps)
        for first in (0, half)
    ]
    x_low, x_high = exchange(x_low, x_high, "gx")
    y_low = jnp.concatenate([x_low[:1], y_low, x_high[:1]], axis=0)
    y_high = jnp.concatenate([x_low[-1:], y_high, x_high[-1:]], axis=0)
    y_low, y_high = exchange(y_low, y_high, "gy")

    result = pl.pallas_call(
        up_kernel,
        out_shape=jax.ShapeDtypeStruct(blank.shape, blank.dtype),
        in_specs=[smem] + [vmem] * 8 + [hbm, hbm],
        out_specs=hbm,
        input_output_aliases={10: 0},
        scratch_shapes=[
            pltpu.VMEM((MOST,) + brick, jnp.bfloat16),
            pltpu.VMEM((gsx, gsy, gsz, chan), jnp.float32),
            pltpu.VMEM((gsx, gsy, 2 * gsz, chan), jnp.float32),
            pltpu.SMEM((slots,), jnp.int32),
            pltpu.SemaphoreType.DMA((MOST,)),
            pltpu.SemaphoreType.DMA((MOST,)),
        ],
        compiler_params=params,
        name="rim_up",
    )(
        owner, *own, x_low, x_high, y_low, y_high, taps, w_up.reshape(8, chan, chan),
        features.reshape(blank.shape), blank,
    )
    return result.reshape(features.shape)


def solution(mesh):
    in_specs = (
        P("gx", "gy", None, None, None),
        P("gx", "gy", None),
        P(),
        P(),
        P(),
        P(),
        P(),
        P(),
        P(),
    )
    out_specs = P("gx", "gy", None, None, None)
    return jax.shard_map(local, mesh=mesh, in_specs=in_specs, out_specs=out_specs, check_vma=False)
```

time: 126 us -> 114 us (0.905)
  the two profiles are of different devices: /device:TPU:10 before, /device:TPU:19 now
where the time goes in v4:
time: 114 us; the launch traced here: 112 us
  Pallas kernels  100 us (88%)
  starting transfers between devices  10.7 us (9%)
    pallas_call x1, Pallas kernels, local(): pl.pallas_call(down_kernel, out_shape=[cells(gsx, gsy), cells(gsy), cells...  81.4 us
    pallas_call x2, Pallas kernels, local(): pl.pallas_call(functools.partial(own_kernel, first), out_shape=cells(half...  9.65 us
    pallas_call x1, Pallas kernels, local(): pl.pallas_call(up_kernel, out_shape=jax.ShapeDtypeStruct(blank.shape, bla...  9.11 us
    ppermute x2, starting transfers between devices, exchange(): lax.ppermute(low, axis, [(j, i) for i, j in up])  7.48 us
    ppermute x2, starting transfers between devices, exchange(): lax.ppermute(high, axis, up)  3.21 us
  transfers between devices with their start and end apart: 4, of which 1 were waited for; matrix products, arithmetic and copies ran while one was open for 0% of the time, Pallas kernels for 9%

profile of v4, /device:TPU:19, one launch (start us, length us, event | category | flops | bytes accessed | tf_op | source)
XLA Modules:
  0.0 112.4 jit_solution(1803113285069346878)
XLA Ops:
  0.0 81.4 %voxel_ff_down.1 = (bf16[8,8,64,128]{3,2,1,0:T(8,128)(2,1)}, bf16[8,64,128]{2,1,0:T(8,128)(2,1)}, bf16[8,64,128]{2,1,0:T(8,128)(2,1)}, bf16[8,64,128]{2,1,0:T(8,...) custom-call(s32[2,2,16]{2,1,0:T(2,128)} %owner_ref.3, ...), custom_call_target="tpu_custom_call" | custom-call | tf_op jit(solution)/shard_map/voxel_ff_down/pallas_call | solution.py:337
  81.4 1.3 %collective-permute-start = (bf16[8,64,128]{2,1,0:T(8,128)(2,1)}, bf16[8,64,128]{2,1,0:T(8,128)(2,1)S(1)}, u32[]{:S(2)}, u32[]{:S(2)}) collective-permute-start(bf16[8,64,128]{2,1,0:T(8,128)(2,1)} %get-tuple-element.12), channel_id=1, source_target_pairs={{0,8},{8,16},{16,24},{1,9},{9,17},{17,25},{2,10},{10,18},{18,26},{... | collective-permute-start | bytes 393224 | tf_op jit(solution)/shard_map/ppermute | solution.py:319
  82.7 3.2 %collective-permute-start.1 = (bf16[8,64,128]{2,1,0:T(8,128)(2,1)}, bf16[8,64,128]{2,1,0:T(8,128)(2,1)S(1)}, u32[]{:S(2)}, u32[]{:S(2)}) collective-permute-start(bf16[8,64,128]{2,1,0:T(8,128)(2,1)} %get-tuple-element.13), channel_id=1, source_target_pairs={{8,0},{16,8},{24,16},{9,1},{17,9},{25,17},{10,2},{18,10},{26,18},{... | collective-permute-start | bytes 393224 | tf_op jit(solution)/shard_map/ppermute | solution.py:319
  85.9 0.0 copy-start.5
  86.0 0.0 copy-start.4
  86.0 4.8 %conv_own.3.far_ref = bf16[4,8,64,128]{3,2,1,0:T(8,128)(2,1)} custom-call(bf16[8,8,64,128]{3,2,1,0:T(8,128)(2,1)} %get-tuple-element.11.cells_ref, bf16[27,128,128]{2,1,0:T(8,128)(2,1)} %bitcast.6), custom_call_target="tpu_custom_call" | custom-call | flops 7247757312 | bytes 4194304 | tf_op jit(solution)/shard_map/conv_own/pallas_call | solution.py:363
  90.8 0.0 collective-permute-done.x_low_ref
  90.8 0.0 copy-start
  90.8 0.0 collective-permute-done.1.x_high_ref
  90.8 0.0 copy-start.1
  90.9 0.0 copy-done.5
  90.9 1.9 %collective-permute-start.2 = (bf16[10,64,128]{2,1,0:T(8,128)(2,1)S(1)}, bf16[10,64,128]{2,1,0:T(8,128)(2,1)S(1)}, u32[]{:S(2)}, u32[]{:S(2)}) collective-permute-start(bf16[10,64,128]{2,1,0:T(8,128)(2,1)S(1)} %pad_maximum_fusion), channel_id=1, source_target_pairs={{0,1},{1,2},{2,3},{3,4},{4,5},{5,6},{6,7},{8,9},{9,10},{10,11},{11... | collective-permute-start | bytes 491528 | tf_op jit(solution)/shard_map/ppermute | solution.py:319
  92.8 0.0 copy-done.4
  92.9 4.3 %collective-permute-start.3 = (bf16[10,64,128]{2,1,0:T(8,128)(2,1)S(1)}, bf16[10,64,128]{2,1,0:T(8,128)(2,1)S(1)}, u32[]{:S(2)}, u32[]{:S(2)}) collective-permute-start(bf16[10,64,128]{2,1,0:T(8,128)(2,1)S(1)} %pad_maximum_fusion.1), channel_id=1, source_target_pairs={{1,0},{2,1},{3,2},{4,3},{5,4},{6,5},{7,6},{9,8},{10,9},{11,10},{12... | collective-permute-start | bytes 491528 | tf_op jit(solution)/shard_map/ppermute | solution.py:319
  97.1 4.8 %conv_own.2.near_ref = bf16[4,8,64,128]{3,2,1,0:T(8,128)(2,1)} custom-call(bf16[8,8,64,128]{3,2,1,0:T(8,128)(2,1)} %get-tuple-element.11.cells_ref, bf16[27,128,128]{2,1,0:T(8,128)(2,1)} %bitcast.7), custom_call_target="tpu_custom_call" | custom-call | flops 7247757312 | bytes 4194304 | tf_op jit(solution)/shard_map/conv_own/pallas_call | solution.py:363
  101.9 0.0 copy-done
  102.0 0.0 copy-done.1
  102.0 0.0 collective-permute-done.2.y_low_ref
  102.0 0.0 copy-start.2
  102.0 0.5 collective-permute-done.3.y_high_ref
  102.4 0.0 copy-start.3
  102.4 0.2 copy-done.2
  102.6 0.5 copy-done.3
  103.1 9.1 %rim_up.1 = bf16[2,2,16,4,2,64,128]{6,5,4,3,2,1,0:T(8,128)(2,1)} custom-call(s32[2,2,16]{2,1,0:T(2,128)} %owner_ref.3, bf16[4,8,64,128]{3,2,1,0:T(8,128)(2,1)} %conv_own.2.near_ref, bf16[4,8,64,128]{3,2,1,0:T(8,128)(2,1)} %conv_own.3.far_ref, bf16[8,64,128]{2,1,0:T(8,128)(2,1)} %copy-done, ...), custom_call_target="tpu_custom_call", output_to_operand_aliasing={{}: (10, {})} | custom-call | tf_op jit(solution)/shard_map/rim_up/pallas_call | solution.py:381
  (4 shorter events, 0.1 us)
Async XLA Ops:
  81.4 9.4 %collective-permute-start = (bf16[8,64,128]{2,1,0:T(8,128)(2,1)}, bf16[8,64,128]{2,1,0:T(8,128)(2,1)S(1)}, u32[]{:S(2)}, u32[]{:S(2)}) collective-permute-start(bf16[8,64,128]{2,1,0:T(8,128)(2,1)} %get-tuple-element.12), channel_id=1, source_target_pairs={{0,8},{8,16},{16,24},{1,9},{9,17},{17,25},{2,10},{10,18},{18,26},{... | collective-permute-start | bytes 393224 | tf_op jit(solution)/shard_map/ppermute | solution.py:319
  82.7 8.1 %collective-permute-start.1 = (bf16[8,64,128]{2,1,0:T(8,128)(2,1)}, bf16[8,64,128]{2,1,0:T(8,128)(2,1)S(1)}, u32[]{:S(2)}, u32[]{:S(2)}) collective-permute-start(bf16[8,64,128]{2,1,0:T(8,128)(2,1)} %get-tuple-element.13), channel_id=1, source_target_pairs={{8,0},{16,8},{24,16},{9,1},{17,9},{25,17},{10,2},{18,10},{26,18},{... | collective-permute-start | bytes 393224 | tf_op jit(solution)/shard_map/ppermute | solution.py:319
  85.9 4.9 %copy-start.5 = (bf16[8,64,128]{2,1,0:T(8,128)(2,1)S(1)}, bf16[8,64,128]{2,1,0:T(8,128)(2,1)}, u32[]{:S(2)}) copy-start(bf16[8,64,128]{2,1,0:T(8,128)(2,1)} %get-tuple-element.14) | copy-start | bytes 393220
  86.0 6.9 %copy-start.4 = (bf16[8,64,128]{2,1,0:T(8,128)(2,1)S(1)}, bf16[8,64,128]{2,1,0:T(8,128)(2,1)}, u32[]{:S(2)}) copy-start(bf16[8,64,128]{2,1,0:T(8,128)(2,1)} %get-tuple-element.15) | copy-start | bytes 393220
  90.8 11.1 %copy-start = (bf16[8,64,128]{2,1,0:T(8,128)(2,1)}, bf16[8,64,128]{2,1,0:T(8,128)(2,1)S(1)}, u32[]{:S(2)}) copy-start(bf16[8,64,128]{2,1,0:T(8,128)(2,1)S(1)} %collective-permute-done.x_low_ref) | copy-start | bytes 393220
  90.8 11.1 %copy-start.1 = (bf16[8,64,128]{2,1,0:T(8,128)(2,1)}, bf16[8,64,128]{2,1,0:T(8,128)(2,1)S(1)}, u32[]{:S(2)}) copy-start(bf16[8,64,128]{2,1,0:T(8,128)(2,1)S(1)} %collective-permute-done.1.x_high_ref) | copy-start | bytes 393220
  90.9 11.1 %collective-permute-start.2 = (bf16[10,64,128]{2,1,0:T(8,128)(2,1)S(1)}, bf16[10,64,128]{2,1,0:T(8,128)(2,1)S(1)}, u32[]{:S(2)}, u32[]{:S(2)}) collective-permute-start(bf16[10,64,128]{2,1,0:T(8,128)(2,1)S(1)} %pad_maximum_fusion), channel_id=1, source_target_pairs={{0,1},{1,2},{2,3},{3,4},{4,5},{5,6},{6,7},{8,9},{9,10},{10,11},{11... | collective-permute-start | bytes 491528 | tf_op jit(solution)/shard_map/ppermute | solution.py:319
  92.9 9.6 %collective-permute-start.3 = (bf16[10,64,128]{2,1,0:T(8,128)(2,1)S(1)}, bf16[10,64,128]{2,1,0:T(8,128)(2,1)S(1)}, u32[]{:S(2)}, u32[]{:S(2)}) collective-permute-start(bf16[10,64,128]{2,1,0:T(8,128)(2,1)S(1)} %pad_maximum_fusion.1), channel_id=1, source_target_pairs={{1,0},{2,1},{3,2},{4,3},{5,4},{6,5},{7,6},{9,8},{10,9},{11,10},{12... | collective-permute-start | bytes 491528 | tf_op jit(solution)/shard_map/ppermute | solution.py:319
  102.0 0.7 copy-start.2
  102.4 0.7 copy-start.3

commit v5 on v4

--- a/solution.py
+++ b/solution.py
@@ -7,9 +7,11 @@
 from jax.experimental.pallas import tpu as pltpu
 from jax.sharding import PartitionSpec as P
 
-GROUP = 4
+GROUP = 8
+LIFT = 4
 MOST = 32
-VMEM_LIMIT = 56 * 1024 * 1024
+BLANKS = 4
+MIB = 1024 * 1024
 
 
 def silu(value):
@@ -23,8 +25,8 @@
 
 def down_kernel(
     owner_ref, feat_ref, gain_ref, shift_ref, w_in_ref, w_out_ref, w_down_ref,
-    out_ref, x_low_ref, x_high_ref, y_low_ref, y_high_ref, blank_ref,
-    held, stream, made, w_in, w_out, volume, zeros, index, sem, w_sem, zero_sem,
+    out_ref, x_low_ref, x_high_ref, y_low_ref, y_high_ref, index, blank_ref,
+    held, stream, made, w_in, w_out, volume, zeros, sem, w_sem, zero_sem,
 ):
     cols_x, cols_y, zcap, voxels, chan = feat_ref.shape
     slots = cols_x * cols_y * zcap
@@ -35,24 +37,16 @@
     ]
     for load in loads:
         load.start()
-    zeros[...] = jnp.zeros_like(zeros)
 
     def at(slot):
         return place(slot, cols_y, zcap)
 
-    def blank(slot):
-        return pltpu.make_async_copy(zeros, blank_ref.at[at(slot)], zero_sem.at[slot])
-
     def scan(slot, count):
-        alive = owner_ref[at(slot)] >= 0
-
-        @pl.when(alive)
-        def _():
-            index[count] = slot
-
-        return count + alive.astype(jnp.int32)
-
-    count = lax.fori_loop(0, slots, scan, 0)
+        index[count] = slot
+        return count + (owner_ref[at(slot)] >= 0).astype(jnp.int32)
+
+    count = lax.fori_loop(0, slots, scan, 0, unroll=8)
+    index[slots] = count
     groups = (count + GROUP - 1) // GROUP
 
     def slot_of(group, b):
@@ -72,12 +66,20 @@
         for copy in copies(0):
             copy.start()
 
-    @pl.loop(0, slots)
-    def _(slot):
-        @pl.when(owner_ref[at(slot)] < 0)
-        def _():
-            blank(slot).start()
-
+    zeros[...] = jnp.zeros_like(zeros)
+    parts = zcap // BLANKS
+    blanks = [
+        pltpu.make_async_copy(
+            zeros,
+            blank_ref.at[
+                part // (parts * cols_y), part // parts % cols_y, pl.ds(part % parts * BLANKS, BLANKS)
+            ],
+            zero_sem.at[part],
+        )
+        for part in range(slots // BLANKS)
+    ]
+    for copy in blanks:
+        copy.start()
     volume[...] = jnp.zeros_like(volume)
     across = lax.broadcasted_iota(jnp.int32, (chan, chan), 1)
     below = lax.broadcasted_iota(jnp.int32, (chan, chan), 0)
@@ -174,11 +176,8 @@
     y_low_ref[...] = out_ref[:, 0]
     y_high_ref[...] = out_ref[:, out_ref.shape[1] - 1]
 
-    @pl.loop(0, slots)
-    def _(slot):
-        @pl.when(owner_ref[at(slot)] < 0)
-        def _():
-            blank(slot).wait()
+    for copy in blanks:
+        copy.wait()
 
 
 def shifted(sums, chan):
@@ -212,27 +211,31 @@
     return lines
 
 
-def own_kernel(first, cells_ref, w_conv_ref, out_ref):
+def own_kernel(wanted, cells_ref, *refs):
+    rims, (w_conv_ref, out_ref) = refs[:-2], refs[-2:]
     gsx = cells_ref.shape[0]
-    for plane in range(out_ref.shape[0]):
-        x = first + plane
-        pieces = [
-            (d, e, moved_lines(cells_ref[x + d - 1], e))
-            for d in range(3)
-            if 0 <= x + d - 1 < gsx
-            for e in range(3)
-        ]
+    for spot, x in enumerate(wanted):
+        planes = [(d, x + d - 1, cells_ref) for d in range(3)]
+        if rims:
+            low_ref, high_ref = rims
+            planes = [
+                (d, i, low_ref if i < 0 else high_ref if i == gsx else ref) for d, i, ref in planes
+            ]
+        pieces = []
+        for d, i, ref in planes:
+            lines = ref[i] if 0 <= i < gsx else ref[...]
+            pieces += [(d, e, moved_lines(lines, e)) for e in range(3)]
         total = cells_ref[x].astype(jnp.float32) + conv_lines(pieces, w_conv_ref)
-        out_ref[plane] = total.astype(jnp.bfloat16)
+        out_ref[spot] = total.astype(jnp.bfloat16)
 
 
 def up_kernel(
-    owner_ref, near_ref, far_ref, x_low_ref, x_high_ref, y_low_ref, y_high_ref, w_conv_ref, w_up_ref,
-    feat_ref, blank_ref, out_ref, held, total, twice, index, in_sem, out_sem,
+    index, inner_ref, outer_ref, y_low_ref, y_high_ref, w_conv_ref, w_up_ref,
+    feat_ref, blank_ref, out_ref, held, total, twice, in_sem, out_sem,
 ):
     gsx, gsy, gsz, chan = total.shape
     cols_x, cols_y, zcap = feat_ref.shape[:3]
-    slots = cols_x * cols_y * zcap
+    count = index[cols_x * cols_y * zcap]
 
     def at(slot):
         return place(slot, cols_y, zcap)
@@ -243,42 +246,33 @@
     def store(spot):
         return pltpu.make_async_copy(held.at[spot], out_ref.at[at(index[spot])], out_sem.at[spot])
 
-    def scan(slot, count):
-        alive = owner_ref[at(slot)] >= 0
-
-        @pl.when(alive)
-        def _():
-            index[count] = slot
-            load(count).start()
-
-        return count + alive.astype(jnp.int32)
-
-    count = lax.fori_loop(0, slots, scan, 0)
-    groups = (count + GROUP - 1) // GROUP
-
-    half = gsx // 2
-    total[:half] = near_ref[...].astype(jnp.float32)
-    total[half:] = far_ref[...].astype(jnp.float32)
+    @pl.loop(0, count)
+    def _(spot):
+        load(spot).start()
+
+    groups = (count + LIFT - 1) // LIFT
+
+    inner, outer = split_planes(gsx)
+    for wanted, ref in ((inner, inner_ref), (outer, outer_ref)):
+        for spot, x in enumerate(wanted):
+            total[x] = ref[spot].astype(jnp.float32)
     for line, ref, e in ((0, y_low_ref, 0), (gsy - 1, y_high_ref, 2)):
         pieces = [(d, e, ref[d : d + gsx]) for d in range(3)]
         total[:, line] = total[:, line] + conv_lines(pieces, w_conv_ref)
-    for plane, ref, d in ((0, x_low_ref, 0), (gsx - 1, x_high_ref, 2)):
-        pieces = [(d, e, moved_lines(ref[...], e)) for e in range(3)]
-        total[plane] = total[plane] + conv_lines(pieces, w_conv_ref)
     for x in range(gsx):
         for c in range(2):
             twice[x, :, pl.ds(c, gsz, stride=2)] = total[x]
 
     @pl.loop(0, groups)
     def _(group):
-        for b in range(GROUP):
-            @pl.when(group * GROUP + b < count)
+        for b in range(LIFT):
+            @pl.when(group * LIFT + b < count)
             def _():
-                load(group * GROUP + b).wait()
+                load(group * LIFT + b).wait()
 
         cells = []
-        for b in range(GROUP):
-            x, y, z = at(index[jnp.minimum(group * GROUP + b, count - 1)])
+        for b in range(LIFT):
+            x, y, z = at(index[jnp.minimum(group * LIFT + b, count - 1)])
             where = (pl.ds(4 * x, 4), pl.ds(4 * y, 4), pl.ds(pl.multiple_of(8 * z, 8), 8))
             cells.append(twice[where].reshape(128, chan))
         cells = jnp.concatenate(cells, axis=0)
@@ -296,21 +290,26 @@
             axis=0,
         )
         lifted = jnp.dot(split, weights, preferred_element_type=jnp.float32)
-        for b in range(GROUP):
+        for b in range(LIFT):
             top = lifted[128 * b : 128 * b + 128].reshape(16, 8, 4 * chan)
-            spot = group * GROUP + b
+            spot = group * LIFT + b
             for a in range(2):
                 pair = [top[:, :, (2 * a + e) * chan : (2 * a + e + 1) * chan] for e in range(2)]
                 pair = jnp.concatenate(pair, axis=1).reshape(4, 64, chan)
                 held[spot, :, a] = (held[spot, :, a].astype(jnp.float32) + pair).astype(jnp.bfloat16)
-        for b in range(GROUP):
-            @pl.when(group * GROUP + b < count)
+        for b in range(LIFT):
+            @pl.when(group * LIFT + b < count)
             def _():
-                store(group * GROUP + b).start()
+                store(group * LIFT + b).start()
 
     @pl.loop(0, count)
     def _(spot):
         store(spot).wait()
+
+
+def split_planes(gsx):
+    inner = range(gsx // 4, gsx - gsx // 4)
+    return inner, [x for x in range(gsx) if x not in inner]
 
 
 def exchange(low, high, axis):
@@ -326,19 +325,24 @@
     layers, _, hid = w_in.shape
     vmem = pl.BlockSpec(memory_space=pltpu.VMEM)
     smem = pl.BlockSpec(memory_space=pltpu.SMEM)
-    params = pltpu.CompilerParams(vmem_limit_bytes=VMEM_LIMIT)
+    hbm = pl.BlockSpec(memory_space=pl.ANY)
+
+    def limit(mib):
+        return pltpu.CompilerParams(vmem_limit_bytes=mib * MIB)
 
     def cells(*shape):
         return jax.ShapeDtypeStruct(shape + (gsz, chan), jnp.bfloat16)
 
     brick = (4, 2, voxels // 8, chan)
-    hbm = pl.BlockSpec(memory_space=pl.ANY)
     blank = jax.ShapeDtypeStruct((cols_x, cols_y, zcap) + brick, jnp.bfloat16)
-    grid, x_low, x_high, y_low, y_high, blank = pl.pallas_call(
+    grid, x_low, x_high, y_low, y_high, index, blank = pl.pallas_call(
         down_kernel,
-        out_shape=[cells(gsx, gsy), cells(gsy), cells(gsy), cells(gsx), cells(gsx), blank],
+        out_shape=[
+            cells(gsx, gsy), cells(gsy), cells(gsy), cells(gsx), cells(gsx),
+            jax.ShapeDtypeStruct((slots + 1,), jnp.int32), blank,
+        ],
         in_specs=[smem, hbm, vmem, vmem, hbm, hbm, vmem],
-        out_specs=[vmem] * 5 + [hbm],
+        out_specs=[vmem] * 5 + [smem, hbm],
         scratch_shapes=[
             pltpu.VMEM((2, GROUP, voxels, chan), jnp.bfloat16),
             pltpu.VMEM((GROUP, voxels, chan), jnp.float32),
@@ -346,34 +350,35 @@
             pltpu.VMEM((layers, chan, hid), jnp.bfloat16),
             pltpu.VMEM((layers, hid, chan), jnp.bfloat16),
             pltpu.VMEM((gsx, gsy, gsz, chan), jnp.float32),
-            pltpu.VMEM(brick, jnp.bfloat16),
-            pltpu.SMEM((slots,), jnp.int32),
+            pltpu.VMEM((BLANKS,) + brick, jnp.bfloat16),
             pltpu.SemaphoreType.DMA((2, GROUP)),
             pltpu.SemaphoreType.DMA((2,)),
-            pltpu.SemaphoreType.DMA((slots,)),
+            pltpu.SemaphoreType.DMA((slots // BLANKS,)),
         ],
-        compiler_params=params,
+        compiler_params=limit(52),
         name="voxel_ff_down",
     )(owner, features, norm_gain, time_shift, w_in, w_out, w_down.reshape(8, chan, chan))
 
     taps = w_conv.reshape(27, chan, chan)
-    half = gsx // 2
-    flops = 2 * 27 * half * gsy * gsz * chan * chan
-    own = [
-        pl.pallas_call(
-            functools.partial(own_kernel, first),
-            out_shape=cells(half, gsy),
-            in_specs=[vmem, vmem],
+    flops = 2 * 27 * gsx // 2 * gsy * gsz * chan * chan
+
+    def own(wanted, *operands):
+        return pl.pallas_call(
+            functools.partial(own_kernel, wanted),
+            out_shape=cells(len(wanted), gsy),
+            in_specs=[vmem] * len(operands),
             out_specs=vmem,
-            compiler_params=params,
+            compiler_params=limit(20),
             cost_estimate=pl.CostEstimate(
-                flops=4 * flops, bytes_accessed=4 * 1024 * 1024, transcendentals=0
+                flops=4 * flops, bytes_accessed=4 * MIB, transcendentals=0
             ),
             name="conv_own",
-        )(grid, taps)
-        for first in (0, half)
-    ]
+        )(*operands)
+
+    inner, outer = split_planes(gsx)
+    inner = own(inner, grid, taps)
     x_low, x_high = exchange(x_low, x_high, "gx")
+    outer = own(outer, grid, x_low, x_high, taps)
     y_low = jnp.concatenate([x_low[:1], y_low, x_high[:1]], axis=0)
     y_high = jnp.concatenate([x_low[-1:], y_high, x_high[-1:]], axis=0)
     y_low, y_high = exchange(y_low, y_high, "gy")
@@ -381,21 +386,20 @@
     result = pl.pallas_call(
         up_kernel,
         out_shape=jax.ShapeDtypeStruct(blank.shape, blank.dtype),
-        in_specs=[smem] + [vmem] * 8 + [hbm, hbm],
+        in_specs=[smem] + [vmem] * 6 + [hbm, hbm],
         out_specs=hbm,
-        input_output_aliases={10: 0},
+        input_output_aliases={8: 0},
         scratch_shapes=[
             pltpu.VMEM((MOST,) + brick, jnp.bfloat16),
             pltpu.VMEM((gsx, gsy, gsz, chan), jnp.float32),
             pltpu.VMEM((gsx, gsy, 2 * gsz, chan), jnp.float32),
-            pltpu.SMEM((slots,), jnp.int32),
             pltpu.SemaphoreType.DMA((MOST,)),
             pltpu.SemaphoreType.DMA((MOST,)),
         ],
-        compiler_params=params,
+        compiler_params=limit(32),
         name="rim_up",
     )(
-        owner, *own, x_low, x_high, y_low, y_high, taps, w_up.reshape(8, chan, chan),
+        index, inner, outer, y_low, y_high, taps, w_up.reshape(8, chan, chan),
         features.reshape(blank.shape), blank,
     )
     return result.reshape(features.shape)

time: 114 us -> 113 us (level)
  the two profiles are of different devices: /device:TPU:19 before, /device:TPU:10 now
where the time goes in v5:
time: 113 us; the launch traced here: 112 us
  Pallas kernels  94.6 us (84%)
  starting transfers between devices  12.6 us (11%)
  local copies, waits for them, and re-layouts  3.15 us (3%)
  waiting for transfers between devices  1.74 us (2%)
    pallas_call x1, Pallas kernels, local(): pl.pallas_call(down_kernel, out_shape=[cells(gsx, gsy), cells(gsy), cells...  77.7 us
    pallas_call x1, Pallas kernels, local(): pl.pallas_call(up_kernel, out_shape=jax.ShapeDtypeStruct(blank.shape, bla...  11.3 us
    ppermute x2, starting transfers between devices, exchange(): lax.ppermute(low, axis, [(j, i) for i, j in up])  7.22 us
    pallas_call x2, Pallas kernels, own(): pl.pallas_call(functools.partial(own_kernel, wanted), out_shape=cells(len...  5.56 us
    ppermute x2, starting transfers between devices, exchange(): lax.ppermute(high, axis, up)  5.35 us
    unnamed x16, local copies, waits for them, and re-layouts  3.14 us
  transfers between devices with their start and end apart: 4, of which 1 were waited for; matrix products, arithmetic and copies ran while one was open for 0% of the time, Pallas kernels for 5%

profile of v5, /device:TPU:10, one launch (start us, length us, event | category | flops | bytes accessed | tf_op | source)
XLA Modules:
  0.0 112.4 jit_solution(5524127967095095185)
XLA Ops:
  0.0 0.0 copy-start
  0.0 0.0 copy-start.2
  0.0 1.0 copy-done.2
  1.0 0.0 copy-start.3
  1.0 0.7 copy-done.3
  1.8 0.0 copy-start.4
  1.8 0.7 copy-done.4
  2.4 0.0 copy-start.5
  2.4 0.7 copy-done.5
  3.1 77.7 %voxel_ff_down.1 = (bf16[8,8,64,128]{3,2,1,0:T(8,128)(2,1)S(1)}, bf16[8,64,128]{2,1,0:T(8,128)(2,1)S(1)}, bf16[8,64,128]{2,1,0:T(8,128)(2,1)S(1)}, bf16[8,64,128...) custom-call(s32[2,2,16]{2,1,0:T(2,128)S(1)} %copy-done.5, ...), custom_call_target="tpu_custom_call" | custom-call | tf_op jit(solution)/shard_map/voxel_ff_down/pallas_call | solution.py:338
  80.8 1.9 %collective-permute-start = (bf16[8,64,128]{2,1,0:T(8,128)(2,1)S(1)}, bf16[8,64,128]{2,1,0:T(8,128)(2,1)S(1)}, u32[]{:S(2)}, u32[]{:S(2)}) collective-permute-start(bf16[8,64,128]{2,1,0:T(8,128)(2,1)S(1)} %get-tuple-element.14), channel_id=1, source_target_pairs={{0,8},{8,16},{16,24},{1,9},{9,17},{17,25},{2,10},{10,18},{18,26},{... | collective-permute-start | bytes 393224 | tf_op jit(solution)/shard_map/ppermute | solution.py:318
  82.7 3.6 %collective-permute-start.1 = (bf16[8,64,128]{2,1,0:T(8,128)(2,1)S(1)}, bf16[8,64,128]{2,1,0:T(8,128)(2,1)S(1)}, u32[]{:S(2)}, u32[]{:S(2)}) collective-permute-start(bf16[8,64,128]{2,1,0:T(8,128)(2,1)S(1)} %get-tuple-element.15), channel_id=1, source_target_pairs={{8,0},{16,8},{24,16},{9,1},{17,9},{25,17},{10,2},{18,10},{26,18},{... | collective-permute-start | bytes 393224 | tf_op jit(solution)/shard_map/ppermute | solution.py:318
  86.4 0.0 copy-done
  86.4 2.8 %conv_own.2.inner_ref = bf16[4,8,64,128]{3,2,1,0:T(8,128)(2,1)S(1)} custom-call(bf16[8,8,64,128]{3,2,1,0:T(8,128)(2,1)S(1)} %get-tuple-element.13.cells_ref, bf16[27,128,128]{2,1,0:T(8,128)(2,1)S(1)} %bitcast.8), custom_call_target="tpu_custom_call" | custom-call | flops 7247757312 | bytes 4194304 | tf_op jit(solution)/shard_map/conv_own/pallas_call | solution.py:366
  89.2 0.0 collective-permute-done.refs_0_
  89.2 0.0 collective-permute-done.1.refs_1_
  89.3 3.4 %collective-permute-start.2 = (bf16[10,64,128]{2,1,0:T(8,128)(2,1)S(1)}, bf16[10,64,128]{2,1,0:T(8,128)(2,1)S(1)}, u32[]{:S(2)}, u32[]{:S(2)}) collective-permute-start(bf16[10,64,128]{2,1,0:T(8,128)(2,1)S(1)} %pad_maximum_fusion), channel_id=1, source_target_pairs={{0,1},{1,2},{2,3},{3,4},{4,5},{5,6},{6,7},{8,9},{9,10},{10,11},{11... | collective-permute-start | bytes 491528 | tf_op jit(solution)/shard_map/ppermute | solution.py:318
  92.7 0.0 slice-start
  92.7 0.0 slice-start.1
  92.8 0.0 copy-start.1
  92.8 3.6 %collective-permute-start.3 = (bf16[10,64,128]{2,1,0:T(8,128)(2,1)S(1)}, bf16[10,64,128]{2,1,0:T(8,128)(2,1)S(1)}, u32[]{:S(2)}, u32[]{:S(2)}) collective-permute-start(bf16[10,64,128]{2,1,0:T(8,128)(2,1)S(1)} %pad_maximum_fusion.1), channel_id=1, source_target_pairs={{1,0},{2,1},{3,2},{4,3},{5,4},{6,5},{7,6},{9,8},{10,9},{11,10},{12... | collective-permute-start | bytes 491528 | tf_op jit(solution)/shard_map/ppermute | solution.py:318
  96.4 2.8 %conv_own.3.outer_ref = bf16[4,8,64,128]{3,2,1,0:T(8,128)(2,1)S(1)} custom-call(bf16[8,8,64,128]{3,2,1,0:T(8,128)(2,1)S(1)} %get-tuple-element.13.cells_ref, bf16[8,64,128]{2,1,0:T(8,128)(2,1)S(1)} %collective-permute-done.refs_0_, bf16[8,64,128]{2,1,0:T(8,128)(2,1)S(1)} %collective-permute-done.1.refs_1_, bf16[27,128,128]{2,1,0:T(8,128)(2,1)S(1)} %bitcast.9), custom_call_target="tpu_custom_call" | custom-call | flops 7247757312 | bytes 4194304 | tf_op jit(solution)/shard_map/conv_own/pallas_call | solution.py:366
  99.1 0.0 collective-permute-done.2.y_low_ref
  99.2 1.7 %collective-permute-done.3.y_high_ref = bf16[10,64,128]{2,1,0:T(8,128)(2,1)S(1)} collective-permute-done((bf16[10,64,128]{2,1,0:T(8,128)(2,1)S(1)}, bf16[10,64,128]{2,1,0:T(8,128)(2,1)S(1)}, u32[]{:S(2)}, u32[]{:S(2)}) %collective-permute-start.3) | collective-permute-done | bytes 163872 | tf_op jit(solution)/shard_map/ppermute | solution.py:318
  100.9 0.0 slice-done
  100.9 0.0 slice-done.1
  100.9 0.0 copy-done.1
  100.9 11.3 %rim_up.1 = bf16[2,2,16,4,2,64,128]{6,5,4,3,2,1,0:T(8,128)(2,1)} custom-call(s32[65]{0:T(128)S(1)} %get-tuple-element.12.index, bf16[4,8,64,128]{3,2,1,0:T(8,128)(2,1)S(1)} %conv_own.2.inner_ref, bf16[4,8,64,128]{3,2,1,0:T(8,128)(2,1)S(1)} %conv_own.3.outer_ref, ...), custom_call_target="tpu_custom_call", output_to_operand_aliasing={{}: (8, {})} | custom-call | tf_op jit(solution)/shard_map/rim_up/pallas_call | solution.py:386
  (5 shorter events, 0.1 us)
Async XLA Ops:
  0.0 86.4 %copy-start = (bf16[3,3,3,128,128]{4,3,2,1,0:T(8,128)(2,1)S(1)}, bf16[3,3,3,128,128]{4,3,2,1,0:T(8,128)(2,1)}, u32[]{:S(2)}) copy-start(bf16[3,3,3,128,128]{4,3,2,1,0:T(8,128)(2,1)} %param.16) | copy-start | bytes 2654212
  0.0 1.0 copy-start.2
  1.0 0.7 copy-start.3
  1.8 0.7 copy-start.4
  2.4 0.7 copy-start.5
  80.8 8.4 %collective-permute-start = (bf16[8,64,128]{2,1,0:T(8,128)(2,1)S(1)}, bf16[8,64,128]{2,1,0:T(8,128)(2,1)S(1)}, u32[]{:S(2)}, u32[]{:S(2)}) collective-permute-start(bf16[8,64,128]{2,1,0:T(8,128)(2,1)S(1)} %get-tuple-element.14), channel_id=1, source_target_pairs={{0,8},{8,16},{16,24},{1,9},{9,17},{17,25},{2,10},{10,18},{18,26},{... | collective-permute-start | bytes 393224 | tf_op jit(solution)/shard_map/ppermute | solution.py:318
  82.7 6.5 %collective-permute-start.1 = (bf16[8,64,128]{2,1,0:T(8,128)(2,1)S(1)}, bf16[8,64,128]{2,1,0:T(8,128)(2,1)S(1)}, u32[]{:S(2)}, u32[]{:S(2)}) collective-permute-start(bf16[8,64,128]{2,1,0:T(8,128)(2,1)S(1)} %get-tuple-element.15), channel_id=1, source_target_pairs={{8,0},{16,8},{24,16},{9,1},{17,9},{25,17},{10,2},{18,10},{26,18},{... | collective-permute-start | bytes 393224 | tf_op jit(solution)/shard_map/ppermute | solution.py:318
  89.3 9.9 %collective-permute-start.2 = (bf16[10,64,128]{2,1,0:T(8,128)(2,1)S(1)}, bf16[10,64,128]{2,1,0:T(8,128)(2,1)S(1)}, u32[]{:S(2)}, u32[]{:S(2)}) collective-permute-start(bf16[10,64,128]{2,1,0:T(8,128)(2,1)S(1)} %pad_maximum_fusion), channel_id=1, source_target_pairs={{0,1},{1,2},{2,3},{3,4},{4,5},{5,6},{6,7},{8,9},{9,10},{10,11},{11... | collective-permute-start | bytes 491528 | tf_op jit(solution)/shard_map/ppermute | solution.py:318
  92.7 8.2 %slice-start = ((s8[8388608]{0:T(1024)(128)(4,1)}), s8[4194304]{0:T(1024)(128)(4,1)S(1)}, s32[]{:S(2)}) async-start(s8[8388608]{0:T(1024)(128)(4,1)} %bitcast.5), calls=%async_computation | async-start | bytes 8388608
  92.7 8.1 %slice-start.1 = ((s8[8388608]{0:T(1024)(128)(4,1)}), s8[4194304]{0:T(1024)(128)(4,1)S(1)}, s32[]{:S(2)}) async-start(s8[8388608]{0:T(1024)(128)(4,1)} %bitcast.5), calls=%async_computation.1 | async-start | bytes 8388608
  92.8 8.1 %copy-start.1 = (bf16[2,2,2,128,128]{4,3,2,1,0:T(8,128)(2,1)S(1)}, bf16[2,2,2,128,128]{4,3,2,1,0:T(8,128)(2,1)}, u32[]{:S(2)}) copy-start(bf16[2,2,2,128,128]{4,3,2,1,0:T(8,128)(2,1)} %param.17) | copy-start | bytes 786436
  92.8 8.1 %collective-permute-start.3 = (bf16[10,64,128]{2,1,0:T(8,128)(2,1)S(1)}, bf16[10,64,128]{2,1,0:T(8,128)(2,1)S(1)}, u32[]{:S(2)}, u32[]{:S(2)}) collective-permute-start(bf16[10,64,128]{2,1,0:T(8,128)(2,1)S(1)} %pad_maximum_fusion.1), channel_id=1, source_target_pairs={{1,0},{2,1},{3,2},{4,3},{5,4},{6,5},{7,6},{9,8},{10,9},{11,10},{12... | collective-permute-start | bytes 491528 | tf_op jit(solution)/shard_map/ppermute | solution.py:318

commit v6 on v5

--- a/solution.py
+++ b/solution.py
@@ -24,19 +24,31 @@
 
 
 def down_kernel(
-    owner_ref, feat_ref, gain_ref, shift_ref, w_in_ref, w_out_ref, w_down_ref,
+    owner_hbm, feat_ref, gain_hbm, shift_hbm, w_in_hbm, w_out_hbm, w_down_hbm,
     out_ref, x_low_ref, x_high_ref, y_low_ref, y_high_ref, index, blank_ref,
-    held, stream, made, w_in, w_out, volume, zeros, sem, w_sem, zero_sem,
+    held, owner_ref, gain_ref, shift_ref, w_in, w_out, w_down_ref, stream, made, volume, zeros,
+    sem, arg_sem, zero_sem,
 ):
     cols_x, cols_y, zcap, voxels, chan = feat_ref.shape
     slots = cols_x * cols_y * zcap
     layers = w_in.shape[0]
+    pairs = (
+        (owner_hbm, owner_ref),
+        (gain_hbm, gain_ref),
+        (shift_hbm, shift_ref),
+        (w_in_hbm, w_in),
+        (w_out_hbm, w_out),
+        (w_down_hbm, w_down_ref),
+    )
     loads = [
-        pltpu.make_async_copy(w_in_ref, w_in, w_sem.at[0]),
-        pltpu.make_async_copy(w_out_ref, w_out, w_sem.at[1]),
+        pltpu.make_async_copy(source, target, arg_sem.at[i])
+        for i, (source, target) in enumerate(pairs)
     ]
     for load in loads:
         load.start()
+    volume[...] = jnp.zeros_like(volume)
+    zeros[...] = jnp.zeros_like(zeros)
+    loads[0].wait()
 
     def at(slot):
         return place(slot, cols_y, zcap)
@@ -53,10 +65,9 @@
         return index[jnp.minimum(group * GROUP + b, count - 1)]
 
     def copies(group):
-        side = lax.rem(group, 2)
         return [
             pltpu.make_async_copy(
-                feat_ref.at[at(slot_of(group, b))], held.at[side, b], sem.at[side, b]
+                feat_ref.at[at(slot_of(group, b))], held.at[group * GROUP + b], sem.at[group * GROUP + b]
             )
             for b in range(GROUP)
         ]
@@ -66,7 +77,6 @@
         for copy in copies(0):
             copy.start()
 
-    zeros[...] = jnp.zeros_like(zeros)
     parts = zcap // BLANKS
     blanks = [
         pltpu.make_async_copy(
@@ -80,15 +90,14 @@
     ]
     for copy in blanks:
         copy.start()
-    volume[...] = jnp.zeros_like(volume)
     across = lax.broadcasted_iota(jnp.int32, (chan, chan), 1)
     below = lax.broadcasted_iota(jnp.int32, (chan, chan), 0)
-    loads[0].wait()
+    for load in loads[1:]:
+        load.wait()
     for layer in range(layers):
         gain = jnp.where(across == below, gain_ref[layer : layer + 1], 0.0)
         gain = jnp.sum(gain, axis=1, keepdims=True) * (0.5 * chan**0.5)
         w_in[layer] = (w_in[layer].astype(jnp.float32) * gain).astype(jnp.bfloat16)
-    loads[1].wait()
 
     def down(group, b):
         slot = slot_of(group, b)
@@ -130,10 +139,9 @@
 
         for copy in copies(group):
             copy.wait()
-        side = lax.rem(group, 2)
 
         def value(layer, b):
-            return held[side, b].astype(jnp.float32) if layer == 0 else stream[b]
+            return held[group * GROUP + b].astype(jnp.float32) if layer == 0 else stream[b]
 
         def enter(layer, b):
             x = value(layer, b)
@@ -230,11 +238,11 @@
 
 
 def up_kernel(
-    index, inner_ref, outer_ref, y_low_ref, y_high_ref, w_conv_ref, w_up_ref,
-    feat_ref, blank_ref, out_ref, held, total, twice, in_sem, out_sem,
+    index, inner_ref, outer_ref, y_low_ref, y_high_ref, w_conv_ref, w_up_ref, feat_ref, blank_ref,
+    out_ref, held, total, twice, in_sem, out_sem,
 ):
     gsx, gsy, gsz, chan = total.shape
-    cols_x, cols_y, zcap = feat_ref.shape[:3]
+    cols_x, cols_y, zcap = out_ref.shape[:3]
     count = index[cols_x * cols_y * zcap]
 
     def at(slot):
@@ -325,7 +333,7 @@
     layers, _, hid = w_in.shape
     vmem = pl.BlockSpec(memory_space=pltpu.VMEM)
     smem = pl.BlockSpec(memory_space=pltpu.SMEM)
-    hbm = pl.BlockSpec(memory_space=pl.ANY)
+    hbm = pl.BlockSpec(memory_space=pltpu.HBM)
 
     def limit(mib):
         return pltpu.CompilerParams(vmem_limit_bytes=mib * MIB)
@@ -339,23 +347,28 @@
         down_kernel,
         out_shape=[
             cells(gsx, gsy), cells(gsy), cells(gsy), cells(gsx), cells(gsx),
-            jax.ShapeDtypeStruct((slots + 1,), jnp.int32), blank,
+            jax.ShapeDtypeStruct((slots + 1,), jnp.int32),
+            blank,
         ],
-        in_specs=[smem, hbm, vmem, vmem, hbm, hbm, vmem],
+        in_specs=[hbm] * 7,
         out_specs=[vmem] * 5 + [smem, hbm],
         scratch_shapes=[
-            pltpu.VMEM((2, GROUP, voxels, chan), jnp.bfloat16),
+            pltpu.VMEM((MOST, voxels, chan), jnp.bfloat16),
+            pltpu.SMEM(owner.shape, jnp.int32),
+            pltpu.VMEM(norm_gain.shape, jnp.float32),
+            pltpu.VMEM(time_shift.shape, jnp.float32),
+            pltpu.VMEM((layers, chan, hid), jnp.bfloat16),
+            pltpu.VMEM((layers, hid, chan), jnp.bfloat16),
+            pltpu.VMEM((8, chan, chan), jnp.bfloat16),
             pltpu.VMEM((GROUP, voxels, chan), jnp.float32),
             pltpu.VMEM((GROUP, voxels, chan), jnp.float32),
-            pltpu.VMEM((layers, chan, hid), jnp.bfloat16),
-            pltpu.VMEM((layers, hid, chan), jnp.bfloat16),
             pltpu.VMEM((gsx, gsy, gsz, chan), jnp.float32),
             pltpu.VMEM((BLANKS,) + brick, jnp.bfloat16),
-            pltpu.SemaphoreType.DMA((2, GROUP)),
-            pltpu.SemaphoreType.DMA((2,)),
+            pltpu.SemaphoreType.DMA((MOST,)),
+            pltpu.SemaphoreType.DMA((7,)),
             pltpu.SemaphoreType.DMA((slots // BLANKS,)),
         ],
-        compiler_params=limit(52),
+        compiler_params=limit(55),
         name="voxel_ff_down",
     )(owner, features, norm_gain, time_shift, w_in, w_out, w_down.reshape(8, chan, chan))
 
@@ -396,7 +409,7 @@
             pltpu.SemaphoreType.DMA((MOST,)),
             pltpu.SemaphoreType.DMA((MOST,)),
         ],
-        compiler_params=limit(32),
+        compiler_params=limit(48),
         name="rim_up",
     )(
         index, inner, outer, y_low, y_high, taps, w_up.reshape(8, chan, chan),

time: 113 us -> 106 us (0.938)
  the two profiles are of different devices: /device:TPU:10 before, /device:TPU:26 now
where the time goes in v6:
time: 106 us; the launch traced here: 105 us
  Pallas kernels  89.6 us (85%)
  starting transfers between devices  12.4 us (12%)
  waiting for transfers between devices  1.47 us (1%)
  local copies, waits for them, and re-layouts  1.25 us (1%)
    pallas_call x1, Pallas kernels, local(): pl.pallas_call(down_kernel, out_shape=[cells(gsx, gsy), cells(gsy), cells...  78.8 us
    ppermute x2, starting transfers between devices, exchange(): lax.ppermute(low, axis, [(j, i) for i, j in up])  8.59 us
    pallas_call x2, Pallas kernels, own(): pl.pallas_call(functools.partial(own_kernel, wanted), out_shape=cells(len...  5.5 us
    pallas_call x1, Pallas kernels, local(): pl.pallas_call(up_kernel, out_shape=jax.ShapeDtypeStruct(blank.shape, bla...  5.3 us
    ppermute x2, starting transfers between devices, exchange(): lax.ppermute(high, axis, up)  3.84 us
  transfers between devices with their start and end apart: 4, of which 1 were waited for; matrix products, arithmetic and copies ran while one was open for 0% of the time, Pallas kernels for 5%

profile of v6, /device:TPU:26, one launch (start us, length us, event | category | flops | bytes accessed | tf_op | source)
XLA Modules:
  0.0 105.1 jit_solution(1469861826701861676)
XLA Ops:
  0.0 0.0 copy-start
  0.0 78.8 %voxel_ff_down.1 = (bf16[8,8,64,128]{3,2,1,0:T(8,128)(2,1)}, bf16[8,64,128]{2,1,0:T(8,128)(2,1)}, bf16[8,64,128]{2,1,0:T(8,128)(2,1)}, bf16[8,64,128]{2,1,0:T(8,...) custom-call(s32[2,2,16]{2,1,0:T(2,128)} %owner_hbm.1, ...), custom_call_target="tpu_custom_call" | custom-call | tf_op jit(solution)/shard_map/voxel_ff_down/pallas_call | solution.py:346
  78.8 1.9 %collective-permute-start = (bf16[8,64,128]{2,1,0:T(8,128)(2,1)}, bf16[8,64,128]{2,1,0:T(8,128)(2,1)S(1)}, u32[]{:S(2)}, u32[]{:S(2)}) collective-permute-start(bf16[8,64,128]{2,1,0:T(8,128)(2,1)} %get-tuple-element.14), channel_id=1, source_target_pairs={{0,8},{8,16},{16,24},{1,9},{9,17},{17,25},{2,10},{10,18},{18,26},{... | collective-permute-start | bytes 393224 | tf_op jit(solution)/shard_map/ppermute | solution.py:326
  80.7 3.6 %collective-permute-start.1 = (bf16[8,64,128]{2,1,0:T(8,128)(2,1)}, bf16[8,64,128]{2,1,0:T(8,128)(2,1)S(1)}, u32[]{:S(2)}, u32[]{:S(2)}) collective-permute-start(bf16[8,64,128]{2,1,0:T(8,128)(2,1)} %get-tuple-element.15), channel_id=1, source_target_pairs={{8,0},{16,8},{24,16},{9,1},{17,9},{25,17},{10,2},{18,10},{26,18},{... | collective-permute-start | bytes 393224 | tf_op jit(solution)/shard_map/ppermute | solution.py:326
  84.4 0.0 copy-done
  84.4 0.0 copy-start.3
  84.4 1.2 %copy-done.3 = bf16[8,8,64,128]{3,2,1,0:T(8,128)(2,1)S(1)} copy-done((bf16[8,8,64,128]{3,2,1,0:T(8,128)(2,1)S(1)}, bf16[8,8,64,128]{3,2,1,0:T(8,128)(2,1)}, u32[]{:S(2)}) %copy-start.3) | copy-done | bytes 1048600
  85.6 0.0 copy-start.5
  85.6 0.0 copy-start.4
  85.6 2.8 %conv_own.2.inner_ref = bf16[4,8,64,128]{3,2,1,0:T(8,128)(2,1)S(1)} custom-call(bf16[8,8,64,128]{3,2,1,0:T(8,128)(2,1)S(1)} %copy-done.3, bf16[27,128,128]{2,1,0:T(8,128)(2,1)S(1)} %bitcast.5), custom_call_target="tpu_custom_call" | custom-call | flops 7247757312 | bytes 4194304 | tf_op jit(solution)/shard_map/conv_own/pallas_call | solution.py:379
  88.4 0.0 collective-permute-done.refs_0_
  88.4 0.0 collective-permute-done.1.refs_1_
  88.4 0.0 copy-done.5
  88.5 1.9 %collective-permute-start.2 = (bf16[10,64,128]{2,1,0:T(8,128)(2,1)S(1)}, bf16[10,64,128]{2,1,0:T(8,128)(2,1)S(1)}, u32[]{:S(2)}, u32[]{:S(2)}) collective-permute-start(bf16[10,64,128]{2,1,0:T(8,128)(2,1)S(1)} %pad_maximum_fusion), channel_id=1, source_target_pairs={{0,1},{1,2},{2,3},{3,4},{4,5},{5,6},{6,7},{8,9},{9,10},{10,11},{11... | collective-permute-start | bytes 491528 | tf_op jit(solution)/shard_map/ppermute | solution.py:326
  90.4 0.0 copy-done.4
  90.4 0.0 copy-start.1
  90.4 0.0 copy-start.2
  90.4 5.0 %collective-permute-start.3 = (bf16[10,64,128]{2,1,0:T(8,128)(2,1)S(1)}, bf16[10,64,128]{2,1,0:T(8,128)(2,1)S(1)}, u32[]{:S(2)}, u32[]{:S(2)}) collective-permute-start(bf16[10,64,128]{2,1,0:T(8,128)(2,1)S(1)} %pad_maximum_fusion.1), channel_id=1, source_target_pairs={{1,0},{2,1},{3,2},{4,3},{5,4},{6,5},{7,6},{9,8},{10,9},{11,10},{12... | collective-permute-start | bytes 491528 | tf_op jit(solution)/shard_map/ppermute | solution.py:326
  95.4 2.8 %conv_own.3.outer_ref = bf16[4,8,64,128]{3,2,1,0:T(8,128)(2,1)S(1)} custom-call(bf16[8,8,64,128]{3,2,1,0:T(8,128)(2,1)S(1)} %copy-done.3, bf16[8,64,128]{2,1,0:T(8,128)(2,1)S(1)} %collective-permute-done.refs_0_, bf16[8,64,128]{2,1,0:T(8,128)(2,1)S(1)} %collective-permute-done.1.refs_1_, bf16[27,128,128]{2,1,0:T(8,128)(2,1)S(1)} %bitcast.6), custom_call_target="tpu_custom_call" | custom-call | flops 7247757312 | bytes 4194304 | tf_op jit(solution)/shard_map/conv_own/pallas_call | solution.py:379
  98.2 0.0 collective-permute-done.2.y_low_ref
  98.2 1.5 %collective-permute-done.3.y_high_ref = bf16[10,64,128]{2,1,0:T(8,128)(2,1)S(1)} collective-permute-done((bf16[10,64,128]{2,1,0:T(8,128)(2,1)S(1)}, bf16[10,64,128]{2,1,0:T(8,128)(2,1)S(1)}, u32[]{:S(2)}, u32[]{:S(2)}) %collective-permute-start.3) | collective-permute-done | bytes 163872 | tf_op jit(solution)/shard_map/ppermute | solution.py:326
  99.6 0.0 copy-done.1
  99.6 0.0 copy-done.2
  99.6 5.3 %rim_up.1 = bf16[2,2,16,4,2,64,128]{6,5,4,3,2,1,0:T(8,128)(2,1)} custom-call(s32[65]{0:T(128)S(1)} %copy-done.2, bf16[4,8,64,128]{3,2,1,0:T(8,128)(2,1)S(1)} %conv_own.2.inner_ref, bf16[4,8,64,128]{3,2,1,0:T(8,128)(2,1)S(1)} %conv_own.3.outer_ref, bf16[10,64,128]{2,1,0:T(8,128)(2,1)S(1)} %collective-permute-done.2.y_low_ref, ...), custom_call_target="tpu_custom_call", output_to_operand_aliasing={{}: (8, {})} | custom-call | tf_op jit(solution)/shard_map/rim_up/pallas_call | solution.py:399
  (4 shorter events, 0.1 us)
Async XLA Ops:
  0.0 84.4 %copy-start = (bf16[3,3,3,128,128]{4,3,2,1,0:T(8,128)(2,1)S(1)}, bf16[3,3,3,128,128]{4,3,2,1,0:T(8,128)(2,1)}, u32[]{:S(2)}) copy-start(bf16[3,3,3,128,128]{4,3,2,1,0:T(8,128)(2,1)} %param.16) | copy-start | bytes 2654212
  78.8 9.6 %collective-permute-start = (bf16[8,64,128]{2,1,0:T(8,128)(2,1)}, bf16[8,64,128]{2,1,0:T(8,128)(2,1)S(1)}, u32[]{:S(2)}, u32[]{:S(2)}) collective-permute-start(bf16[8,64,128]{2,1,0:T(8,128)(2,1)} %get-tuple-element.14), channel_id=1, source_target_pairs={{0,8},{8,16},{16,24},{1,9},{9,17},{17,25},{2,10},{10,18},{18,26},{... | collective-permute-start | bytes 393224 | tf_op jit(solution)/shard_map/ppermute | solution.py:326
  80.7 7.7 %collective-permute-start.1 = (bf16[8,64,128]{2,1,0:T(8,128)(2,1)}, bf16[8,64,128]{2,1,0:T(8,128)(2,1)S(1)}, u32[]{:S(2)}, u32[]{:S(2)}) collective-permute-start(bf16[8,64,128]{2,1,0:T(8,128)(2,1)} %get-tuple-element.15), channel_id=1, source_target_pairs={{8,0},{16,8},{24,16},{9,1},{17,9},{25,17},{10,2},{18,10},{26,18},{... | collective-permute-start | bytes 393224 | tf_op jit(solution)/shard_map/ppermute | solution.py:326
  84.4 1.2 %copy-start.3 = (bf16[8,8,64,128]{3,2,1,0:T(8,128)(2,1)S(1)}, bf16[8,8,64,128]{3,2,1,0:T(8,128)(2,1)}, u32[]{:S(2)}) copy-start(bf16[8,8,64,128]{3,2,1,0:T(8,128)(2,1)} %get-tuple-element.13.cells_ref) | copy-start | bytes 3145732
  85.6 2.8 %copy-start.5 = (bf16[8,64,128]{2,1,0:T(8,128)(2,1)S(1)}, bf16[8,64,128]{2,1,0:T(8,128)(2,1)}, u32[]{:S(2)}) copy-start(bf16[8,64,128]{2,1,0:T(8,128)(2,1)} %get-tuple-element.16) | copy-start | bytes 393220
  85.6 4.8 %copy-start.4 = (bf16[8,64,128]{2,1,0:T(8,128)(2,1)S(1)}, bf16[8,64,128]{2,1,0:T(8,128)(2,1)}, u32[]{:S(2)}) copy-start(bf16[8,64,128]{2,1,0:T(8,128)(2,1)} %get-tuple-element.17) | copy-start | bytes 393220
  88.5 9.7 %collective-permute-start.2 = (bf16[10,64,128]{2,1,0:T(8,128)(2,1)S(1)}, bf16[10,64,128]{2,1,0:T(8,128)(2,1)S(1)}, u32[]{:S(2)}, u32[]{:S(2)}) collective-permute-start(bf16[10,64,128]{2,1,0:T(8,128)(2,1)S(1)} %pad_maximum_fusion), channel_id=1, source_target_pairs={{0,1},{1,2},{2,3},{3,4},{4,5},{5,6},{6,7},{8,9},{9,10},{10,11},{11... | collective-permute-start | bytes 491528 | tf_op jit(solution)/shard_map/ppermute | solution.py:326
  90.4 9.2 %copy-start.1 = (bf16[2,2,2,128,128]{4,3,2,1,0:T(8,128)(2,1)S(1)}, bf16[2,2,2,128,128]{4,3,2,1,0:T(8,128)(2,1)}, u32[]{:S(2)}) copy-start(bf16[2,2,2,128,128]{4,3,2,1,0:T(8,128)(2,1)} %param.17) | copy-start | bytes 786436
  90.4 9.2 %copy-start.2 = (s32[65]{0:T(128)S(1)}, s32[65]{0:T(128)}, u32[]{:S(2)}) copy-start(s32[65]{0:T(128)} %get-tuple-element.12.index) | copy-start | bytes 784
  90.4 9.2 %collective-permute-start.3 = (bf16[10,64,128]{2,1,0:T(8,128)(2,1)S(1)}, bf16[10,64,128]{2,1,0:T(8,128)(2,1)S(1)}, u32[]{:S(2)}, u32[]{:S(2)}) collective-permute-start(bf16[10,64,128]{2,1,0:T(8,128)(2,1)S(1)} %pad_maximum_fusion.1), channel_id=1, source_target_pairs={{1,0},{2,1},{3,2},{4,3},{5,4},{6,5},{7,6},{9,8},{10,9},{11,10},{12... | collective-permute-start | bytes 491528 | tf_op jit(solution)/shard_map/ppermute | solution.py:326

commit v7 on v6

--- a/solution.py
+++ b/solution.py
@@ -26,18 +26,19 @@
 def down_kernel(
     owner_hbm, feat_ref, gain_hbm, shift_hbm, w_in_hbm, w_out_hbm, w_down_hbm,
     out_ref, x_low_ref, x_high_ref, y_low_ref, y_high_ref, index, blank_ref,
-    held, owner_ref, gain_ref, shift_ref, w_in, w_out, w_down_ref, stream, made, volume, zeros,
+    held, owner_ref, gain_ref, shift_ref, w_in_ref, w_out_ref, w_down_ref, w_in, w_out, shifts,
+    stream, made, volume, zeros,
     sem, arg_sem, zero_sem,
 ):
     cols_x, cols_y, zcap, voxels, chan = feat_ref.shape
     slots = cols_x * cols_y * zcap
-    layers = w_in.shape[0]
+    layers = w_in_ref.shape[0]
     pairs = (
         (owner_hbm, owner_ref),
         (gain_hbm, gain_ref),
         (shift_hbm, shift_ref),
-        (w_in_hbm, w_in),
-        (w_out_hbm, w_out),
+        (w_in_hbm, w_in_ref),
+        (w_out_hbm, w_out_ref),
         (w_down_hbm, w_down_ref),
     )
     loads = [
@@ -90,14 +91,14 @@
     ]
     for copy in blanks:
         copy.start()
-    across = lax.broadcasted_iota(jnp.int32, (chan, chan), 1)
-    below = lax.broadcasted_iota(jnp.int32, (chan, chan), 0)
     for load in loads[1:]:
         load.wait()
     for layer in range(layers):
-        gain = jnp.where(across == below, gain_ref[layer : layer + 1], 0.0)
-        gain = jnp.sum(gain, axis=1, keepdims=True) * (0.5 * chan**0.5)
-        w_in[layer] = (w_in[layer].astype(jnp.float32) * gain).astype(jnp.bfloat16)
+        gain = gain_ref[layer : layer + 1] * (0.5 * chan**0.5)
+        w_in[layer] = (w_in_ref[layer].astype(jnp.float32).T * gain).astype(jnp.bfloat16)
+        w_out[layer] = w_out_ref[layer].astype(jnp.float32).T.astype(jnp.bfloat16)
+        shift = jnp.broadcast_to(0.5 * shift_ref[layer : layer + 1], (chan, shift_ref.shape[1]))
+        shifts[layer] = shift.T.astype(jnp.bfloat16)
 
     def down(group, b):
         slot = slot_of(group, b)
@@ -141,25 +142,25 @@
             copy.wait()
 
         def value(layer, b):
-            return held[group * GROUP + b].astype(jnp.float32) if layer == 0 else stream[b]
+            return held[group * GROUP + b].astype(jnp.float32).T if layer == 0 else stream[b]
 
         def enter(layer, b):
             x = value(layer, b)
-            power = jnp.sum(x * x, axis=-1, keepdims=True)
+            power = jnp.sum(x * x, axis=0, keepdims=True)
             normed = (x * lax.rsqrt(power + chan * 1e-6)).astype(jnp.bfloat16)
-            raw = jnp.dot(normed, w_in[layer], preferred_element_type=jnp.float32)
-            shift = (0.5 * shift_ref[layer : layer + 1]).astype(jnp.bfloat16)
+            raw = jnp.dot(w_in[layer], normed, preferred_element_type=jnp.float32)
+            shift = jnp.concatenate([shifts[layer]] * (voxels // chan), axis=1)
             return raw.astype(jnp.bfloat16) + shift
 
         def leave(layer, b, half):
             hidden = half + half * jnp.tanh(half)
             result = value(layer, b) + jnp.dot(
-                hidden, w_out[layer], preferred_element_type=jnp.float32
+                w_out[layer], hidden, preferred_element_type=jnp.float32
             )
             if layer + 1 < layers:
                 stream[b] = result
             else:
-                made[b] = result
+                made[b] = result.T
 
         order = [(layer, b) for layer in range(layers) for b in range(GROUP)]
         half = enter(*order[0])
@@ -360,7 +361,10 @@
             pltpu.VMEM((layers, chan, hid), jnp.bfloat16),
             pltpu.VMEM((layers, hid, chan), jnp.bfloat16),
             pltpu.VMEM((8, chan, chan), jnp.bfloat16),
-            pltpu.VMEM((GROUP, voxels, chan), jnp.float32),
+            pltpu.VMEM((layers, hid, chan), jnp.bfloat16),
+            pltpu.VMEM((layers, chan, hid), jnp.bfloat16),
+            pltpu.VMEM((layers, hid, chan), jnp.bfloat16),
+            pltpu.VMEM((GROUP, chan, voxels), jnp.float32),
             pltpu.VMEM((GROUP, voxels, chan), jnp.float32),
             pltpu.VMEM((gsx, gsy, gsz, chan), jnp.float32),
             pltpu.VMEM((BLANKS,) + brick, jnp.bfloat16),

time: 106 us -> 102 us (0.962)
  the two profiles are of different devices: /device:TPU:26 before, /device:TPU:10 now
where the time goes in v7:
time: 102 us; the launch traced here: 101 us
  Pallas kernels  85.6 us (84%)
  starting transfers between devices  12.4 us (12%)
  waiting for transfers between devices  1.47 us (1%)
  local copies, waits for them, and re-layouts  1.25 us (1%)
    pallas_call x1, Pallas kernels, local(): pl.pallas_call(down_kernel, out_shape=[cells(gsx, gsy), cells(gsy), cells...  74.8 us
    ppermute x2, starting transfers between devices, exchange(): lax.ppermute(low, axis, [(j, i) for i, j in up])  8.59 us
    pallas_call x2, Pallas kernels, own(): pl.pallas_call(functools.partial(own_kernel, wanted), out_shape=cells(len...  5.5 us
    pallas_call x1, Pallas kernels, local(): pl.pallas_call(up_kernel, out_shape=jax.ShapeDtypeStruct(blank.shape, bla...  5.3 us
    ppermute x2, starting transfers between devices, exchange(): lax.ppermute(high, axis, up)  3.84 us
  transfers between devices with their start and end apart: 4, of which 1 were waited for; matrix products, arithmetic and copies ran while one was open for 0% of the time, Pallas kernels for 5%

profile of v7, /device:TPU:10, one launch (start us, length us, event | category | flops | bytes accessed | tf_op | source)
XLA Modules:
  0.0 101.1 jit_solution(9069738374444139380)
XLA Ops:
  0.0 0.0 copy-start
  0.0 74.8 %voxel_ff_down.1 = (bf16[8,8,64,128]{3,2,1,0:T(8,128)(2,1)}, bf16[8,64,128]{2,1,0:T(8,128)(2,1)}, bf16[8,64,128]{2,1,0:T(8,128)(2,1)}, bf16[8,64,128]{2,1,0:T(8,...) custom-call(s32[2,2,16]{2,1,0:T(2,128)} %owner_hbm.1, ...), custom_call_target="tpu_custom_call" | custom-call | tf_op jit(solution)/shard_map/voxel_ff_down/pallas_call | solution.py:347
  74.8 1.9 %collective-permute-start = (bf16[8,64,128]{2,1,0:T(8,128)(2,1)}, bf16[8,64,128]{2,1,0:T(8,128)(2,1)S(1)}, u32[]{:S(2)}, u32[]{:S(2)}) collective-permute-start(bf16[8,64,128]{2,1,0:T(8,128)(2,1)} %get-tuple-element.14), channel_id=1, source_target_pairs={{0,8},{8,16},{16,24},{1,9},{9,17},{17,25},{2,10},{10,18},{18,26},{... | collective-permute-start | bytes 393224 | tf_op jit(solution)/shard_map/ppermute | solution.py:327
  76.8 3.6 %collective-permute-start.1 = (bf16[8,64,128]{2,1,0:T(8,128)(2,1)}, bf16[8,64,128]{2,1,0:T(8,128)(2,1)S(1)}, u32[]{:S(2)}, u32[]{:S(2)}) collective-permute-start(bf16[8,64,128]{2,1,0:T(8,128)(2,1)} %get-tuple-element.15), channel_id=1, source_target_pairs={{8,0},{16,8},{24,16},{9,1},{17,9},{25,17},{10,2},{18,10},{26,18},{... | collective-permute-start | bytes 393224 | tf_op jit(solution)/shard_map/ppermute | solution.py:327
  80.4 0.0 copy-done
  80.4 0.0 copy-start.3
  80.4 1.2 %copy-done.3 = bf16[8,8,64,128]{3,2,1,0:T(8,128)(2,1)S(1)} copy-done((bf16[8,8,64,128]{3,2,1,0:T(8,128)(2,1)S(1)}, bf16[8,8,64,128]{3,2,1,0:T(8,128)(2,1)}, u32[]{:S(2)}) %copy-start.3) | copy-done | bytes 1048600
  81.6 0.0 copy-start.5
  81.6 0.0 copy-start.4
  81.6 2.7 %conv_own.2.inner_ref = bf16[4,8,64,128]{3,2,1,0:T(8,128)(2,1)S(1)} custom-call(bf16[8,8,64,128]{3,2,1,0:T(8,128)(2,1)S(1)} %copy-done.3, bf16[27,128,128]{2,1,0:T(8,128)(2,1)S(1)} %bitcast.5), custom_call_target="tpu_custom_call" | custom-call | flops 7247757312 | bytes 4194304 | tf_op jit(solution)/shard_map/conv_own/pallas_call | solution.py:383
  84.4 0.0 collective-permute-done.refs_0_
  84.4 0.0 collective-permute-done.1.refs_1_
  84.4 0.0 copy-done.5
  84.5 1.9 %collective-permute-start.2 = (bf16[10,64,128]{2,1,0:T(8,128)(2,1)S(1)}, bf16[10,64,128]{2,1,0:T(8,128)(2,1)S(1)}, u32[]{:S(2)}, u32[]{:S(2)}) collective-permute-start(bf16[10,64,128]{2,1,0:T(8,128)(2,1)S(1)} %pad_maximum_fusion), channel_id=1, source_target_pairs={{0,1},{1,2},{2,3},{3,4},{4,5},{5,6},{6,7},{8,9},{9,10},{10,11},{11... | collective-permute-start | bytes 491528 | tf_op jit(solution)/shard_map/ppermute | solution.py:327
  86.4 0.0 copy-done.4
  86.5 0.0 copy-start.1
  86.5 0.0 copy-start.2
  86.5 5.0 %collective-permute-start.3 = (bf16[10,64,128]{2,1,0:T(8,128)(2,1)S(1)}, bf16[10,64,128]{2,1,0:T(8,128)(2,1)S(1)}, u32[]{:S(2)}, u32[]{:S(2)}) collective-permute-start(bf16[10,64,128]{2,1,0:T(8,128)(2,1)S(1)} %pad_maximum_fusion.1), channel_id=1, source_target_pairs={{1,0},{2,1},{3,2},{4,3},{5,4},{6,5},{7,6},{9,8},{10,9},{11,10},{12... | collective-permute-start | bytes 491528 | tf_op jit(solution)/shard_map/ppermute | solution.py:327
  91.4 2.8 %conv_own.3.outer_ref = bf16[4,8,64,128]{3,2,1,0:T(8,128)(2,1)S(1)} custom-call(bf16[8,8,64,128]{3,2,1,0:T(8,128)(2,1)S(1)} %copy-done.3, bf16[8,64,128]{2,1,0:T(8,128)(2,1)S(1)} %collective-permute-done.refs_0_, bf16[8,64,128]{2,1,0:T(8,128)(2,1)S(1)} %collective-permute-done.1.refs_1_, bf16[27,128,128]{2,1,0:T(8,128)(2,1)S(1)} %bitcast.6), custom_call_target="tpu_custom_call" | custom-call | flops 7247757312 | bytes 4194304 | tf_op jit(solution)/shard_map/conv_own/pallas_call | solution.py:383
  94.2 0.0 collective-permute-done.2.y_low_ref
  94.2 1.5 %collective-permute-done.3.y_high_ref = bf16[10,64,128]{2,1,0:T(8,128)(2,1)S(1)} collective-permute-done((bf16[10,64,128]{2,1,0:T(8,128)(2,1)S(1)}, bf16[10,64,128]{2,1,0:T(8,128)(2,1)S(1)}, u32[]{:S(2)}, u32[]{:S(2)}) %collective-permute-start.3) | collective-permute-done | bytes 163872 | tf_op jit(solution)/shard_map/ppermute | solution.py:327
  95.7 0.0 copy-done.1
  95.7 0.0 copy-done.2
  95.7 5.3 %rim_up.1 = bf16[2,2,16,4,2,64,128]{6,5,4,3,2,1,0:T(8,128)(2,1)} custom-call(s32[65]{0:T(128)S(1)} %copy-done.2, bf16[4,8,64,128]{3,2,1,0:T(8,128)(2,1)S(1)} %conv_own.2.inner_ref, bf16[4,8,64,128]{3,2,1,0:T(8,128)(2,1)S(1)} %conv_own.3.outer_ref, bf16[10,64,128]{2,1,0:T(8,128)(2,1)S(1)} %collective-permute-done.2.y_low_ref, ...), custom_call_target="tpu_custom_call", output_to_operand_aliasing={{}: (8, {})} | custom-call | tf_op jit(solution)/shard_map/rim_up/pallas_call | solution.py:403
  (4 shorter events, 0.1 us)
Async XLA Ops:
  0.0 80.4 %copy-start = (bf16[3,3,3,128,128]{4,3,2,1,0:T(8,128)(2,1)S(1)}, bf16[3,3,3,128,128]{4,3,2,1,0:T(8,128)(2,1)}, u32[]{:S(2)}) copy-start(bf16[3,3,3,128,128]{4,3,2,1,0:T(8,128)(2,1)} %param.16) | copy-start | bytes 2654212
  74.8 9.6 %collective-permute-start = (bf16[8,64,128]{2,1,0:T(8,128)(2,1)}, bf16[8,64,128]{2,1,0:T(8,128)(2,1)S(1)}, u32[]{:S(2)}, u32[]{:S(2)}) collective-permute-start(bf16[8,64,128]{2,1,0:T(8,128)(2,1)} %get-tuple-element.14), channel_id=1, source_target_pairs={{0,8},{8,16},{16,24},{1,9},{9,17},{17,25},{2,10},{10,18},{18,26},{... | collective-permute-start | bytes 393224 | tf_op jit(solution)/shard_map/ppermute | solution.py:327
  76.8 7.7 %collective-permute-start.1 = (bf16[8,64,128]{2,1,0:T(8,128)(2,1)}, bf16[8,64,128]{2,1,0:T(8,128)(2,1)S(1)}, u32[]{:S(2)}, u32[]{:S(2)}) collective-permute-start(bf16[8,64,128]{2,1,0:T(8,128)(2,1)} %get-tuple-element.15), channel_id=1, source_target_pairs={{8,0},{16,8},{24,16},{9,1},{17,9},{25,17},{10,2},{18,10},{26,18},{... | collective-permute-start | bytes 393224 | tf_op jit(solution)/shard_map/ppermute | solution.py:327
  80.4 1.2 %copy-start.3 = (bf16[8,8,64,128]{3,2,1,0:T(8,128)(2,1)S(1)}, bf16[8,8,64,128]{3,2,1,0:T(8,128)(2,1)}, u32[]{:S(2)}) copy-start(bf16[8,8,64,128]{3,2,1,0:T(8,128)(2,1)} %get-tuple-element.13.cells_ref) | copy-start | bytes 3145732
  81.6 2.8 %copy-start.5 = (bf16[8,64,128]{2,1,0:T(8,128)(2,1)S(1)}, bf16[8,64,128]{2,1,0:T(8,128)(2,1)}, u32[]{:S(2)}) copy-start(bf16[8,64,128]{2,1,0:T(8,128)(2,1)} %get-tuple-element.16) | copy-start | bytes 393220
  81.6 4.8 %copy-start.4 = (bf16[8,64,128]{2,1,0:T(8,128)(2,1)S(1)}, bf16[8,64,128]{2,1,0:T(8,128)(2,1)}, u32[]{:S(2)}) copy-start(bf16[8,64,128]{2,1,0:T(8,128)(2,1)} %get-tuple-element.17) | copy-start | bytes 393220
  84.5 9.7 %collective-permute-start.2 = (bf16[10,64,128]{2,1,0:T(8,128)(2,1)S(1)}, bf16[10,64,128]{2,1,0:T(8,128)(2,1)S(1)}, u32[]{:S(2)}, u32[]{:S(2)}) collective-permute-start(bf16[10,64,128]{2,1,0:T(8,128)(2,1)S(1)} %pad_maximum_fusion), channel_id=1, source_target_pairs={{0,1},{1,2},{2,3},{3,4},{4,5},{5,6},{6,7},{8,9},{9,10},{10,11},{11... | collective-permute-start | bytes 491528 | tf_op jit(solution)/shard_map/ppermute | solution.py:327
  86.5 9.2 %copy-start.1 = (bf16[2,2,2,128,128]{4,3,2,1,0:T(8,128)(2,1)S(1)}, bf16[2,2,2,128,128]{4,3,2,1,0:T(8,128)(2,1)}, u32[]{:S(2)}) copy-start(bf16[2,2,2,128,128]{4,3,2,1,0:T(8,128)(2,1)} %param.17) | copy-start | bytes 786436
  86.5 9.2 %copy-start.2 = (s32[65]{0:T(128)S(1)}, s32[65]{0:T(128)}, u32[]{:S(2)}) copy-start(s32[65]{0:T(128)} %get-tuple-element.12.index) | copy-start | bytes 784
  86.5 9.2 %collective-permute-start.3 = (bf16[10,64,128]{2,1,0:T(8,128)(2,1)S(1)}, bf16[10,64,128]{2,1,0:T(8,128)(2,1)S(1)}, u32[]{:S(2)}, u32[]{:S(2)}) collective-permute-start(bf16[10,64,128]{2,1,0:T(8,128)(2,1)S(1)} %pad_maximum_fusion.1), channel_id=1, source_target_pairs={{1,0},{2,1},{3,2},{4,3},{5,4},{6,5},{7,6},{9,8},{10,9},{11,10},{12... | collective-permute-start | bytes 491528 | tf_op jit(solution)/shard_map/ppermute | solution.py:327

commit v8 on v7

--- a/solution.py
+++ b/solution.py
@@ -8,6 +8,8 @@
 from jax.sharding import PartitionSpec as P
 
 GROUP = 8
+WAIT = 2
+CHUNK = 256
 LIFT = 4
 MOST = 32
 BLANKS = 4
@@ -95,10 +97,10 @@
         load.wait()
     for layer in range(layers):
         gain = gain_ref[layer : layer + 1] * (0.5 * chan**0.5)
-        w_in[layer] = (w_in_ref[layer].astype(jnp.float32).T * gain).astype(jnp.bfloat16)
-        w_out[layer] = w_out_ref[layer].astype(jnp.float32).T.astype(jnp.bfloat16)
+        w_in[layer] = (w_in_ref[layer].T.astype(jnp.float32) * gain).astype(jnp.bfloat16)
+        w_out[layer] = w_out_ref[layer].T
         shift = jnp.broadcast_to(0.5 * shift_ref[layer : layer + 1], (chan, shift_ref.shape[1]))
-        shifts[layer] = shift.T.astype(jnp.bfloat16)
+        shifts[layer] = shift.astype(jnp.bfloat16).T
 
     def down(group, b):
         slot = slot_of(group, b)
@@ -141,42 +143,52 @@
         for copy in copies(group):
             copy.wait()
 
-        def value(layer, b):
-            return held[group * GROUP + b].astype(jnp.float32).T if layer == 0 else stream[b]
-
-        def enter(layer, b):
-            x = value(layer, b)
+        def value(layer, b, span):
+            if layer == 0:
+                return held[group * GROUP + b, span].astype(jnp.float32).T
+            return stream[b, :, span]
+
+        def enter(layer, b, span):
+            x = value(layer, b, span)
             power = jnp.sum(x * x, axis=0, keepdims=True)
             normed = (x * lax.rsqrt(power + chan * 1e-6)).astype(jnp.bfloat16)
             raw = jnp.dot(w_in[layer], normed, preferred_element_type=jnp.float32)
-            shift = jnp.concatenate([shifts[layer]] * (voxels // chan), axis=1)
+            shift = jnp.concatenate([shifts[layer]] * (CHUNK // chan), axis=1)
             return raw.astype(jnp.bfloat16) + shift
 
-        def leave(layer, b, half):
+        def leave(layer, b, span, half):
             hidden = half + half * jnp.tanh(half)
-            result = value(layer, b) + jnp.dot(
+            result = value(layer, b, span) + jnp.dot(
                 w_out[layer], hidden, preferred_element_type=jnp.float32
             )
             if layer + 1 < layers:
-                stream[b] = result
+                stream[b, :, span] = result
             else:
-                made[b] = result.T
-
-        order = [(layer, b) for layer in range(layers) for b in range(GROUP)]
+                made[b, span] = result.T
+
+        order = [
+            (layer, b, slice(v, v + CHUNK))
+            for layer in range(layers)
+            for b in range(GROUP)
+            for v in range(0, voxels, CHUNK)
+        ]
         half = enter(*order[0])
-        for spot, here in enumerate(order):
+        for spot, (layer, b, span) in enumerate(order):
             later = enter(*order[spot + 1]) if spot + 1 < len(order) else None
-            leave(*here, half)
-            if here[0] == 1:
-                down(jnp.maximum(group - 1, 0), here[1])
+            leave(layer, b, span, half)
             half = later
+            if span.stop == voxels:
+                if layer == 1 and b >= GROUP - WAIT:
+                    down(jnp.maximum(group - 1, 0), b)
+                if layer + 1 == layers and b < GROUP - WAIT:
+                    down(group, b)
         return carry
 
     lax.fori_loop(0, groups, work, 0)
 
     @pl.when(groups > 0)
     def _():
-        for b in range(GROUP):
+        for b in range(GROUP - WAIT, GROUP):
             down(groups - 1, b)
 
     out_ref[...] = volume[...].astype(jnp.bfloat16)

time: 102 us -> 117 us (1.15)
  Pallas kernels: 85.6 us -> 100 us
    pallas_call x1, Pallas kernels: 74.8 us -> 89.5 us  [local(): pl.pallas_call(down_kernel, out_shape=[cells(gsx, gsy), cells(gsy), cells...]
where the time goes in v8:
time: 117 us; the launch traced here: 116 us
  Pallas kernels  100 us (85%)
  starting transfers between devices  12.4 us (11%)
  waiting for transfers between devices  1.47 us (1%)
  local copies, waits for them, and re-layouts  1.25 us (1%)
    pallas_call x1, Pallas kernels, local(): pl.pallas_call(down_kernel, out_shape=[cells(gsx, gsy), cells(gsy), cells...  89.5 us
    ppermute x2, starting transfers between devices, exchange(): lax.ppermute(low, axis, [(j, i) for i, j in up])  8.59 us
    pallas_call x2, Pallas kernels, own(): pl.pallas_call(functools.partial(own_kernel, wanted), out_shape=cells(len...  5.5 us
    pallas_call x1, Pallas kernels, local(): pl.pallas_call(up_kernel, out_shape=jax.ShapeDtypeStruct(blank.shape, bla...  5.31 us
    ppermute x2, starting transfers between devices, exchange(): lax.ppermute(high, axis, up)  3.84 us
  transfers between devices with their start and end apart: 4, of which 1 were waited for; matrix products, arithmetic and copies ran while one was open for 0% of the time, Pallas kernels for 5%

profile of v8, /device:TPU:10, one launch (start us, length us, event | category | flops | bytes accessed | tf_op | source)
XLA Modules:
  0.0 115.8 jit_solution(329165762959636004)
XLA Ops:
  0.0 0.0 copy-start
  0.0 89.5 %voxel_ff_down.1 = (bf16[8,8,64,128]{3,2,1,0:T(8,128)(2,1)}, bf16[8,64,128]{2,1,0:T(8,128)(2,1)}, bf16[8,64,128]{2,1,0:T(8,128)(2,1)}, bf16[8,64,128]{2,1,0:T(8,...) custom-call(s32[2,2,16]{2,1,0:T(2,128)} %owner_hbm.1, ...), custom_call_target="tpu_custom_call" | custom-call | tf_op jit(solution)/shard_map/voxel_ff_down/pallas_call | solution.py:359
  89.5 1.9 %collective-permute-start = (bf16[8,64,128]{2,1,0:T(8,128)(2,1)}, bf16[8,64,128]{2,1,0:T(8,128)(2,1)S(1)}, u32[]{:S(2)}, u32[]{:S(2)}) collective-permute-start(bf16[8,64,128]{2,1,0:T(8,128)(2,1)} %get-tuple-element.14), channel_id=1, source_target_pairs={{0,8},{8,16},{16,24},{1,9},{9,17},{17,25},{2,10},{10,18},{18,26},{... | collective-permute-start | bytes 393224 | tf_op jit(solution)/shard_map/ppermute | solution.py:339
  91.5 3.6 %collective-permute-start.1 = (bf16[8,64,128]{2,1,0:T(8,128)(2,1)}, bf16[8,64,128]{2,1,0:T(8,128)(2,1)S(1)}, u32[]{:S(2)}, u32[]{:S(2)}) collective-permute-start(bf16[8,64,128]{2,1,0:T(8,128)(2,1)} %get-tuple-element.15), channel_id=1, source_target_pairs={{8,0},{16,8},{24,16},{9,1},{17,9},{25,17},{10,2},{18,10},{26,18},{... | collective-permute-start | bytes 393224 | tf_op jit(solution)/shard_map/ppermute | solution.py:339
  95.1 0.0 copy-done
  95.1 0.0 copy-start.3
  95.1 1.2 %copy-done.3 = bf16[8,8,64,128]{3,2,1,0:T(8,128)(2,1)S(1)} copy-done((bf16[8,8,64,128]{3,2,1,0:T(8,128)(2,1)S(1)}, bf16[8,8,64,128]{3,2,1,0:T(8,128)(2,1)}, u32[]{:S(2)}) %copy-start.3) | copy-done | bytes 1048600
  96.3 0.0 copy-start.5
  96.3 0.0 copy-start.4
  96.3 2.8 %conv_own.2.inner_ref = bf16[4,8,64,128]{3,2,1,0:T(8,128)(2,1)S(1)} custom-call(bf16[8,8,64,128]{3,2,1,0:T(8,128)(2,1)S(1)} %copy-done.3, bf16[27,128,128]{2,1,0:T(8,128)(2,1)S(1)} %bitcast.5), custom_call_target="tpu_custom_call" | custom-call | flops 7247757312 | bytes 4194304 | tf_op jit(solution)/shard_map/conv_own/pallas_call | solution.py:395
  99.1 0.0 collective-permute-done.refs_0_
  99.1 0.0 collective-permute-done.1.refs_1_
  99.1 0.0 copy-done.5
  99.2 1.9 %collective-permute-start.2 = (bf16[10,64,128]{2,1,0:T(8,128)(2,1)S(1)}, bf16[10,64,128]{2,1,0:T(8,128)(2,1)S(1)}, u32[]{:S(2)}, u32[]{:S(2)}) collective-permute-start(bf16[10,64,128]{2,1,0:T(8,128)(2,1)S(1)} %pad_maximum_fusion), channel_id=1, source_target_pairs={{0,1},{1,2},{2,3},{3,4},{4,5},{5,6},{6,7},{8,9},{9,10},{10,11},{11... | collective-permute-start | bytes 491528 | tf_op jit(solution)/shard_map/ppermute | solution.py:339
  101.1 0.0 copy-done.4
  101.2 0.0 copy-start.1
  101.2 0.0 copy-start.2
  101.2 5.0 %collective-permute-start.3 = (bf16[10,64,128]{2,1,0:T(8,128)(2,1)S(1)}, bf16[10,64,128]{2,1,0:T(8,128)(2,1)S(1)}, u32[]{:S(2)}, u32[]{:S(2)}) collective-permute-start(bf16[10,64,128]{2,1,0:T(8,128)(2,1)S(1)} %pad_maximum_fusion.1), channel_id=1, source_target_pairs={{1,0},{2,1},{3,2},{4,3},{5,4},{6,5},{7,6},{9,8},{10,9},{11,10},{12... | collective-permute-start | bytes 491528 | tf_op jit(solution)/shard_map/ppermute | solution.py:339
  106.1 2.8 %conv_own.3.outer_ref = bf16[4,8,64,128]{3,2,1,0:T(8,128)(2,1)S(1)} custom-call(bf16[8,8,64,128]{3,2,1,0:T(8,128)(2,1)S(1)} %copy-done.3, bf16[8,64,128]{2,1,0:T(8,128)(2,1)S(1)} %collective-permute-done.refs_0_, bf16[8,64,128]{2,1,0:T(8,128)(2,1)S(1)} %collective-permute-done.1.refs_1_, bf16[27,128,128]{2,1,0:T(8,128)(2,1)S(1)} %bitcast.6), custom_call_target="tpu_custom_call" | custom-call | flops 7247757312 | bytes 4194304 | tf_op jit(solution)/shard_map/conv_own/pallas_call | solution.py:395
  108.9 0.0 collective-permute-done.2.y_low_ref
  108.9 1.5 %collective-permute-done.3.y_high_ref = bf16[10,64,128]{2,1,0:T(8,128)(2,1)S(1)} collective-permute-done((bf16[10,64,128]{2,1,0:T(8,128)(2,1)S(1)}, bf16[10,64,128]{2,1,0:T(8,128)(2,1)S(1)}, u32[]{:S(2)}, u32[]{:S(2)}) %collective-permute-start.3) | collective-permute-done | bytes 163872 | tf_op jit(solution)/shard_map/ppermute | solution.py:339
  110.4 0.0 copy-done.1
  110.4 0.0 copy-done.2
  110.4 5.3 %rim_up.1 = bf16[2,2,16,4,2,64,128]{6,5,4,3,2,1,0:T(8,128)(2,1)} custom-call(s32[65]{0:T(128)S(1)} %copy-done.2, bf16[4,8,64,128]{3,2,1,0:T(8,128)(2,1)S(1)} %conv_own.2.inner_ref, bf16[4,8,64,128]{3,2,1,0:T(8,128)(2,1)S(1)} %conv_own.3.outer_ref, bf16[10,64,128]{2,1,0:T(8,128)(2,1)S(1)} %collective-permute-done.2.y_low_ref, ...), custom_call_target="tpu_custom_call", output_to_operand_aliasing={{}: (8, {})} | custom-call | tf_op jit(solution)/shard_map/rim_up/pallas_call | solution.py:415
  (4 shorter events, 0.1 us)
Async XLA Ops:
  0.0 95.1 %copy-start = (bf16[3,3,3,128,128]{4,3,2,1,0:T(8,128)(2,1)S(1)}, bf16[3,3,3,128,128]{4,3,2,1,0:T(8,128)(2,1)}, u32[]{:S(2)}) copy-start(bf16[3,3,3,128,128]{4,3,2,1,0:T(8,128)(2,1)} %param.16) | copy-start | bytes 2654212
  89.5 9.6 %collective-permute-start = (bf16[8,64,128]{2,1,0:T(8,128)(2,1)}, bf16[8,64,128]{2,1,0:T(8,128)(2,1)S(1)}, u32[]{:S(2)}, u32[]{:S(2)}) collective-permute-start(bf16[8,64,128]{2,1,0:T(8,128)(2,1)} %get-tuple-element.14), channel_id=1, source_target_pairs={{0,8},{8,16},{16,24},{1,9},{9,17},{17,25},{2,10},{10,18},{18,26},{... | collective-permute-start | bytes 393224 | tf_op jit(solution)/shard_map/ppermute | solution.py:339
  91.5 7.7 %collective-permute-start.1 = (bf16[8,64,128]{2,1,0:T(8,128)(2,1)}, bf16[8,64,128]{2,1,0:T(8,128)(2,1)S(1)}, u32[]{:S(2)}, u32[]{:S(2)}) collective-permute-start(bf16[8,64,128]{2,1,0:T(8,128)(2,1)} %get-tuple-element.15), channel_id=1, source_target_pairs={{8,0},{16,8},{24,16},{9,1},{17,9},{25,17},{10,2},{18,10},{26,18},{... | collective-permute-start | bytes 393224 | tf_op jit(solution)/shard_map/ppermute | solution.py:339
  95.1 1.2 %copy-start.3 = (bf16[8,8,64,128]{3,2,1,0:T(8,128)(2,1)S(1)}, bf16[8,8,64,128]{3,2,1,0:T(8,128)(2,1)}, u32[]{:S(2)}) copy-start(bf16[8,8,64,128]{3,2,1,0:T(8,128)(2,1)} %get-tuple-element.13.cells_ref) | copy-start | bytes 3145732
  96.3 2.8 %copy-start.5 = (bf16[8,64,128]{2,1,0:T(8,128)(2,1)S(1)}, bf16[8,64,128]{2,1,0:T(8,128)(2,1)}, u32[]{:S(2)}) copy-start(bf16[8,64,128]{2,1,0:T(8,128)(2,1)} %get-tuple-element.16) | copy-start | bytes 393220
  96.3 4.8 %copy-start.4 = (bf16[8,64,128]{2,1,0:T(8,128)(2,1)S(1)}, bf16[8,64,128]{2,1,0:T(8,128)(2,1)}, u32[]{:S(2)}) copy-start(bf16[8,64,128]{2,1,0:T(8,128)(2,1)} %get-tuple-element.17) | copy-start | bytes 393220
  99.2 9.7 %collective-permute-start.2 = (bf16[10,64,128]{2,1,0:T(8,128)(2,1)S(1)}, bf16[10,64,128]{2,1,0:T(8,128)(2,1)S(1)}, u32[]{:S(2)}, u32[]{:S(2)}) collective-permute-start(bf16[10,64,128]{2,1,0:T(8,128)(2,1)S(1)} %pad_maximum_fusion), channel_id=1, source_target_pairs={{0,1},{1,2},{2,3},{3,4},{4,5},{5,6},{6,7},{8,9},{9,10},{10,11},{11... | collective-permute-start | bytes 491528 | tf_op jit(solution)/shard_map/ppermute | solution.py:339
  101.2 9.2 %copy-start.1 = (bf16[2,2,2,128,128]{4,3,2,1,0:T(8,128)(2,1)S(1)}, bf16[2,2,2,128,128]{4,3,2,1,0:T(8,128)(2,1)}, u32[]{:S(2)}) copy-start(bf16[2,2,2,128,128]{4,3,2,1,0:T(8,128)(2,1)} %param.17) | copy-start | bytes 786436
  101.2 9.2 %copy-start.2 = (s32[65]{0:T(128)S(1)}, s32[65]{0:T(128)}, u32[]{:S(2)}) copy-start(s32[65]{0:T(128)} %get-tuple-element.12.index) | copy-start | bytes 784
  101.2 9.2 %collective-permute-start.3 = (bf16[10,64,128]{2,1,0:T(8,128)(2,1)S(1)}, bf16[10,64,128]{2,1,0:T(8,128)(2,1)S(1)}, u32[]{:S(2)}, u32[]{:S(2)}) collective-permute-start(bf16[10,64,128]{2,1,0:T(8,128)(2,1)S(1)} %pad_maximum_fusion.1), channel_id=1, source_target_pairs={{1,0},{2,1},{3,2},{4,3},{5,4},{6,5},{7,6},{9,8},{10,9},{11,10},{12... | collective-permute-start | bytes 491528 | tf_op jit(solution)/shard_map/ppermute | solution.py:339

commit v9 on v7

--- a/solution.py
+++ b/solution.py
@@ -8,6 +8,7 @@
 from jax.sharding import PartitionSpec as P
 
 GROUP = 8
+PIECE = 2
 LIFT = 4
 MOST = 32
 BLANKS = 4
@@ -95,10 +96,10 @@
         load.wait()
     for layer in range(layers):
         gain = gain_ref[layer : layer + 1] * (0.5 * chan**0.5)
-        w_in[layer] = (w_in_ref[layer].astype(jnp.float32).T * gain).astype(jnp.bfloat16)
-        w_out[layer] = w_out_ref[layer].astype(jnp.float32).T.astype(jnp.bfloat16)
+        w_in[layer] = (w_in_ref[layer].T.astype(jnp.float32) * gain).astype(jnp.bfloat16)
+        w_out[layer] = w_out_ref[layer].T
         shift = jnp.broadcast_to(0.5 * shift_ref[layer : layer + 1], (chan, shift_ref.shape[1]))
-        shifts[layer] = shift.T.astype(jnp.bfloat16)
+        shifts[layer] = shift.astype(jnp.bfloat16).T
 
     def down(group, b):
         slot = slot_of(group, b)
@@ -141,35 +142,40 @@
         for copy in copies(group):
             copy.wait()
 
-        def value(layer, b):
-            return held[group * GROUP + b].astype(jnp.float32).T if layer == 0 else stream[b]
-
-        def enter(layer, b):
-            x = value(layer, b)
+        def value(layer, piece):
+            if layer > 0:
+                return stream[piece]
+            bricks = [group * GROUP + piece * PIECE + b for b in range(PIECE)]
+            return jnp.concatenate([held[b].astype(jnp.float32).T for b in bricks], axis=1)
+
+        def enter(layer, piece):
+            x = value(layer, piece)
             power = jnp.sum(x * x, axis=0, keepdims=True)
             normed = (x * lax.rsqrt(power + chan * 1e-6)).astype(jnp.bfloat16)
             raw = jnp.dot(w_in[layer], normed, preferred_element_type=jnp.float32)
-            shift = jnp.concatenate([shifts[layer]] * (voxels // chan), axis=1)
+            shift = jnp.concatenate([shifts[layer]] * (PIECE * voxels // chan), axis=1)
             return raw.astype(jnp.bfloat16) + shift
 
-        def leave(layer, b, half):
+        def leave(layer, piece, half):
             hidden = half + half * jnp.tanh(half)
-            result = value(layer, b) + jnp.dot(
+            result = value(layer, piece) + jnp.dot(
                 w_out[layer], hidden, preferred_element_type=jnp.float32
             )
             if layer + 1 < layers:
-                stream[b] = result
+                stream[piece] = result
             else:
-                made[b] = result.T
-
-        order = [(layer, b) for layer in range(layers) for b in range(GROUP)]
+                for b in range(PIECE):
+                    made[piece * PIECE + b] = result[:, b * voxels : (b + 1) * voxels].T
+
+        order = [(layer, piece) for layer in range(layers) for piece in range(GROUP // PIECE)]
         half = enter(*order[0])
         for spot, here in enumerate(order):
             later = enter(*order[spot + 1]) if spot + 1 < len(order) else None
             leave(*here, half)
+            half = later
             if here[0] == 1:
-                down(jnp.maximum(group - 1, 0), here[1])
-            half = later
+                for b in range(PIECE):
+                    down(jnp.maximum(group - 1, 0), here[1] * PIECE + b)
         return carry
 
     lax.fori_loop(0, groups, work, 0)
@@ -364,7 +370,7 @@
             pltpu.VMEM((layers, hid, chan), jnp.bfloat16),
             pltpu.VMEM((layers, chan, hid), jnp.bfloat16),
             pltpu.VMEM((layers, hid, chan), jnp.bfloat16),
-            pltpu.VMEM((GROUP, chan, voxels), jnp.float32),
+            pltpu.VMEM((GROUP // PIECE, chan, PIECE * voxels), jnp.float32),
             pltpu.VMEM((GROUP, voxels, chan), jnp.float32),
             pltpu.VMEM((gsx, gsy, gsz, chan), jnp.float32),
             pltpu.VMEM((BLANKS,) + brick, jnp.bfloat16),

time: 102 us -> 106 us (1.039)
  the two profiles are of different devices: /device:TPU:10 before, /device:TPU:14 now
where the time goes in v9:
time: 106 us; the launch traced here: 105 us
  Pallas kernels  88.9 us (84%)
  starting transfers between devices  11.5 us (11%)
  waiting for transfers between devices  3.01 us (3%)
  local copies, waits for them, and re-layouts  1.25 us (1%)
    pallas_call x1, Pallas kernels, local(): pl.pallas_call(down_kernel, out_shape=[cells(gsx, gsy), cells(gsy), cells...  78.1 us
    ppermute x2, starting transfers between devices, exchange(): lax.ppermute(low, axis, [(j, i) for i, j in up])  6.11 us
    pallas_call x2, Pallas kernels, own(): pl.pallas_call(functools.partial(own_kernel, wanted), out_shape=cells(len...  5.5 us
    ppermute x2, starting transfers between devices, exchange(): lax.ppermute(high, axis, up)  5.43 us
    pallas_call x1, Pallas kernels, local(): pl.pallas_call(up_kernel, out_shape=jax.ShapeDtypeStruct(blank.shape, bla...  5.31 us
    ppermute x2, waiting for transfers between devices, exchange(): lax.ppermute(low, axis, [(j, i) for i, j in up])  3 us
  transfers between devices with their start and end apart: 4, of which 1 were waited for; matrix products, arithmetic and copies ran while one was open for 0% of the time, Pallas kernels for 5%

profile of v9, /device:TPU:14, one launch (start us, length us, event | category | flops | bytes accessed | tf_op | source)
XLA Modules:
  0.0 105.1 jit_solution(15155598106895666436)
XLA Ops:
  0.0 0.0 copy-start
  0.0 78.1 %voxel_ff_down.1 = (bf16[8,8,64,128]{3,2,1,0:T(8,128)(2,1)}, bf16[8,64,128]{2,1,0:T(8,128)(2,1)}, bf16[8,64,128]{2,1,0:T(8,128)(2,1)}, bf16[8,64,128]{2,1,0:T(8,...) custom-call(s32[2,2,16]{2,1,0:T(2,128)} %owner_hbm.1, ...), custom_call_target="tpu_custom_call" | custom-call | tf_op jit(solution)/shard_map/voxel_ff_down/pallas_call | solution.py:353
  78.1 1.9 %collective-permute-start = (bf16[8,64,128]{2,1,0:T(8,128)(2,1)}, bf16[8,64,128]{2,1,0:T(8,128)(2,1)S(1)}, u32[]{:S(2)}, u32[]{:S(2)}) collective-permute-start(bf16[8,64,128]{2,1,0:T(8,128)(2,1)} %get-tuple-element.14), channel_id=1, source_target_pairs={{0,8},{8,16},{16,24},{1,9},{9,17},{17,25},{2,10},{10,18},{18,26},{... | collective-permute-start | bytes 393224 | tf_op jit(solution)/shard_map/ppermute | solution.py:333
  80.1 3.6 %collective-permute-start.1 = (bf16[8,64,128]{2,1,0:T(8,128)(2,1)}, bf16[8,64,128]{2,1,0:T(8,128)(2,1)S(1)}, u32[]{:S(2)}, u32[]{:S(2)}) collective-permute-start(bf16[8,64,128]{2,1,0:T(8,128)(2,1)} %get-tuple-element.15), channel_id=1, source_target_pairs={{8,0},{16,8},{24,16},{9,1},{17,9},{25,17},{10,2},{18,10},{26,18},{... | collective-permute-start | bytes 393224 | tf_op jit(solution)/shard_map/ppermute | solution.py:333
  83.7 0.0 copy-done
  83.7 0.0 copy-start.3
  83.7 1.2 %copy-done.3 = bf16[8,8,64,128]{3,2,1,0:T(8,128)(2,1)S(1)} copy-done((bf16[8,8,64,128]{3,2,1,0:T(8,128)(2,1)S(1)}, bf16[8,8,64,128]{3,2,1,0:T(8,128)(2,1)}, u32[]{:S(2)}) %copy-start.3) | copy-done | bytes 1048600
  85.0 0.0 copy-start.5
  85.0 0.0 copy-start.4
  85.0 2.8 %conv_own.2.inner_ref = bf16[4,8,64,128]{3,2,1,0:T(8,128)(2,1)S(1)} custom-call(bf16[8,8,64,128]{3,2,1,0:T(8,128)(2,1)S(1)} %copy-done.3, bf16[27,128,128]{2,1,0:T(8,128)(2,1)S(1)} %bitcast.5), custom_call_target="tpu_custom_call" | custom-call | flops 7247757312 | bytes 4194304 | tf_op jit(solution)/shard_map/conv_own/pallas_call | solution.py:389
  87.7 0.0 collective-permute-done.refs_0_
  87.7 0.0 collective-permute-done.1.refs_1_
  87.8 0.0 copy-done.5
  87.8 3.5 %collective-permute-start.2 = (bf16[10,64,128]{2,1,0:T(8,128)(2,1)S(1)}, bf16[10,64,128]{2,1,0:T(8,128)(2,1)S(1)}, u32[]{:S(2)}, u32[]{:S(2)}) collective-permute-start(bf16[10,64,128]{2,1,0:T(8,128)(2,1)S(1)} %pad_maximum_fusion), channel_id=1, source_target_pairs={{0,1},{1,2},{2,3},{3,4},{4,5},{5,6},{6,7},{8,9},{9,10},{10,11},{11... | collective-permute-start | bytes 491528 | tf_op jit(solution)/shard_map/ppermute | solution.py:333
  91.3 0.0 copy-done.4
  91.4 0.0 copy-start.1
  91.4 0.0 copy-start.2
  91.4 2.5 %collective-permute-start.3 = (bf16[10,64,128]{2,1,0:T(8,128)(2,1)S(1)}, bf16[10,64,128]{2,1,0:T(8,128)(2,1)S(1)}, u32[]{:S(2)}, u32[]{:S(2)}) collective-permute-start(bf16[10,64,128]{2,1,0:T(8,128)(2,1)S(1)} %pad_maximum_fusion.1), channel_id=1, source_target_pairs={{1,0},{2,1},{3,2},{4,3},{5,4},{6,5},{7,6},{9,8},{10,9},{11,10},{12... | collective-permute-start | bytes 491528 | tf_op jit(solution)/shard_map/ppermute | solution.py:333
  93.9 2.8 %conv_own.3.outer_ref = bf16[4,8,64,128]{3,2,1,0:T(8,128)(2,1)S(1)} custom-call(bf16[8,8,64,128]{3,2,1,0:T(8,128)(2,1)S(1)} %copy-done.3, bf16[8,64,128]{2,1,0:T(8,128)(2,1)S(1)} %collective-permute-done.refs_0_, bf16[8,64,128]{2,1,0:T(8,128)(2,1)S(1)} %collective-permute-done.1.refs_1_, bf16[27,128,128]{2,1,0:T(8,128)(2,1)S(1)} %bitcast.6), custom_call_target="tpu_custom_call" | custom-call | flops 7247757312 | bytes 4194304 | tf_op jit(solution)/shard_map/conv_own/pallas_call | solution.py:389
  96.6 0.0 collective-permute-done.2.y_low_ref
  96.6 3.0 %collective-permute-done.3.y_high_ref = bf16[10,64,128]{2,1,0:T(8,128)(2,1)S(1)} collective-permute-done((bf16[10,64,128]{2,1,0:T(8,128)(2,1)S(1)}, bf16[10,64,128]{2,1,0:T(8,128)(2,1)S(1)}, u32[]{:S(2)}, u32[]{:S(2)}) %collective-permute-start.3) | collective-permute-done | bytes 163872 | tf_op jit(solution)/shard_map/ppermute | solution.py:333
  99.6 0.0 copy-done.1
  99.6 0.0 copy-done.2
  99.6 5.3 %rim_up.1 = bf16[2,2,16,4,2,64,128]{6,5,4,3,2,1,0:T(8,128)(2,1)} custom-call(s32[65]{0:T(128)S(1)} %copy-done.2, bf16[4,8,64,128]{3,2,1,0:T(8,128)(2,1)S(1)} %conv_own.2.inner_ref, bf16[4,8,64,128]{3,2,1,0:T(8,128)(2,1)S(1)} %conv_own.3.outer_ref, bf16[10,64,128]{2,1,0:T(8,128)(2,1)S(1)} %collective-permute-done.2.y_low_ref, ...), custom_call_target="tpu_custom_call", output_to_operand_aliasing={{}: (8, {})} | custom-call | tf_op jit(solution)/shard_map/rim_up/pallas_call | solution.py:409
  (4 shorter events, 0.1 us)
Async XLA Ops:
  0.0 83.7 %copy-start = (bf16[3,3,3,128,128]{4,3,2,1,0:T(8,128)(2,1)S(1)}, bf16[3,3,3,128,128]{4,3,2,1,0:T(8,128)(2,1)}, u32[]{:S(2)}) copy-start(bf16[3,3,3,128,128]{4,3,2,1,0:T(8,128)(2,1)} %param.16) | copy-start | bytes 2654212
  78.1 9.6 %collective-permute-start = (bf16[8,64,128]{2,1,0:T(8,128)(2,1)}, bf16[8,64,128]{2,1,0:T(8,128)(2,1)S(1)}, u32[]{:S(2)}, u32[]{:S(2)}) collective-permute-start(bf16[8,64,128]{2,1,0:T(8,128)(2,1)} %get-tuple-element.14), channel_id=1, source_target_pairs={{0,8},{8,16},{16,24},{1,9},{9,17},{17,25},{2,10},{10,18},{18,26},{... | collective-permute-start | bytes 393224 | tf_op jit(solution)/shard_map/ppermute | solution.py:333
  80.1 7.7 %collective-permute-start.1 = (bf16[8,64,128]{2,1,0:T(8,128)(2,1)}, bf16[8,64,128]{2,1,0:T(8,128)(2,1)S(1)}, u32[]{:S(2)}, u32[]{:S(2)}) collective-permute-start(bf16[8,64,128]{2,1,0:T(8,128)(2,1)} %get-tuple-element.15), channel_id=1, source_target_pairs={{8,0},{16,8},{24,16},{9,1},{17,9},{25,17},{10,2},{18,10},{26,18},{... | collective-permute-start | bytes 393224 | tf_op jit(solution)/shard_map/ppermute | solution.py:333
  83.7 1.2 %copy-start.3 = (bf16[8,8,64,128]{3,2,1,0:T(8,128)(2,1)S(1)}, bf16[8,8,64,128]{3,2,1,0:T(8,128)(2,1)}, u32[]{:S(2)}) copy-start(bf16[8,8,64,128]{3,2,1,0:T(8,128)(2,1)} %get-tuple-element.13.cells_ref) | copy-start | bytes 3145732
  85.0 2.8 %copy-start.5 = (bf16[8,64,128]{2,1,0:T(8,128)(2,1)S(1)}, bf16[8,64,128]{2,1,0:T(8,128)(2,1)}, u32[]{:S(2)}) copy-start(bf16[8,64,128]{2,1,0:T(8,128)(2,1)} %get-tuple-element.16) | copy-start | bytes 393220
  85.0 6.4 %copy-start.4 = (bf16[8,64,128]{2,1,0:T(8,128)(2,1)S(1)}, bf16[8,64,128]{2,1,0:T(8,128)(2,1)}, u32[]{:S(2)}) copy-start(bf16[8,64,128]{2,1,0:T(8,128)(2,1)} %get-tuple-element.17) | copy-start | bytes 393220
  87.8 8.8 %collective-permute-start.2 = (bf16[10,64,128]{2,1,0:T(8,128)(2,1)S(1)}, bf16[10,64,128]{2,1,0:T(8,128)(2,1)S(1)}, u32[]{:S(2)}, u32[]{:S(2)}) collective-permute-start(bf16[10,64,128]{2,1,0:T(8,128)(2,1)S(1)} %pad_maximum_fusion), channel_id=1, source_target_pairs={{0,1},{1,2},{2,3},{3,4},{4,5},{5,6},{6,7},{8,9},{9,10},{10,11},{11... | collective-permute-start | bytes 491528 | tf_op jit(solution)/shard_map/ppermute | solution.py:333
  91.4 8.3 %copy-start.1 = (bf16[2,2,2,128,128]{4,3,2,1,0:T(8,128)(2,1)S(1)}, bf16[2,2,2,128,128]{4,3,2,1,0:T(8,128)(2,1)}, u32[]{:S(2)}) copy-start(bf16[2,2,2,128,128]{4,3,2,1,0:T(8,128)(2,1)} %param.17) | copy-start | bytes 786436
  91.4 8.3 %copy-start.2 = (s32[65]{0:T(128)S(1)}, s32[65]{0:T(128)}, u32[]{:S(2)}) copy-start(s32[65]{0:T(128)} %get-tuple-element.12.index) | copy-start | bytes 784
  91.4 8.2 %collective-permute-start.3 = (bf16[10,64,128]{2,1,0:T(8,128)(2,1)S(1)}, bf16[10,64,128]{2,1,0:T(8,128)(2,1)S(1)}, u32[]{:S(2)}, u32[]{:S(2)}) collective-permute-start(bf16[10,64,128]{2,1,0:T(8,128)(2,1)S(1)} %pad_maximum_fusion.1), channel_id=1, source_target_pairs={{1,0},{2,1},{3,2},{4,3},{5,4},{6,5},{7,6},{9,8},{10,9},{11,10},{12... | collective-permute-start | bytes 491528 | tf_op jit(solution)/shard_map/ppermute | solution.py:333

commit v10 on v7

--- a/solution.py
+++ b/solution.py
@@ -222,24 +222,24 @@
 
 def own_kernel(wanted, cells_ref, *refs):
     rims, (w_conv_ref, out_ref) = refs[:-2], refs[-2:]
-    gsx = cells_ref.shape[0]
-    for spot, x in enumerate(wanted):
-        planes = [(d, x + d - 1, cells_ref) for d in range(3)]
-        if rims:
-            low_ref, high_ref = rims
-            planes = [
-                (d, i, low_ref if i < 0 else high_ref if i == gsx else ref) for d, i, ref in planes
-            ]
+    gsy = cells_ref.shape[1]
+    for spot, y in enumerate(wanted):
         pieces = []
-        for d, i, ref in planes:
-            lines = ref[i] if 0 <= i < gsx else ref[...]
-            pieces += [(d, e, moved_lines(lines, e)) for e in range(3)]
-        total = cells_ref[x].astype(jnp.float32) + conv_lines(pieces, w_conv_ref)
+        for e in range(3):
+            i = y + e - 1
+            if 0 <= i < gsy:
+                lines = cells_ref[:, i]
+            elif rims:
+                lines = rims[0 if i < 0 else 1][...]
+            else:
+                continue
+            pieces += [(d, e, moved_lines(lines, d)) for d in range(3)]
+        total = cells_ref[:, y].astype(jnp.float32) + conv_lines(pieces, w_conv_ref)
         out_ref[spot] = total.astype(jnp.bfloat16)
 
 
 def up_kernel(
-    index, inner_ref, outer_ref, y_low_ref, y_high_ref, w_conv_ref, w_up_ref, feat_ref, blank_ref,
+    index, inner_ref, outer_ref, x_low_ref, x_high_ref, w_conv_ref, w_up_ref, feat_ref, blank_ref,
     out_ref, held, total, twice, in_sem, out_sem,
 ):
     gsx, gsy, gsz, chan = total.shape
@@ -261,13 +261,13 @@
 
     groups = (count + LIFT - 1) // LIFT
 
-    inner, outer = split_planes(gsx)
+    inner, outer = split_planes(gsy)
     for wanted, ref in ((inner, inner_ref), (outer, outer_ref)):
-        for spot, x in enumerate(wanted):
-            total[x] = ref[spot].astype(jnp.float32)
-    for line, ref, e in ((0, y_low_ref, 0), (gsy - 1, y_high_ref, 2)):
-        pieces = [(d, e, ref[d : d + gsx]) for d in range(3)]
-        total[:, line] = total[:, line] + conv_lines(pieces, w_conv_ref)
+        for spot, y in enumerate(wanted):
+            total[:, y] = ref[spot].astype(jnp.float32)
+    for plane, ref, d in ((0, x_low_ref, 0), (gsx - 1, x_high_ref, 2)):
+        pieces = [(d, e, ref[e : e + gsy]) for e in range(3)]
+        total[plane] = total[plane] + conv_lines(pieces, w_conv_ref)
     for x in range(gsx):
         for c in range(2):
             twice[x, :, pl.ds(c, gsz, stride=2)] = total[x]
@@ -316,9 +316,8 @@
         store(spot).wait()
 
 
-def split_planes(gsx):
-    inner = range(gsx // 4, gsx - gsx // 4)
-    return inner, [x for x in range(gsx) if x not in inner]
+def split_planes(gsy):
+    return range(1, gsy - 1), (0, gsy - 1)
 
 
 def exchange(low, high, axis):
@@ -377,28 +376,28 @@
     )(owner, features, norm_gain, time_shift, w_in, w_out, w_down.reshape(8, chan, chan))
 
     taps = w_conv.reshape(27, chan, chan)
-    flops = 2 * 27 * gsx // 2 * gsy * gsz * chan * chan
-
     def own(wanted, *operands):
         return pl.pallas_call(
             functools.partial(own_kernel, wanted),
-            out_shape=cells(len(wanted), gsy),
+            out_shape=cells(len(wanted), gsx),
             in_specs=[vmem] * len(operands),
             out_specs=vmem,
             compiler_params=limit(20),
             cost_estimate=pl.CostEstimate(
-                flops=4 * flops, bytes_accessed=4 * MIB, transcendentals=0
+                flops=200 * len(wanted) * gsx * gsz * chan * chan,
+                bytes_accessed=4 * MIB,
+                transcendentals=0,
             ),
             name="conv_own",
         )(*operands)
 
-    inner, outer = split_planes(gsx)
+    inner, outer = split_planes(gsy)
+    y_low, y_high = exchange(y_low, y_high, "gy")
     inner = own(inner, grid, taps)
+    outer = own(outer, grid, y_low, y_high, taps)
+    x_low = jnp.concatenate([y_low[:1], x_low, y_high[:1]], axis=0)
+    x_high = jnp.concatenate([y_low[-1:], x_high, y_high[-1:]], axis=0)
     x_low, x_high = exchange(x_low, x_high, "gx")
-    outer = own(outer, grid, x_low, x_high, taps)
-    y_low = jnp.concatenate([x_low[:1], y_low, x_high[:1]], axis=0)
-    y_high = jnp.concatenate([x_low[-1:], y_high, x_high[-1:]], axis=0)
-    y_low, y_high = exchange(y_low, y_high, "gy")
 
     result = pl.pallas_call(
         up_kernel,
@@ -416,7 +415,7 @@
         compiler_params=limit(48),
         name="rim_up",
     )(
-        index, inner, outer, y_low, y_high, taps, w_up.reshape(8, chan, chan),
+        index, inner, outer, x_low, x_high, taps, w_up.reshape(8, chan, chan),
         features.reshape(blank.shape), blank,
     )
     return result.reshape(features.shape)

time: 102 us -> 102 us (level)
  no operation moved by 1% of the time
where the time goes in v10:
time: 102 us; the launch traced here: 101 us
  Pallas kernels  85.6 us (84%)
  starting transfers between devices  12.3 us (12%)
  waiting for transfers between devices  1.34 us (1%)
  local copies, waits for them, and re-layouts  1.25 us (1%)
    pallas_call x1, Pallas kernels, local(): pl.pallas_call(down_kernel, out_shape=[cells(gsx, gsy), cells(gsy), cells...  74.8 us
    ppermute x2, starting transfers between devices, exchange(): lax.ppermute(low, axis, [(j, i) for i, j in up])  8.46 us
    pallas_call x2, Pallas kernels, own(): pl.pallas_call(functools.partial(own_kernel, wanted), out_shape=cells(len...  5.5 us
    pallas_call x1, Pallas kernels, local(): pl.pallas_call(up_kernel, out_shape=jax.ShapeDtypeStruct(blank.shape, bla...  5.3 us
    ppermute x2, starting transfers between devices, exchange(): lax.ppermute(high, axis, up)  3.84 us
  transfers between devices with their start and end apart: 4, of which 1 were waited for; matrix products, arithmetic and copies ran while one was open for 0% of the time, Pallas kernels for 5%

profile of v10, /device:TPU:10, one launch (start us, length us, event | category | flops | bytes accessed | tf_op | source)
XLA Modules:
  0.0 100.9 jit_solution(5277729269925673174)
XLA Ops:
  0.0 0.0 copy-start
  0.0 74.8 %voxel_ff_down.1 = (bf16[8,8,64,128]{3,2,1,0:T(8,128)(2,1)}, bf16[8,64,128]{2,1,0:T(8,128)(2,1)}, bf16[8,64,128]{2,1,0:T(8,128)(2,1)}, bf16[8,64,128]{2,1,0:T(8,...) custom-call(s32[2,2,16]{2,1,0:T(2,128)} %owner_hbm.1, ...), custom_call_target="tpu_custom_call" | custom-call | tf_op jit(solution)/shard_map/voxel_ff_down/pallas_call | solution.py:346
  74.8 1.9 %collective-permute-start = (bf16[8,64,128]{2,1,0:T(8,128)(2,1)}, bf16[8,64,128]{2,1,0:T(8,128)(2,1)S(1)}, u32[]{:S(2)}, u32[]{:S(2)}) collective-permute-start(bf16[8,64,128]{2,1,0:T(8,128)(2,1)} %get-tuple-element.14), channel_id=1, source_target_pairs={{0,1},{1,2},{2,3},{3,4},{4,5},{5,6},{6,7},{8,9},{9,10},{10,11},{11... | collective-permute-start | bytes 393224 | tf_op jit(solution)/shard_map/ppermute | solution.py:326
  76.7 4.8 %collective-permute-start.1 = (bf16[8,64,128]{2,1,0:T(8,128)(2,1)}, bf16[8,64,128]{2,1,0:T(8,128)(2,1)S(1)}, u32[]{:S(2)}, u32[]{:S(2)}) collective-permute-start(bf16[8,64,128]{2,1,0:T(8,128)(2,1)} %get-tuple-element.15), channel_id=1, source_target_pairs={{1,0},{2,1},{3,2},{4,3},{5,4},{6,5},{7,6},{9,8},{10,9},{11,10},{12... | collective-permute-start | bytes 393224 | tf_op jit(solution)/shard_map/ppermute | solution.py:326
  81.6 0.0 copy-done
  81.6 0.0 copy-start.3
  81.6 1.2 %copy-done.3 = bf16[8,8,64,128]{3,2,1,0:T(8,128)(2,1)S(1)} copy-done((bf16[8,8,64,128]{3,2,1,0:T(8,128)(2,1)S(1)}, bf16[8,8,64,128]{3,2,1,0:T(8,128)(2,1)}, u32[]{:S(2)}) %copy-start.3) | copy-done | bytes 1048600
  82.8 0.0 copy-start.5
  82.8 0.0 copy-start.4
  82.8 4.0 %conv_own.2.inner_ref = bf16[6,8,64,128]{3,2,1,0:T(8,128)(2,1)S(1)} custom-call(bf16[8,8,64,128]{3,2,1,0:T(8,128)(2,1)S(1)} %copy-done.3, bf16[27,128,128]{2,1,0:T(8,128)(2,1)S(1)} %bitcast.5), custom_call_target="tpu_custom_call" | custom-call | flops 10066329600 | bytes 4194304 | tf_op jit(solution)/shard_map/conv_own/pallas_call | solution.py:380
  86.9 0.0 copy-start.1
  86.9 0.0 copy-start.2
  86.9 0.0 collective-permute-done.refs_0_
  86.9 0.0 collective-permute-done.1.refs_1_
  86.9 0.0 copy-done.5
  87.0 1.9 %collective-permute-start.2 = (bf16[10,64,128]{2,1,0:T(8,128)(2,1)S(1)}, bf16[10,64,128]{2,1,0:T(8,128)(2,1)S(1)}, u32[]{:S(2)}, u32[]{:S(2)}) collective-permute-start(bf16[10,64,128]{2,1,0:T(8,128)(2,1)S(1)} %pad_maximum_fusion), channel_id=1, source_target_pairs={{0,8},{8,16},{16,24},{1,9},{9,17},{17,25},{2,10},{10,18},{18,26},{... | collective-permute-start | bytes 491528 | tf_op jit(solution)/shard_map/ppermute | solution.py:326
  88.9 0.0 copy-done.4
  88.9 3.6 %collective-permute-start.3 = (bf16[10,64,128]{2,1,0:T(8,128)(2,1)S(1)}, bf16[10,64,128]{2,1,0:T(8,128)(2,1)S(1)}, u32[]{:S(2)}, u32[]{:S(2)}) collective-permute-start(bf16[10,64,128]{2,1,0:T(8,128)(2,1)S(1)} %pad_maximum_fusion.1), channel_id=1, source_target_pairs={{8,0},{16,8},{24,16},{9,1},{17,9},{25,17},{10,2},{18,10},{26,18},{... | collective-permute-start | bytes 491528 | tf_op jit(solution)/shard_map/ppermute | solution.py:326
  92.6 1.5 %conv_own.3.outer_ref = bf16[2,8,64,128]{3,2,1,0:T(8,128)(2,1)S(1)} custom-call(bf16[8,8,64,128]{3,2,1,0:T(8,128)(2,1)S(1)} %copy-done.3, bf16[8,64,128]{2,1,0:T(8,128)(2,1)S(1)} %collective-permute-done.refs_0_, bf16[8,64,128]{2,1,0:T(8,128)(2,1)S(1)} %collective-permute-done.1.refs_1_, bf16[27,128,128]{2,1,0:T(8,128)(2,1)S(1)} %bitcast.6), custom_call_target="tpu_custom_call" | custom-call | flops 3355443200 | bytes 4194304 | tf_op jit(solution)/shard_map/conv_own/pallas_call | solution.py:380
  94.1 0.0 collective-permute-done.2.x_low_ref
  94.1 1.3 %collective-permute-done.3.x_high_ref = bf16[10,64,128]{2,1,0:T(8,128)(2,1)S(1)} collective-permute-done((bf16[10,64,128]{2,1,0:T(8,128)(2,1)S(1)}, bf16[10,64,128]{2,1,0:T(8,128)(2,1)S(1)}, u32[]{:S(2)}, u32[]{:S(2)}) %collective-permute-start.3) | collective-permute-done | bytes 163872 | tf_op jit(solution)/shard_map/ppermute | solution.py:326
  95.4 0.0 copy-done.1
  95.4 0.0 copy-done.2
  95.4 5.3 %rim_up.1 = bf16[2,2,16,4,2,64,128]{6,5,4,3,2,1,0:T(8,128)(2,1)} custom-call(s32[65]{0:T(128)S(1)} %copy-done.2, bf16[6,8,64,128]{3,2,1,0:T(8,128)(2,1)S(1)} %conv_own.2.inner_ref, bf16[2,8,64,128]{3,2,1,0:T(8,128)(2,1)S(1)} %conv_own.3.outer_ref, bf16[10,64,128]{2,1,0:T(8,128)(2,1)S(1)} %collective-permute-done.2.x_low_ref, ...), custom_call_target="tpu_custom_call", output_to_operand_aliasing={{}: (8, {})} | custom-call | tf_op jit(solution)/shard_map/rim_up/pallas_call | solution.py:402
  (4 shorter events, 0.1 us)
Async XLA Ops:
  0.0 81.6 %copy-start = (bf16[3,3,3,128,128]{4,3,2,1,0:T(8,128)(2,1)S(1)}, bf16[3,3,3,128,128]{4,3,2,1,0:T(8,128)(2,1)}, u32[]{:S(2)}) copy-start(bf16[3,3,3,128,128]{4,3,2,1,0:T(8,128)(2,1)} %param.16) | copy-start | bytes 2654212
  74.8 12.1 %collective-permute-start = (bf16[8,64,128]{2,1,0:T(8,128)(2,1)}, bf16[8,64,128]{2,1,0:T(8,128)(2,1)S(1)}, u32[]{:S(2)}, u32[]{:S(2)}) collective-permute-start(bf16[8,64,128]{2,1,0:T(8,128)(2,1)} %get-tuple-element.14), channel_id=1, source_target_pairs={{0,1},{1,2},{2,3},{3,4},{4,5},{5,6},{6,7},{8,9},{9,10},{10,11},{11... | collective-permute-start | bytes 393224 | tf_op jit(solution)/shard_map/ppermute | solution.py:326
  76.7 10.2 %collective-permute-start.1 = (bf16[8,64,128]{2,1,0:T(8,128)(2,1)}, bf16[8,64,128]{2,1,0:T(8,128)(2,1)S(1)}, u32[]{:S(2)}, u32[]{:S(2)}) collective-permute-start(bf16[8,64,128]{2,1,0:T(8,128)(2,1)} %get-tuple-element.15), channel_id=1, source_target_pairs={{1,0},{2,1},{3,2},{4,3},{5,4},{6,5},{7,6},{9,8},{10,9},{11,10},{12... | collective-permute-start | bytes 393224 | tf_op jit(solution)/shard_map/ppermute | solution.py:326
  81.6 1.2 %copy-start.3 = (bf16[8,8,64,128]{3,2,1,0:T(8,128)(2,1)S(1)}, bf16[8,8,64,128]{3,2,1,0:T(8,128)(2,1)}, u32[]{:S(2)}) copy-start(bf16[8,8,64,128]{3,2,1,0:T(8,128)(2,1)} %get-tuple-element.13.cells_ref) | copy-start | bytes 3145732
  82.8 4.1 %copy-start.5 = (bf16[8,64,128]{2,1,0:T(8,128)(2,1)S(1)}, bf16[8,64,128]{2,1,0:T(8,128)(2,1)}, u32[]{:S(2)}) copy-start(bf16[8,64,128]{2,1,0:T(8,128)(2,1)} %get-tuple-element.16) | copy-start | bytes 393220
  82.8 6.1 %copy-start.4 = (bf16[8,64,128]{2,1,0:T(8,128)(2,1)S(1)}, bf16[8,64,128]{2,1,0:T(8,128)(2,1)}, u32[]{:S(2)}) copy-start(bf16[8,64,128]{2,1,0:T(8,128)(2,1)} %get-tuple-element.17) | copy-start | bytes 393220
  86.9 8.6 %copy-start.1 = (bf16[2,2,2,128,128]{4,3,2,1,0:T(8,128)(2,1)S(1)}, bf16[2,2,2,128,128]{4,3,2,1,0:T(8,128)(2,1)}, u32[]{:S(2)}) copy-start(bf16[2,2,2,128,128]{4,3,2,1,0:T(8,128)(2,1)} %param.17) | copy-start | bytes 786436
  86.9 8.5 %copy-start.2 = (s32[65]{0:T(128)S(1)}, s32[65]{0:T(128)}, u32[]{:S(2)}) copy-start(s32[65]{0:T(128)} %get-tuple-element.12.index) | copy-start | bytes 784
  87.0 7.1 %collective-permute-start.2 = (bf16[10,64,128]{2,1,0:T(8,128)(2,1)S(1)}, bf16[10,64,128]{2,1,0:T(8,128)(2,1)S(1)}, u32[]{:S(2)}, u32[]{:S(2)}) collective-permute-start(bf16[10,64,128]{2,1,0:T(8,128)(2,1)S(1)} %pad_maximum_fusion), channel_id=1, source_target_pairs={{0,8},{8,16},{16,24},{1,9},{9,17},{17,25},{2,10},{10,18},{18,26},{... | collective-permute-start | bytes 491528 | tf_op jit(solution)/shard_map/ppermute | solution.py:326
  88.9 6.5 %collective-permute-start.3 = (bf16[10,64,128]{2,1,0:T(8,128)(2,1)S(1)}, bf16[10,64,128]{2,1,0:T(8,128)(2,1)S(1)}, u32[]{:S(2)}, u32[]{:S(2)}) collective-permute-start(bf16[10,64,128]{2,1,0:T(8,128)(2,1)S(1)} %pad_maximum_fusion.1), channel_id=1, source_target_pairs={{8,0},{16,8},{24,16},{9,1},{17,9},{25,17},{10,2},{18,10},{26,18},{... | collective-permute-start | bytes 491528 | tf_op jit(solution)/shard_map/ppermute | solution.py:326
